TPU v7x, 32 devices: a whole 2x2x4 slice. The times are simulated.
32 devices in a mesh: spec: 4 (over x, core), neuron: 8 (over z, y).
Axes of the slice: x: 2, y: 2, z: 4, core: 2. Of those that a mesh axis runs over, the one named last changes fastest.
Arguments:
- center: float32 [32, 8192], P('spec', 'neuron'), may hold values from -6 to 6
- radius: float32 [32, 8192], P('spec', 'neuron'), may hold values from 0.002 to 0.02
- weight: float32 [4096, 8192], P('neuron'), may hold values from -0.0625 to 0.0625
- bias: float32 [4096], P('neuron'), may hold values from -3 to 3
- out_weight: float32 [1000, 4096], P(None, 'neuron'), may hold values from -0.09375 to 0.09375
- masks: int32 [32, 4096], P(None, 'neuron'), may hold values from 0 to 2
- image_labels: int32 [32], replicated, may hold values from 0 to 999
- runner_up: int32 [2048], P('spec'), may hold values from 0 to 999
- spec_image: int32 [2048], P('spec'), may hold values from 0 to 31
Outputs:
- input_coeffs: float32 [2048, 8192], P('spec', 'neuron')
- margin_bounds: float32 [2048], P('spec')
All inputs are finite; a program needn't handle non-finite values.
Results may differ from a plain program's by a relative error of at most 0.000098.
Values sent between devices are 32-bit elements; how exact they have to be, the bound alone decides.
No kernel may reach another device: no remote copies, remote signals or barrier semaphores. Data moves between devices by JAX's collectives and lax.ppermute only.
A program may use at most 128 MiB of HBM per device.

v0:
```python
import jax
import jax.numpy as jnp
from jax import lax
from jax.sharding import PartitionSpec as P


def relax(pre_center, pre_radius, masks):
    upper = pre_center + pre_radius
    lower = pre_center - pre_radius
    slope = jnp.clip(upper / (upper - lower), 0.0, 1.0)
    slopes = jnp.where(
        masks == 1, jnp.ones_like(slope), jnp.where(masks == 2, slope, jnp.zeros_like(slope))
    )
    offsets = jnp.where(masks == 2, slope * lower, jnp.zeros_like(slope))
    return (slopes, offsets)


def interval(center_full, radius_full, weight, bias, masks):
    highest = lax.Precision.HIGHEST
    dims = (((1,), (1,)), ((), ()))
    pre_center = lax.dot_general(center_full, weight, dims, precision=highest) + bias
    pre_radius = lax.dot_general(radius_full, jnp.abs(weight), dims, precision=highest)
    return relax(pre_center, pre_radius, masks)


def local(center, radius, weight, bias, out_weight, masks, image_labels, runner_up, spec_image):
    highest = lax.Precision.HIGHEST
    center_all, radius_all = (
        lax.all_gather(center, "spec", axis=0, tiled=True),
        lax.all_gather(radius, "spec", axis=0, tiled=True),
    )
    center_full, radius_full = (
        lax.all_gather(center_all, "neuron", axis=1, tiled=True),
        lax.all_gather(radius_all, "neuron", axis=1, tiled=True),
    )
    slopes_all, offsets_all = interval(center_full, radius_full, weight, bias, masks)
    true_class = jnp.take(image_labels, spec_image, axis=0)
    spec_coeff = jnp.take(out_weight, true_class, axis=0) - jnp.take(out_weight, runner_up, axis=0)
    scaled = spec_coeff * jnp.take(slopes_all, spec_image, axis=0)
    offset_rows = jnp.take(offsets_all, spec_image, axis=0)
    relax_part = -jnp.sum(jnp.minimum(spec_coeff, 0.0) * offset_rows, axis=1) + jnp.sum(
        scaled * bias, axis=1
    )
    input_coeffs = lax.psum_scatter(
        lax.dot_general(weight, scaled, (((0,), (1,)), ((), ())), precision=highest),
        "neuron",
        scatter_dimension=0,
        tiled=True,
    ).T
    center_rows = jnp.take(center_all, spec_image, axis=0)
    radius_rows = jnp.take(radius_all, spec_image, axis=0)
    input_part = jnp.sum(input_coeffs * center_rows - jnp.abs(input_coeffs) * radius_rows, axis=1)
    margin_bounds = lax.psum(input_part + relax_part, "neuron")
    return (input_coeffs, margin_bounds)


def solution(mesh):
    return jax.shard_map(
        local,
        mesh=mesh,
        in_specs=(
            P("spec", "neuron"),
            P("spec", "neuron"),
            P("neuron", None),
            P("neuron"),
            P(None, "neuron"),
            P(None, "neuron"),
            P(),
            P("spec"),
            P("spec"),
        ),
        out_specs=(P("spec", "neuron"), P("spec")),
        check_vma=False,
    )
```

profile of v0, /device:TPU:0, one launch (start us, length us, event | category | flops | bytes accessed | tf_op | source)
XLA Modules:
  0.0 466.2 jit_solution(13708435990625315921)
XLA Ops:
  7.2 0.0 all-gather.5.cloned.1.call-start
  7.2 8.5 %all_gather.14 = f32[32,1024]{1,0:T(8,128)} all-gather(f32[8,1024]{1,0:T(8,128)} %param.16), channel_id=1, replica_groups=mesh['spec'=4,'neuron'=8] {'spec'}, dimensions={0}, use_global_device_ids=true | all-gather | bytes 163840 | tf_op jit(solution)/shard_map/all_gather | solution.py:30
  15.7 0.0 all-gather.3.cloned.1.call-start
  15.8 6.1 %all_gather.12 = f32[32,1024]{1,0:T(8,128)} all-gather(f32[8,1024]{1,0:T(8,128)} %param.15), channel_id=1, replica_groups=mesh['spec'=4,'neuron'=8] {'spec'}, dimensions={0}, use_global_device_ids=true | all-gather | bytes 163840 | tf_op jit(solution)/shard_map/all_gather | solution.py:29
  21.9 0.0 reduce-scatter.2.cloned.1.call-start
  22.0 2.1 fusion.7
  24.0 1.8 fusion.8
  25.9 20.7 %compare_and_fusion.1 = (pred[512]{0:T(512)(128)(4,1)S(1)}, s32[512]{0:T(512)S(1)}) fusion(s32[]{:T(128)} %bitcast.31, s32[]{:T(128)} %bitcast.30, s32[]{:T(128)} %bitcast.29, s32[]{:T(128)} %bitcast.28, s32[]{:T(128)} %bitcast.27, s32[]{:T(128)} %bitcast.26, s32[]{:T(128)} %bitcast.25, s32[]{:T(128)} %bitcast.24, s32[]{:T(128)} %bitcast.23, s32[]{:T(128)} %bitcast.22, ...), kind=kLoop, calls=%fused_computation.33 | loop fusion | flops 38400 | bytes 4736 | tf_op jit(solution)/shard_map/jit(_take)/and | solution.py:38
  46.6 2.3 gather_fusion
  48.9 2.3 gather_fusion.1
  51.3 5.2 %all-gather.5.cloned.1.call-done = f32[32,8192]{1,0:T(8,128)} async-done(((f32[32,1024]{1,0:T(8,128)}), f32[32,8192]{1,0:T(8,128)}) %all-gather.5.cloned.1.call-update) | async-done | bytes 1048592 | tf_op jit(solution)/shard_map/all_gather | solution.py:34
  56.6 18.4 %fusion = f32[32,512]{1,0:T(8,128)S(1)} fusion(f32[32,8192]{1,0:T(8,128)} %all-gather.5.cloned.1.call-done, f32[512,8192]{1,0:T(8,128)} %param.17), kind=kOutput, calls=%fused_computation.6 | convolution fusion | flops 1614807040 | bytes 17891328 | tf_op jit(solution)/shard_map/dot_general | solution.py:22
  75.0 22.7 %all-gather.3.cloned.1.call-done = f32[32,8192]{1,0:T(8,128)} async-done(((f32[32,1024]{1,0:T(8,128)}), f32[32,8192]{1,0:T(8,128)}) %all-gather.3.cloned.1.call-update) | async-done | bytes 1048592 | tf_op jit(solution)/shard_map/all_gather | solution.py:33
  97.7 18.4 %select_select_fusion = (f32[32,512]{1,0:T(8,128)S(1)}, f32[32,512]{1,0:T(8,128)S(1)}) fusion(s32[32,512]{1,0:T(8,128)S(1)} %copy-done.3, f32[32,512]{1,0:T(8,128)S(1)} %fusion, f32[512]{0:T(512)S(1)} %copy-done.5, f32[32,8192]{1,0:T(8,128)} %all-gather.3.cloned.1.call-done, f32[512,8192]{1,0:T(8,128)} %param.17), kind=kOutput, calls=%fused_computation.22 | convolution fusion | flops 1610809344 | bytes 18089984 | tf_op jit(solution)/shard_map/dot_general | solution.py:21
  116.1 1.6 gather_fusion.2
  117.8 2.3 gather_fusion.5
  120.1 2.5 fusion.4
  122.6 32.0 %convolution_bitcast_fusion = f32[8192,512]{0,1:T(8,128)} fusion(f32[512,8192]{1,0:T(8,128)} %param.17, f32[512,512]{1,0:T(8,128)S(1)} %get-tuple-element.7, f32[512,512]{1,0:T(8,128)S(1)} %gather_fusion.2, pred[512]{0:T(512)(128)(4,1)S(1)} %compare_and_fusion.2), kind=kOutput, calls=%fused_computation.8 | convolution fusion | flops 25770328064 | bytes 35652096 | tf_op jit(solution)/shard_map/dot_general | solution.py:45
  154.6 0.9 copy-done.1
  155.5 2.7 gather_fusion.4
  158.2 2.7 gather_fusion.3
  160.9 275.1 %reduce-scatter.2.cloned.1.call-done = f32[1024,512]{0,1:T(8,128)} async-done(((f32[8192,512]{0,1:T(8,128)}), f32[1024,512]{0,1:T(8,128)}) %reduce-scatter.2.cloned.1.call-update) | async-done | bytes 2097168 | tf_op jit(solution)/shard_map/reduce_scatter | solution.py:44
  436.0 3.5 fusion.3
  439.5 20.1 %psum.7 = f32[512]{0:T(512)} all-reduce(f32[512]{0:T(512)S(1)} %add_add_fusion), channel_id=1, replica_groups=mesh['spec'=4,'neuron'=8] {'neuron'}, use_global_device_ids=true, to_apply=%region_4.8 | all-reduce | flops 512 | bytes 4096 | tf_op jit(solution)/shard_map/psum | solution.py:53
  (24 shorter events, 0.1 us)
Async XLA Ops:
  7.2 39.4 %copy-start = (f32[1000,512]{1,0:T(8,128)S(1)}, f32[1000,512]{1,0:T(8,128)}, u32[]{:S(2)}) copy-start(f32[1000,512]{1,0:T(8,128)} %param.19) | copy-start | bytes 6144004
  7.2 49.4 %all-gather.5.cloned.1.call-start = ((), (), s32[]{:S(2)}) async-start(), calls=%async_computation.2 | async-start | bytes 1179648 | tf_op jit(solution)/shard_map/all_gather | solution.py:34
  15.7 82.0 %all-gather.3.cloned.1.call-start = ((), (), s32[]{:S(2)}) async-start(), calls=%async_computation.1 | async-start | bytes 1179648 | tf_op jit(solution)/shard_map/all_gather | solution.py:33
  21.9 414.1 %reduce-scatter.2.cloned.1.call-start = ((), (), s32[]{:S(2)}) async-start(), calls=%async_computation.3 | async-start | bytes 18874368 | tf_op jit(solution)/shard_map/reduce_scatter | solution.py:44
  46.6 2.3 copy-start.6
  48.9 2.4 copy-start.4
  51.3 46.4 %copy-start.3 = (s32[32,512]{1,0:T(8,128)S(1)}, s32[32,512]{1,0:T(8,128)}, u32[]{:S(2)}) copy-start(s32[32,512]{1,0:T(8,128)} %param.20) | copy-start | bytes 196612
  51.3 46.4 %copy-start.5 = (f32[512]{0:T(512)S(1)}, f32[512]{0:T(512)}, u32[]{:S(2)}) copy-start(f32[512]{0:T(512)} %param.18) | copy-start | bytes 6148
  154.6 0.9 copy-start.1
  155.5 2.7 copy-start.2
Sparse Core Ops, SparseCore 0:
  15.9 40.6 all-gather.4
  58.7 38.9 all-gather.2
  154.7 281.2 reduce-scatter.1
where the time goes:
time: 467 us; the launch traced here: 466 us
  waiting for transfers between devices  303 us (65%)
  matrix products  68.8 us (15%)
  blocking collectives  34.7 us (7%)
  other arithmetic  26.7 us (6%)
  local copies, waits for them, and re-layouts  18.8 us (4%)
  between operations  13.9 us (3%)
    reduce_scatter x1, waiting for transfers between devices, local(): lax.psum_scatter(lax.dot_general(weight, scaled, (((0,), (1,)), ((), ()))...  275 us
    dot_general x1, matrix products, local(): lax.dot_general(weight, scaled, (((0,), (1,)), ((), ())), precision=highest)  32 us
    all_gather x1, waiting for transfers between devices, local(): lax.all_gather(center_all, 'neuron', axis=1, tiled=True)  22.7 us
    and x1, other arithmetic, local(): jnp.take(out_weight, true_class, axis=0)  20.7 us
    psum x1, blocking collectives, local(): margin_bounds = lax.psum(input_part + relax_part, 'neuron')  20.1 us
    dot_general x1, matrix products, interval(): lax.dot_general(radius_full, jnp.abs(weight), dims, precision=highest)  18.4 us
    dot_general x1, matrix products, interval(): lax.dot_general(center_full, weight, dims, precision=highest) + bias  18.4 us
  transfers between devices with their start and end apart: 3, of which 3 were waited for; matrix products, arithmetic and copies ran while one was open for 11% of the time, Pallas kernels for 0%

commit v1 on v0

v1 whole, which is shorter than its diff:
```python
import functools

import jax
import jax.numpy as jnp
from jax import lax
from jax.experimental import pallas as pl
from jax.experimental.pallas import tpu as pltpu
from jax.sharding import PartitionSpec as P

QUARTERS = 4
F32, BF16 = jnp.float32, jnp.bfloat16
ROWS = (((1,), (0,)), ((), ()))
BOTH = (((1,), (1,)), ((), ()))


def swap(array, axis, size, k):
    return lax.ppermute(array, axis, [(i, i ^ k) for i in range(size)])


def in_order(*values):
    return lax.optimization_barrier(values)


def dot(a, b, dims=ROWS):
    return lax.dot_general(a, b, dims, preferred_element_type=F32)


def two_terms(x):
    high = x.astype(BF16)
    return high, (x - high.astype(F32)).astype(BF16)


def three_terms(x):
    high, rest = x.astype(BF16), None
    rest = x - high.astype(F32)
    middle = rest.astype(BF16)
    return high, middle, (rest - middle.astype(F32)).astype(BF16)


def one_hot(index, size):
    return (index == lax.broadcasted_iota(jnp.int32, (index.shape[0], size), 1)).astype(F32)


def row_sums(x):
    ones = jnp.ones((8, x.shape[1]), BF16)
    return sum(dot(ones, term, BOTH) for term in three_terms(x))


def scale_kernel(parts, with_relax, at_ref, *refs):
    ow_refs, slopes_ref = refs[:parts], refs[parts]
    rest = refs[parts + 1 :]
    at = at_ref[...]
    first = 3 if with_relax else 0
    size = sum(ref.shape[0] for ref in ow_refs)
    pick = (one_hot(at[:, first : first + 1], size) - one_hot(at[:, first + 1 : first + 2], size)).astype(BF16)
    coeff, low = None, 0
    for ref in ow_refs:
        here = pick[:, low : low + ref.shape[0]]
        low += ref.shape[0]
        high_ow, low_ow = two_terms(ref[...])
        got = dot(here, high_ow) + dot(here, low_ow)
        coeff = got if coeff is None else coeff + got
    image = one_hot(at[:, 2:3], slopes_ref.shape[0]).astype(BF16)
    scaled = coeff * sum(dot(image, term) for term in three_terms(slopes_ref[...]))
    if with_relax:
        offsets_ref, bias_ref, high_ref, low_ref, relax_ref = rest
        offsets = sum(dot(image, term) for term in three_terms(offsets_ref[...]))
        relax_ref[...] = row_sums(scaled * bias_ref[...] - jnp.minimum(coeff, 0.0) * offsets)
    else:
        high_ref, low_ref = rest
    high_ref[...], low_ref[...] = two_terms(scaled)


def scale(at, ow_parts, slopes, offsets=None, bias=None):
    specs, rows = at.shape[0], slopes.shape[1]
    with_relax = offsets is not None
    outs = [jax.ShapeDtypeStruct((specs, rows), BF16)] * 2
    extra = []
    if with_relax:
        outs = outs + [jax.ShapeDtypeStruct((8, specs), F32)]
        extra = [offsets, bias]
    size = sum(part.shape[0] for part in ow_parts)
    return pl.pallas_call(
        functools.partial(scale_kernel, len(ow_parts), with_relax),
        out_shape=outs,
        compiler_params=pltpu.CompilerParams(vmem_limit_bytes=40 * 2**20),
        cost_estimate=pl.CostEstimate(
            flops=4 * specs * size * rows, bytes_accessed=4 * size * rows + 4 * specs * rows, transcendentals=0
        ),
    )(at, *ow_parts, slopes, *extra)


def product_kernel(group, final, col_ref, *refs):
    scaled_refs, w_refs = refs[: 2 * group], refs[2 * group : 3 * group]
    rest = refs[3 * group :]
    w_high, w_low = rest[-2:]
    rows = w_refs[0].shape[0]

    @pl.when(pl.program_id(0) == 0)
    def _():
        for j, ref in enumerate(w_refs):
            w_high[pl.ds(j * rows, rows), :], w_low[pl.ds(j * rows, rows), :] = two_terms(ref[...])

    total = None
    for j in range(group):
        high, low = scaled_refs[2 * j][...], scaled_refs[2 * j + 1][...]
        wh, wl = w_high[pl.ds(j * rows, rows), :], w_low[pl.ds(j * rows, rows), :]
        got = dot(high, wh) + (dot(high, wl) + dot(low, wh))
        total = got if total is None else total + got
    if not final:
        rest[0][...] = total
        return
    sums, near = final
    sum_refs, (at_ref, center_ref, radius_ref, margin_in), (out_ref, margin_ref) = (
        rest[:sums],
        rest[sums : sums + 4],
        rest[-4:-2],
    )
    for ref in sum_refs:
        total = total + ref[...]
    out_ref[...] = total
    image = one_hot(at_ref[...][:, 2:3], near).astype(BF16)
    center = sum(dot(image, term) for term in three_terms(center_ref[...]))
    radius = sum(dot(image, term) for term in three_terms(radius_ref[...]))
    margin_ref[...] = margin_in[...] + row_sums(total * center - jnp.abs(total) * radius)


def product(scaled, weight, col, w_parts, final=None):
    specs, rows = scaled[0].shape
    group = len(scaled) // 2
    piece = w_parts[0][0].shape[-1]
    step = min(specs, 128)
    in_specs = [pl.BlockSpec((step, rows), lambda i, col: (i, 0)) for _ in scaled]
    in_specs.append(pl.BlockSpec((rows, piece), lambda i, col: (0, col[0])))
    args = [*scaled, weight]
    for array, place in w_parts:
        if array.ndim == 3:
            in_specs.append(pl.BlockSpec((None, rows, piece), lambda i, col, place=place: (place, 0, 0)))
        else:
            in_specs.append(pl.BlockSpec((rows, piece), lambda i, col: (0, 0)))
        args.append(array)
    block = pl.BlockSpec((step, piece), lambda i, col: (i, 0))
    kept = None
    aliases = {}
    if final is None:
        out_shape = jax.ShapeDtypeStruct((specs, piece), F32)
        out_specs = block
    else:
        sums, at, center, radius, margin, out = final
        near = center.shape[0]
        kept = (len(sums), near)
        in_specs += [block] * len(sums)
        box = pl.BlockSpec((near, piece), lambda i, col: (0, col[1]))
        line = pl.BlockSpec((8, step), lambda i, col: (0, i))
        in_specs += [pl.BlockSpec((step, at.shape[1]), lambda i, col: (i, 0)), box, box, line]
        args += [*sums, at, center, radius, margin]
        if out is not None:
            in_specs.append(pl.BlockSpec(memory_space=pl.ANY))
            args.append(out)
            aliases = {len(args): 0}
        out_shape = [jax.ShapeDtypeStruct((specs, QUARTERS * piece), F32), jax.ShapeDtypeStruct((8, specs), F32)]
        out_specs = [pl.BlockSpec((step, piece), lambda i, col: (i, col[1])), line]
    return pl.pallas_call(
        functools.partial(product_kernel, group, kept),
        out_shape=out_shape,
        grid_spec=pltpu.PrefetchScalarGridSpec(
            num_scalar_prefetch=1,
            grid=(specs // step,),
            in_specs=in_specs,
            out_specs=out_specs,
            scratch_shapes=[pltpu.VMEM((group * rows, piece), BF16)] * 2,
        ),
        input_output_aliases=aliases,
        compiler_params=pltpu.CompilerParams(vmem_limit_bytes=40 * 2**20),
        cost_estimate=pl.CostEstimate(
            flops=6 * specs * group * rows * piece, bytes_accessed=4 * group * rows * (specs + piece), transcendentals=0
        ),
    )(col, *args)


def local(members, sites, center, radius, weight, bias, out_weight, masks, image_labels, runner_up, spec_image):
    g, n = lax.axis_index("spec"), lax.axis_index("neuron")
    q = g % QUARTERS
    rows, cols = weight.shape[0], center.shape[1]
    images, specs, classes = center.shape[0], spec_image.shape[0], out_weight.shape[0]
    piece = cols // QUARTERS
    cut = sites // 2
    group = (0, 1, cut, cut + 1)
    far = [2 * m for m in range(1, sites // 4)]
    over_spec = functools.partial(swap, axis="spec", size=members)
    over_neuron = functools.partial(swap, axis="neuron", size=sites)

    boxes = jnp.stack([center, radius])[None]
    share = -(-classes // QUARTERS // 8) * 8

    def start_of(part):
        return jnp.minimum(part * share, classes - share)

    ow = {0: lax.dynamic_slice(out_weight, (start_of(q), 0), (share, rows))}
    ow[cut] = over_neuron(ow[0], k=cut)
    ow[1] = over_neuron(ow[0], k=1)
    ow[cut + 1] = over_neuron(ow[cut], k=1)

    order = [0]
    k = cut
    while k:
        boxes = jnp.concatenate([boxes, over_neuron(boxes, k=k)])
        order = order + [o ^ k for o in order]
        k //= 2
    spot = [order.index(o) for o in range(sites)]

    def columns(block):
        return lax.dynamic_slice(weight, (0, block * cols + q * piece), (rows, piece))

    targets = far + [0]
    home, last = {}, [boxes, ow[cut]]
    for t in targets:
        for j in (cut, cut + 1):
            send, last[0] = in_order(columns(n ^ j ^ t), last[0])
            home[t, j] = over_neuron(send, k=j)
            last = [last[1], home[t, j]]
    boxes, ow[cut] = boxes, ow[cut]
    beside = jnp.stack([columns(n ^ 1 ^ t) for t in targets])
    beside = over_neuron(beside, k=1)

    def spread(x):
        x2 = over_spec(x, k=2)
        return [x, over_spec(x, k=1), x2, over_spec(x2, k=1)]

    ow_parts = {j: spread(ow[j]) for j in group[1:]}
    beside_parts = spread(beside)
    w_parts = {key: spread(x) for key, x in home.items()}

    natural = jnp.zeros((sites,), jnp.int32)
    for o, s in enumerate(spot):
        natural = jnp.where((n ^ jnp.arange(sites)) == o, s, natural)
    full = jnp.take(boxes, natural, axis=0).transpose(1, 2, 0, 3).reshape(2, images, sites * cols)
    dims = (((1,), (1,)), ((), ()))
    pre_center = lax.dot_general(full[0], weight, dims, precision=lax.Precision.HIGH) + bias
    pre_radius = lax.dot_general(full[1], jnp.abs(weight), dims, precision=lax.Precision.HIGH)
    mask = lax.dynamic_slice(masks, (g * images, 0), (images, rows))
    upper, lower = pre_center + pre_radius, pre_center - pre_radius
    slope = jnp.clip(upper / (upper - lower), 0.0, 1.0)
    slopes = jnp.where(mask == 1, 1.0, jnp.where(mask == 2, slope, 0.0))
    offsets = jnp.where(mask == 2, slope * lower, 0.0)
    both = jnp.stack([slopes, offsets])
    near = jnp.stack([center, radius])
    k = 1
    while k < members:
        both = jnp.concatenate([both, over_spec(both, k=k)], axis=1)
        near = jnp.concatenate([near, over_spec(near, k=k)], axis=1)
        k *= 2
    slopes = {0: both[0]}
    slopes[cut] = over_neuron(slopes[0], k=cut)
    slopes[1] = over_neuron(slopes[0], k=1)
    slopes[cut + 1] = over_neuron(slopes[cut], k=1)

    labels = jnp.sum(jnp.where(spec_image[:, None] == jnp.arange(image_labels.shape[0]), image_labels, 0), axis=1)

    def place(label):
        part = label // share
        return (part ^ q) * share + label - start_of(part)

    at = jnp.stack(
        [
            place(labels),
            place(runner_up),
            ((spec_image // images) ^ g) * images + spec_image % images,
            labels,
            runner_up,
        ],
        axis=1,
    )
    *scaled, margin = scale(at, [out_weight], slopes[0], both[1], bias[None])
    for j in group[1:]:
        scaled += scale(at, ow_parts[j], slopes[j])

    out, sums = None, [[] for _ in range(QUARTERS)]
    for i, t in enumerate(targets):
        for r in range(QUARTERS):
            parts = [(beside_parts[r], i), (w_parts[t, cut][r], 0), (w_parts[t, cut + 1][r], 0)]
            col = jnp.stack([(n ^ t) * QUARTERS + (q ^ r), q ^ r])
            if t:
                sums[r].append(over_neuron(product(scaled, weight, col, parts), k=t))
            else:
                out, margin = product(
                    scaled, weight, col, parts, (sums[r], at, near[0], near[1], margin, out)
                )
    k = 1
    while k < sites:
        margin = margin + over_neuron(margin, k=k)
        k *= 2
    return out, margin[0]


def solution(mesh):
    members, sites = mesh.shape["spec"], mesh.shape["neuron"]
    return jax.shard_map(
        functools.partial(local, members, sites),
        mesh=mesh,
        in_specs=(
            P("spec", "neuron"),
            P("spec", "neuron"),
            P("neuron", None),
            P("neuron"),
            P(None, "neuron"),
            P(None, "neuron"),
            P(),
            P("spec"),
            P("spec"),
        ),
        out_specs=(P("spec", "neuron"), P("spec")),
        check_vma=False,
    )
```

time: 467 us -> 287 us (0.61)
  waiting for transfers between devices: 303 us -> 128 us
  Pallas kernels: 0 us -> 53.1 us
  starting transfers between devices: 0.12 us -> 51.3 us
  matrix products: 68.8 us -> 19.1 us
  blocking collectives: 34.7 us -> 0 us
  other arithmetic: 26.7 us -> 3.72 us
  between operations: 13.9 us -> 1.17 us
  local copies, waits for them, and re-layouts: 18.8 us -> 29.4 us
    reduce_scatter x1 -> x0, waiting for transfers between devices: 275 us -> none  [local(): lax.psum_scatter(lax.dot_general(weight, scaled, (((0,), (1,)), ((), ()))...]
    ppermute x0 -> x49, waiting for transfers between devices: none -> 128 us  [swap(): return lax.ppermute(array, axis, [(i, i ^ k) for i in range(size)])]
    pallas_call x0 -> x12, Pallas kernels: none -> 53.1 us  [the longest x8 43.2 us: product(): pl.pallas_call(functools.partial(product_kernel, group, kept), out_shape=...]
    ppermute x0 -> x49, starting transfers between devices: none -> 51.3 us  [swap(): return lax.ppermute(array, axis, [(i, i ^ k) for i in range(size)])]
    dot_general x3 -> x2, matrix products: 68.8 us -> 19.1 us  [the longest x1 12.6 us: local(): lax.dot_general(full[1], jnp.abs(weight), dims, precision=lax.Precision.H...]
    all_gather x2 -> x0, waiting for transfers between devices: 27.9 us -> none  [the longest x1 22.7 us: local(): lax.all_gather(center_all, 'neuron', axis=1, tiled=True)]
    unnamed x14 -> x88, local copies, waits for them, and re-layouts: 0.92 us -> 22 us
    and x3 -> x0, other arithmetic: 20.7 us -> none  [the longest x1 20.7 us: local(): jnp.take(out_weight, true_class, axis=0)]
  transfers between devices with their start and end apart: 3 -> 49, of which waited for: 3 -> 18; matrix products, arithmetic and copies ran while one was open for 11% -> 10% of each run, Pallas kernels for 0% -> 16%
where the time goes in v1:
time: 287 us; the launch traced here: 286 us
  waiting for transfers between devices  128 us (45%)
  Pallas kernels  53.1 us (19%)
  starting transfers between devices  51.3 us (18%)
  local copies, waits for them, and re-layouts  29.4 us (10%)
  matrix products  19.1 us (7%)
  other arithmetic  3.72 us (1%)
    ppermute x49, waiting for transfers between devices, swap(): return lax.ppermute(array, axis, [(i, i ^ k) for i in range(size)])  128 us
    ppermute x49, starting transfers between devices, swap(): return lax.ppermute(array, axis, [(i, i ^ k) for i in range(size)])  51.3 us
    pallas_call x8, Pallas kernels, product(): pl.pallas_call(functools.partial(product_kernel, group, kept), out_shape=...  43.2 us
    unnamed x88, local copies, waits for them, and re-layouts  22 us
    dot_general x1, matrix products, local(): lax.dot_general(full[1], jnp.abs(weight), dims, precision=lax.Precision.H...  12.6 us
    pallas_call x4, Pallas kernels, scale(): pl.pallas_call(functools.partial(scale_kernel, len(ow_parts), with_relax)...  9.92 us
    dot_general x1, matrix products, local(): lax.dot_general(full[0], weight, dims, precision=lax.Precision.HIGH) + bias  6.58 us
  transfers between devices with their start and end apart: 49, of which 18 were waited for; matrix products, arithmetic and copies ran while one was open for 10% of the time, Pallas kernels for 16%

profile of v1, /device:TPU:0, one launch (start us, length us, event | category | flops | bytes accessed | tf_op | source)
XLA Modules:
  0.0 285.6 jit_solution(16028765884456319255)
XLA Ops:
  1.4 4.1 %collective-permute-start = (f32[1,2,8,1024]{3,2,1,0:T(8,128)S(1)}, f32[1,2,8,1024]{3,2,1,0:T(8,128)S(1)}, u32[]{:S(2)}, u32[]{:S(2)}) collective-permute-start(f32[1,2,8,1024]{3,2,1,0:T(8,128)S(1)} %get-tuple-element.59), channel_id=1, source_target_pairs={{0,4},{1,5},{2,6},{3,7},{4,0},{5,1},{6,2},{7,3},{8,12},{9,13},{10,... | collective-permute-start | bytes 196616 | tf_op jit(solution)/shard_map/ppermute | solution.py:17
  9.3 11.6 %collective-permute-start.1 = (f32[2,2,8,1024]{3,2,1,0:T(8,128)S(1)}, f32[2,2,8,1024]{3,2,1,0:T(8,128)S(1)}, u32[]{:S(2)}, u32[]{:S(2)}) collective-permute-start(f32[2,2,8,1024]{3,2,1,0:T(8,128)S(1)} %pad_maximum_fusion.4), channel_id=1, source_target_pairs={{0,2},{1,3},{2,0},{3,1},{4,6},{5,7},{6,4},{7,5},{8,10},{9,11},{10,... | collective-permute-start | bytes 393224 | tf_op jit(solution)/shard_map/ppermute | solution.py:17
  21.0 13.1 %collective-permute-done.1 = f32[2,2,8,1024]{3,2,1,0:T(8,128)S(1)} collective-permute-done((f32[2,2,8,1024]{3,2,1,0:T(8,128)S(1)}, f32[2,2,8,1024]{3,2,1,0:T(8,128)S(1)}, u32[]{:S(2)}, u32[]{:S(2)}) %collective-permute-start.1) | collective-permute-done | bytes 131104 | tf_op jit(solution)/shard_map/ppermute | solution.py:17
  41.4 12.6 %fusion = f32[8,512]{1,0:T(8,128)S(1)} fusion(f32[8,8192]{1,0:T(8,128)S(1)} %bitcast.48, f32[512,8192]{1,0:T(8,128)} %refs_8_.15), kind=kOutput, calls=%fused_computation.1 | convolution fusion | flops 205520896 | bytes 17055744 | tf_op jit(solution)/shard_map/dot_general | solution.py:240
  53.9 6.6 %convolution_add_fusion = f32[8,512]{1,0:T(8,128)S(1)} fusion(f32[8,8192]{1,0:T(8,128)S(1)} %bitcast.49, f32[512,8192]{1,0:T(8,128)S(1)} %copy-done.31, f32[512]{0:T(512)S(1)} %copy-done.5), kind=kOutput, calls=%fused_computation.3 | convolution fusion | flops 201330688 | bytes 17057792 | tf_op jit(solution)/shard_map/dot_general | solution.py:239
  63.0 4.0 %collective-permute-start.23 = (f32[512,256]{1,0:T(8,128)S(1)}, f32[512,256]{1,0:T(8,128)S(1)}, u32[]{:S(2)}, u32[]{:S(2)}) collective-permute-start(f32[512,256]{1,0:T(8,128)S(1)} %copy-done.32), channel_id=1, source_target_pairs={{0,4},{1,5},{2,6},{3,7},{4,0},{5,1},{6,2},{7,3},{8,12},{9,13},{10,... | collective-permute-start | bytes 1572872 | tf_op jit(solution)/shard_map/ppermute | solution.py:17
  77.8 15.6 %collective-permute-done.14.refs_4_ = f32[32,512]{1,0:T(8,128)S(1)} collective-permute-done((f32[32,512]{1,0:T(8,128)S(1)}, f32[32,512]{1,0:T(8,128)S(1)}, u32[]{:S(2)}, u32[]{:S(2)}) %collective-permute-start.14) | collective-permute-done | bytes 65568 | tf_op jit(solution)/shard_map/ppermute | solution.py:17
  95.0 4.8 %collective-permute-done.9.refs_4_ = f32[32,512]{1,0:T(8,128)S(1)} collective-permute-done((f32[32,512]{1,0:T(8,128)S(1)}, f32[32,512]{1,0:T(8,128)S(1)}, u32[]{:S(2)}, u32[]{:S(2)}) %collective-permute-start.9) | collective-permute-done | bytes 65568 | tf_op jit(solution)/shard_map/ppermute | solution.py:17
  107.4 5.1 %collective-permute-start.27 = (f32[512,256]{1,0:T(8,128)}, f32[512,256]{1,0:T(8,128)}, u32[]{:S(2)}, u32[]{:S(2)}) collective-permute-start(f32[512,256]{1,0:T(8,128)} %get-tuple-element.33), channel_id=1, source_target_pairs={{0,5},{1,4},{2,7},{3,6},{4,1},{5,0},{6,3},{7,2},{8,13},{9,12},{10,... | collective-permute-start | bytes 1572872 | tf_op jit(solution)/shard_map/ppermute | solution.py:17
  113.3 6.3 %collective-permute-done.7.refs_2_ = f32[256,512]{1,0:T(8,128)S(1)} collective-permute-done((f32[256,512]{1,0:T(8,128)S(1)}, f32[256,512]{1,0:T(8,128)S(1)}, u32[]{:S(2)}, u32[]{:S(2)}) %collective-permute-start.7) | collective-permute-done | bytes 524320 | tf_op jit(solution)/shard_map/ppermute | solution.py:17
  123.4 24.6 %collective-permute-done.27.refs_11_ = f32[512,256]{1,0:T(8,128)} collective-permute-done((f32[512,256]{1,0:T(8,128)}, f32[512,256]{1,0:T(8,128)}, u32[]{:S(2)}, u32[]{:S(2)}) %collective-permute-start.27) | collective-permute-done | bytes 524320 | tf_op jit(solution)/shard_map/ppermute | solution.py:17
  149.1 8.7 %collective-permute-done.24.refs_10_ = f32[512,256]{1,0:T(8,128)S(1)} collective-permute-done((f32[512,256]{1,0:T(8,128)}, f32[512,256]{1,0:T(8,128)S(1)}, u32[]{:S(2)}, u32[]{:S(2)}) %collective-permute-start.24) | collective-permute-done | bytes 524320 | tf_op jit(solution)/shard_map/ppermute | solution.py:17
  164.0 20.8 %collective-permute-done.28.refs_11_ = f32[512,256]{1,0:T(8,128)} collective-permute-done((f32[512,256]{1,0:T(8,128)}, f32[512,256]{1,0:T(8,128)}, u32[]{:S(2)}, u32[]{:S(2)}) %collective-permute-start.28) | collective-permute-done | bytes 524320 | tf_op jit(solution)/shard_map/ppermute | solution.py:17
  212.3 4.5 %shard_map.111 = f32[512,256]{1,0:T(8,128)S(1)} custom-call(s32[2]{0:T(128)S(1)} %pad_add_fusion.7.col_ref, bf16[512,512]{1,0:T(8,128)(2,1)S(1)} %get-tuple-element.23.refs_0_, bf16[512,512]{1,0:T(8,128)(2,1)S(1)} %get-tuple-element.24.refs_1_, bf16[512,512]{1,0:T(8,128)(2,1)S(1)} %get-tuple-element.25.refs_2_, ...), custom_call_target="tpu_custom_call" | custom-call | flops 1610612736 | bytes 6291456 | tf_op jit(solution)/shard_map/pallas_call | solution.py:163
  219.2 4.7 %shard_map.109 = f32[512,256]{1,0:T(8,128)S(1)} custom-call(s32[2]{0:T(128)S(1)} %pad_add_fusion.3.col_ref, bf16[512,512]{1,0:T(8,128)(2,1)S(1)} %get-tuple-element.23.refs_0_, bf16[512,512]{1,0:T(8,128)(2,1)S(1)} %get-tuple-element.24.refs_1_, bf16[512,512]{1,0:T(8,128)(2,1)S(1)} %get-tuple-element.25.refs_2_, ...), custom_call_target="tpu_custom_call" | custom-call | flops 1610612736 | bytes 6291456 | tf_op jit(solution)/shard_map/pallas_call | solution.py:163
  223.9 4.7 %shard_map.110 = f32[512,256]{1,0:T(8,128)S(1)} custom-call(s32[2]{0:T(128)S(1)} %pad_add_fusion.5.col_ref, bf16[512,512]{1,0:T(8,128)(2,1)S(1)} %get-tuple-element.23.refs_0_, bf16[512,512]{1,0:T(8,128)(2,1)S(1)} %get-tuple-element.24.refs_1_, bf16[512,512]{1,0:T(8,128)(2,1)S(1)} %get-tuple-element.25.refs_2_, ...), custom_call_target="tpu_custom_call" | custom-call | flops 1610612736 | bytes 6291456 | tf_op jit(solution)/shard_map/pallas_call | solution.py:163
  230.7 4.4 %shard_map.108 = f32[512,256]{1,0:T(8,128)S(1)} custom-call(s32[2]{0:T(128)S(1)} %pad_add_fusion.1.col_ref, bf16[512,512]{1,0:T(8,128)(2,1)S(1)} %get-tuple-element.23.refs_0_, bf16[512,512]{1,0:T(8,128)(2,1)S(1)} %get-tuple-element.24.refs_1_, bf16[512,512]{1,0:T(8,128)(2,1)S(1)} %get-tuple-element.25.refs_2_, ...), custom_call_target="tpu_custom_call" | custom-call | flops 1610612736 | bytes 6291456 | tf_op jit(solution)/shard_map/pallas_call | solution.py:163
  235.3 7.1 %collective-permute-done.29.refs_11_ = f32[512,256]{1,0:T(8,128)S(1)} collective-permute-done((f32[512,256]{1,0:T(8,128)}, f32[512,256]{1,0:T(8,128)S(1)}, u32[]{:S(2)}, u32[]{:S(2)}) %collective-permute-start.29) | collective-permute-done | bytes 524320 | tf_op jit(solution)/shard_map/ppermute | solution.py:17
  242.5 6.3 %shard_map.112 = (f32[512,1024]{1,0:T(8,128)}, f32[8,512]{1,0:T(8,128)S(1)}) custom-call(s32[2]{0:T(128)S(1)} %copy-done.6, bf16[512,512]{1,0:T(8,128)(2,1)S(1)} %get-tuple-element.23.refs_0_, bf16[512,512]{1,0:T(8,128)(2,1)S(1)} %get-tuple-element.24.refs_1_, bf16[512,512]{1,0:T(8,128)(2,1)S(1)} %get-tuple-element.25.refs_2_, ...), custom_call_target="tpu_custom_call" | custom-call | flops 1610612736 | bytes 6291456 | tf_op jit(solution)/shard_map/pallas_call | solution.py:163
  248.8 6.2 %shard_map.113 = (f32[512,1024]{1,0:T(8,128)}, f32[8,512]{1,0:T(8,128)S(1)}) custom-call(s32[2]{0:T(128)S(1)} %pad_add_fusion.4.col_ref, bf16[512,512]{1,0:T(8,128)(2,1)S(1)} %get-tuple-element.23.refs_0_, bf16[512,512]{1,0:T(8,128)(2,1)S(1)} %get-tuple-element.24.refs_1_, ...), custom_call_target="tpu_custom_call", output_to_operand_aliasing={{0}: (18, {})} | custom-call | flops 1610612736 | bytes 6291456 | tf_op jit(solution)/shard_map/pallas_call | solution.py:163
  256.4 6.2 %shard_map.114 = (f32[512,1024]{1,0:T(8,128)}, f32[8,512]{1,0:T(8,128)S(1)}) custom-call(s32[2]{0:T(128)S(1)} %pad_add_fusion.2.col_ref, bf16[512,512]{1,0:T(8,128)(2,1)S(1)} %get-tuple-element.23.refs_0_, bf16[512,512]{1,0:T(8,128)(2,1)S(1)} %get-tuple-element.24.refs_1_, ...), custom_call_target="tpu_custom_call", output_to_operand_aliasing={{0}: (18, {})} | custom-call | flops 1610612736 | bytes 6291456 | tf_op jit(solution)/shard_map/pallas_call | solution.py:163
  262.5 4.2 %collective-permute-done.35.refs_12_ = f32[512,256]{1,0:T(8,128)S(1)} collective-permute-done((f32[512,256]{1,0:T(8,128)S(1)}, f32[512,256]{1,0:T(8,128)S(1)}, u32[]{:S(2)}, u32[]{:S(2)}) %collective-permute-start.35) | collective-permute-done | bytes 524320 | tf_op jit(solution)/shard_map/ppermute | solution.py:17
  266.7 6.2 %shard_map.115 = (f32[512,1024]{1,0:T(8,128)}, f32[8,512]{1,0:T(8,128)S(1)}) custom-call(s32[2]{0:T(128)S(1)} %pad_add_fusion.col_ref, bf16[512,512]{1,0:T(8,128)(2,1)S(1)} %get-tuple-element.23.refs_0_, bf16[512,512]{1,0:T(8,128)(2,1)S(1)} %get-tuple-element.24.refs_1_, ...), custom_call_target="tpu_custom_call", output_to_operand_aliasing={{0}: (18, {})} | custom-call | flops 1610612736 | bytes 6291456 | tf_op jit(solution)/shard_map/pallas_call | solution.py:163
  280.4 4.6 %collective-permute-done.48 = f32[8,512]{1,0:T(8,128)S(1)} collective-permute-done((f32[8,512]{1,0:T(8,128)S(1)}, f32[8,512]{1,0:T(8,128)S(1)}, u32[]{:S(2)}, u32[]{:S(2)}) %collective-permute-start.48) | collective-permute-done | bytes 16416 | tf_op jit(solution)/shard_map/ppermute | solution.py:17
  (214 shorter events, 87.6 us)
Async XLA Ops:
  7.4 61.2 %collective-permute-start.10 = (f32[256,512]{1,0:T(8,128)}, f32[256,512]{1,0:T(8,128)S(1)}, u32[]{:S(2)}, u32[]{:S(2)}) collective-permute-start(f32[256,512]{1,0:T(8,128)} %constant_dynamic-slice_fusion.4), channel_id=1, source_target_pairs={{0,4},{1,5},{2,6},{3,7},{4,0},{5,1},{6,2},{7,3},{8,12},{9,13},{10,... | collective-permute-start | bytes 1572872 | tf_op jit(solution)/shard_map/ppermute | solution.py:17
  7.5 69.8 %collective-permute-start.5 = (f32[256,512]{1,0:T(8,128)}, f32[256,512]{1,0:T(8,128)S(1)}, u32[]{:S(2)}, u32[]{:S(2)}) collective-permute-start(f32[256,512]{1,0:T(8,128)} %constant_dynamic-slice_fusion.4), channel_id=1, source_target_pairs={{0,1},{1,0},{2,3},{3,2},{4,5},{5,4},{6,7},{7,6},{8,9},{9,8},{10,11... | collective-permute-start | bytes 1572872 | tf_op jit(solution)/shard_map/ppermute | solution.py:17
  9.3 24.7 %collective-permute-start.1 = (f32[2,2,8,1024]{3,2,1,0:T(8,128)S(1)}, f32[2,2,8,1024]{3,2,1,0:T(8,128)S(1)}, u32[]{:S(2)}, u32[]{:S(2)}) collective-permute-start(f32[2,2,8,1024]{3,2,1,0:T(8,128)S(1)} %pad_maximum_fusion.4), channel_id=1, source_target_pairs={{0,2},{1,3},{2,0},{3,1},{4,6},{5,7},{6,4},{7,5},{8,10},{9,11},{10,... | collective-permute-start | bytes 393224 | tf_op jit(solution)/shard_map/ppermute | solution.py:17
  61.5 51.8 %collective-permute-start.20 = (f32[2,512,256]{2,1,0:T(8,128)S(1)}, f32[2,512,256]{2,1,0:T(8,128)S(1)}, u32[]{:S(2)}, u32[]{:S(2)}) collective-permute-start(f32[2,512,256]{2,1,0:T(8,128)S(1)} %pad_maximum_fusion), channel_id=1, source_target_pairs={{0,1},{1,0},{2,3},{3,2},{4,5},{5,4},{6,7},{7,6},{8,9},{9,8},{10,11... | collective-permute-start | bytes 3145736 | tf_op jit(solution)/shard_map/ppermute | solution.py:17
  63.0 42.2 %collective-permute-start.23 = (f32[512,256]{1,0:T(8,128)S(1)}, f32[512,256]{1,0:T(8,128)S(1)}, u32[]{:S(2)}, u32[]{:S(2)}) collective-permute-start(f32[512,256]{1,0:T(8,128)S(1)} %copy-done.32), channel_id=1, source_target_pairs={{0,4},{1,5},{2,6},{3,7},{4,0},{5,1},{6,2},{7,3},{8,12},{9,13},{10,... | collective-permute-start | bytes 1572872 | tf_op jit(solution)/shard_map/ppermute | solution.py:17
  68.6 37.8 %collective-permute-start.15 = (f32[256,512]{1,0:T(8,128)S(1)}, f32[256,512]{1,0:T(8,128)}, u32[]{:S(2)}, u32[]{:S(2)}) collective-permute-start(f32[256,512]{1,0:T(8,128)S(1)} %collective-permute-done.10.refs_0_), channel_id=1, source_target_pairs={{0,1},{1,0},{2,3},{3,2},{4,5},{5,4},{6,7},{7,6},{8,9},{9,8},{10,11... | collective-permute-start | bytes 1572872 | tf_op jit(solution)/shard_map/ppermute | solution.py:17
  107.4 40.5 %collective-permute-start.27 = (f32[512,256]{1,0:T(8,128)}, f32[512,256]{1,0:T(8,128)}, u32[]{:S(2)}, u32[]{:S(2)}) collective-permute-start(f32[512,256]{1,0:T(8,128)} %get-tuple-element.33), channel_id=1, source_target_pairs={{0,5},{1,4},{2,7},{3,6},{4,1},{5,0},{6,3},{7,2},{8,13},{9,12},{10,... | collective-permute-start | bytes 1572872 | tf_op jit(solution)/shard_map/ppermute | solution.py:17
  113.3 44.5 %collective-permute-start.24 = (f32[512,256]{1,0:T(8,128)}, f32[512,256]{1,0:T(8,128)S(1)}, u32[]{:S(2)}, u32[]{:S(2)}) collective-permute-start(f32[512,256]{1,0:T(8,128)} %get-tuple-element.32), channel_id=1, source_target_pairs={{0,4},{1,5},{2,6},{3,7},{4,0},{5,1},{6,2},{7,3},{8,12},{9,13},{10,... | collective-permute-start | bytes 1572872 | tf_op jit(solution)/shard_map/ppermute | solution.py:17
  113.3 45.1 %collective-permute-start.42 = (f32[512,256]{1,0:T(8,128)S(1)}, f32[512,256]{1,0:T(8,128)}, u32[]{:S(2)}, u32[]{:S(2)}) collective-permute-start(f32[512,256]{1,0:T(8,128)S(1)} %collective-permute-done.23.refs_10_), channel_id=1, source_target_pairs={{0,8},{8,0},{16,24},{24,16},{1,9},{9,1},{17,25},{25,17},{2,10},{10... | collective-permute-start | bytes 1572872 | tf_op jit(solution)/shard_map/ppermute | solution.py:17
  119.6 38.9 %collective-permute-start.31 = (f32[512,256]{1,0:T(8,128)S(1)}, f32[512,256]{1,0:T(8,128)}, u32[]{:S(2)}, u32[]{:S(2)}) collective-permute-start(f32[512,256]{1,0:T(8,128)S(1)} %collective-permute-done.23.refs_10_), channel_id=1, source_target_pairs={{0,16},{8,24},{16,0},{24,8},{1,17},{9,25},{17,1},{25,9},{2,18},{10... | collective-permute-start | bytes 1572872 | tf_op jit(solution)/shard_map/ppermute | solution.py:17
  122.3 36.6 %collective-permute-start.17 = (f32[256,512]{1,0:T(8,128)}, f32[256,512]{1,0:T(8,128)}, u32[]{:S(2)}, u32[]{:S(2)}) collective-permute-start(f32[256,512]{1,0:T(8,128)} %collective-permute-done.15.refs_0_), channel_id=1, source_target_pairs={{0,16},{8,24},{16,0},{24,8},{1,17},{9,25},{17,1},{25,9},{2,18},{10... | collective-permute-start | bytes 1572872 | tf_op jit(solution)/shard_map/ppermute | solution.py:17
  148.0 38.6 %collective-permute-start.21 = (f32[2,512,256]{2,1,0:T(8,128)S(1)}, f32[2,512,256]{2,1,0:T(8,128)S(1)}, u32[]{:S(2)}, u32[]{:S(2)}) collective-permute-start(f32[2,512,256]{2,1,0:T(8,128)S(1)} %collective-permute-done.20.refs_9_), channel_id=1, source_target_pairs={{0,16},{8,24},{16,0},{24,8},{1,17},{9,25},{17,1},{25,9},{2,18},{10... | collective-permute-start | bytes 3145736 | tf_op jit(solution)/shard_map/ppermute | solution.py:17
  157.8 27.0 %collective-permute-start.28 = (f32[512,256]{1,0:T(8,128)}, f32[512,256]{1,0:T(8,128)}, u32[]{:S(2)}, u32[]{:S(2)}) collective-permute-start(f32[512,256]{1,0:T(8,128)} %get-tuple-element.34), channel_id=1, source_target_pairs={{0,5},{1,4},{2,7},{3,6},{4,1},{5,0},{6,3},{7,2},{8,13},{9,12},{10,... | collective-permute-start | bytes 1572872 | tf_op jit(solution)/shard_map/ppermute | solution.py:17
  161.3 56.3 %collective-permute-start.39 = (f32[2,512,256]{2,1,0:T(8,128)S(1)}, f32[2,512,256]{2,1,0:T(8,128)S(1)}, u32[]{:S(2)}, u32[]{:S(2)}) collective-permute-start(f32[2,512,256]{2,1,0:T(8,128)S(1)} %collective-permute-done.20.refs_9_), channel_id=1, source_target_pairs={{0,8},{8,0},{16,24},{24,16},{1,9},{9,1},{17,25},{25,17},{2,10},{10... | collective-permute-start | bytes 3145736 | tf_op jit(solution)/shard_map/ppermute | solution.py:17
  162.3 24.9 %collective-permute-start.43 = (f32[512,256]{1,0:T(8,128)}, f32[512,256]{1,0:T(8,128)}, u32[]{:S(2)}, u32[]{:S(2)}) collective-permute-start(f32[512,256]{1,0:T(8,128)} %collective-permute-done.27.refs_11_), channel_id=1, source_target_pairs={{0,8},{8,0},{16,24},{24,16},{1,9},{9,1},{17,25},{25,17},{2,10},{10... | collective-permute-start | bytes 1572872 | tf_op jit(solution)/shard_map/ppermute | solution.py:17
  163.5 23.8 %collective-permute-start.33 = (f32[512,256]{1,0:T(8,128)}, f32[512,256]{1,0:T(8,128)}, u32[]{:S(2)}, u32[]{:S(2)}) collective-permute-start(f32[512,256]{1,0:T(8,128)} %collective-permute-done.27.refs_11_), channel_id=1, source_target_pairs={{0,16},{8,24},{16,0},{24,8},{1,17},{9,25},{17,1},{25,9},{2,18},{10... | collective-permute-start | bytes 1572872 | tf_op jit(solution)/shard_map/ppermute | solution.py:17
  186.6 42.0 %collective-permute-start.22 = (f32[2,512,256]{2,1,0:T(8,128)S(1)}, f32[2,512,256]{2,1,0:T(8,128)S(1)}, u32[]{:S(2)}, u32[]{:S(2)}) collective-permute-start(f32[2,512,256]{2,1,0:T(8,128)S(1)} %collective-permute-done.21.refs_9_), channel_id=1, source_target_pairs={{0,8},{8,0},{16,24},{24,16},{1,9},{9,1},{17,25},{25,17},{2,10},{10... | collective-permute-start | bytes 3145736 | tf_op jit(solution)/shard_map/ppermute | solution.py:17
  187.2 29.6 %collective-permute-start.40 = (f32[512,256]{1,0:T(8,128)}, f32[512,256]{1,0:T(8,128)S(1)}, u32[]{:S(2)}, u32[]{:S(2)}) collective-permute-start(f32[512,256]{1,0:T(8,128)} %copy-done.2), channel_id=1, source_target_pairs={{0,8},{8,0},{16,24},{24,16},{1,9},{9,1},{17,25},{25,17},{2,10},{10... | collective-permute-start | bytes 1572872 | tf_op jit(solution)/shard_map/ppermute | solution.py:17
  187.2 30.2 %collective-permute-start.32 = (f32[512,256]{1,0:T(8,128)}, f32[512,256]{1,0:T(8,128)S(1)}, u32[]{:S(2)}, u32[]{:S(2)}) collective-permute-start(f32[512,256]{1,0:T(8,128)} %collective-permute-done.31.refs_10_), channel_id=1, source_target_pairs={{0,8},{8,0},{16,24},{24,16},{1,9},{9,1},{17,25},{25,17},{2,10},{10... | collective-permute-start | bytes 1572872 | tf_op jit(solution)/shard_map/ppermute | solution.py:17
  187.7 31.4 %collective-permute-start.34 = (f32[512,256]{1,0:T(8,128)}, f32[512,256]{1,0:T(8,128)S(1)}, u32[]{:S(2)}, u32[]{:S(2)}) collective-permute-start(f32[512,256]{1,0:T(8,128)} %collective-permute-done.33.refs_11_), channel_id=1, source_target_pairs={{0,8},{8,0},{16,24},{24,16},{1,9},{9,1},{17,25},{25,17},{2,10},{10... | collective-permute-start | bytes 1572872 | tf_op jit(solution)/shard_map/ppermute | solution.py:17
  217.6 24.8 %collective-permute-start.29 = (f32[512,256]{1,0:T(8,128)}, f32[512,256]{1,0:T(8,128)S(1)}, u32[]{:S(2)}, u32[]{:S(2)}) collective-permute-start(f32[512,256]{1,0:T(8,128)} %collective-permute-done.28.refs_11_), channel_id=1, source_target_pairs={{0,16},{8,24},{16,0},{24,8},{1,17},{9,25},{17,1},{25,9},{2,18},{10... | collective-permute-start | bytes 1572872 | tf_op jit(solution)/shard_map/ppermute | solution.py:17
  219.1 23.3 %collective-permute-start.45 = (f32[512,256]{1,0:T(8,128)S(1)}, f32[512,256]{1,0:T(8,128)S(1)}, u32[]{:S(2)}, u32[]{:S(2)}) collective-permute-start(f32[512,256]{1,0:T(8,128)S(1)} %shard_map.111), channel_id=1, source_target_pairs={{0,2},{1,3},{2,0},{3,1},{4,6},{5,7},{6,4},{7,5},{8,10},{9,11},{10,... | collective-permute-start | bytes 1572872 | tf_op jit(solution)/shard_map/ppermute | solution.py:17
  235.1 27.4 %collective-permute-start.26 = (f32[512,256]{1,0:T(8,128)S(1)}, f32[512,256]{1,0:T(8,128)S(1)}, u32[]{:S(2)}, u32[]{:S(2)}) collective-permute-start(f32[512,256]{1,0:T(8,128)S(1)} %collective-permute-done.25.refs_10_), channel_id=1, source_target_pairs={{0,8},{8,0},{16,24},{24,16},{1,9},{9,1},{17,25},{25,17},{2,10},{10... | collective-permute-start | bytes 1572872 | tf_op jit(solution)/shard_map/ppermute | solution.py:17
  242.4 24.3 %collective-permute-start.35 = (f32[512,256]{1,0:T(8,128)S(1)}, f32[512,256]{1,0:T(8,128)S(1)}, u32[]{:S(2)}, u32[]{:S(2)}) collective-permute-start(f32[512,256]{1,0:T(8,128)S(1)} %shard_map.108), channel_id=1, source_target_pairs={{0,2},{1,3},{2,0},{3,1},{4,6},{5,7},{6,4},{7,5},{8,10},{9,11},{10,... | collective-permute-start | bytes 1572872 | tf_op jit(solution)/shard_map/ppermute | solution.py:17
  (69 other events, 935.5 us)

commit v2 on v0

v2 whole, which is shorter than its diff:
```python
import functools

import jax
import jax.numpy as jnp
from jax import lax
from jax.experimental import pallas as pl
from jax.experimental.pallas import tpu as pltpu
from jax.sharding import PartitionSpec as P

QUARTERS = 4
F32, BF16 = jnp.float32, jnp.bfloat16
ROWS = (((1,), (0,)), ((), ()))
BOTH = (((1,), (1,)), ((), ()))
VMEM_BYTES = 40 * 2**20
MORE_VMEM_BYTES = 60 * 2**20


def swap(array, axis, size, k):
    return lax.ppermute(array, axis, [(i, i ^ k) for i in range(size)])


def dot(a, b, dims=ROWS):
    return lax.dot_general(a, b, dims, preferred_element_type=F32)


def two_terms(x):
    high = x.astype(BF16)
    return high, (x - high.astype(F32)).astype(BF16)


def three_terms(x):
    high = x.astype(BF16)
    rest = x - high.astype(F32)
    middle = rest.astype(BF16)
    return high, middle, (rest - middle.astype(F32)).astype(BF16)


def one_hot(index, size):
    return (index == lax.broadcasted_iota(jnp.int32, (index.shape[0], size), 1)).astype(F32)


def row_sums(x):
    ones = jnp.ones((8, x.shape[1]), BF16)
    return sum(dot(ones, term, BOTH) for term in three_terms(x))


def nothing():
    return pl.CostEstimate(flops=0, bytes_accessed=0, transcendentals=0)


def interval_kernel(spot_ref, boxes_ref, weight_ref, bias_ref, masks_ref, out_ref, center_sum, radius_sum):
    i = pl.program_id(0)
    images = boxes_ref.shape[1]
    weight = weight_ref[...]
    high, low = two_terms(weight)
    low_abs = jnp.where(weight < 0, -low.astype(F32), low.astype(F32)).astype(BF16)
    c = jnp.concatenate(two_terms(boxes_ref[0]), axis=0)
    r = jnp.concatenate(two_terms(boxes_ref[1]), axis=0)

    def both(x, y, box):
        main, rest = dot(x, box, BOTH), dot(y, box, BOTH)
        return main[:, :images] + (main[:, images:] + rest[:, :images])

    pre_center = both(high, low, c)
    pre_radius = both(jnp.abs(high), low_abs, r)

    @pl.when(i == 0)
    def _():
        center_sum[...] = pre_center
        radius_sum[...] = pre_radius

    @pl.when(i > 0)
    def _():
        center_sum[...] += pre_center
        radius_sum[...] += pre_radius

    @pl.when(i == pl.num_programs(0) - 1)
    def _():
        center, radius = center_sum[...].T + bias_ref[...], radius_sum[...].T
        upper, lower = center + radius, center - radius
        slope = jnp.clip(upper / (upper - lower), 0.0, 1.0)
        masks = masks_ref[...]
        out_ref[0] = jnp.where(masks == 1, 1.0, jnp.where(masks == 2, slope, 0.0))
        out_ref[1] = jnp.where(masks == 2, slope * lower, 0.0)


def interval(boxes, weight, bias, masks, spot):
    sites, _, images, cols = boxes.shape
    rows = weight.shape[0]
    return pl.pallas_call(
        interval_kernel,
        out_shape=jax.ShapeDtypeStruct((2, images, rows), F32),
        grid_spec=pltpu.PrefetchScalarGridSpec(
            num_scalar_prefetch=1,
            grid=(sites,),
            in_specs=[
                pl.BlockSpec((None, 2, images, cols), lambda i, spot: (spot[i], 0, 0, 0)),
                pl.BlockSpec((rows, cols), lambda i, spot: (0, i)),
                pl.BlockSpec((1, rows), lambda i, spot: (0, 0)),
                pl.BlockSpec((images, rows), lambda i, spot: (spot[sites], 0)),
            ],
            out_specs=pl.BlockSpec((2, images, rows), lambda i, spot: (0, 0, 0)),
            scratch_shapes=[pltpu.VMEM((rows, images), F32)] * 2,
        ),
        compiler_params=pltpu.CompilerParams(vmem_limit_bytes=VMEM_BYTES),
        cost_estimate=nothing(),
    )(spot, boxes, weight, bias, masks)


def scale_kernel(places, at_ref, slopes_ref, *refs):
    ow_refs, rest = refs[: len(places)], refs[len(places) :]
    at = at_ref[...]
    first = 0 if len(rest) == 1 else 3
    size = sum(shape[-2] for shape, _ in places)
    pick = (one_hot(at[:, first : first + 1], size) - one_hot(at[:, first + 1 : first + 2], size)).astype(BF16)
    coeff, low = None, 0
    for (shape, place), ref in zip(places, ow_refs):
        here = pick[:, low : low + shape[-2]]
        low += shape[-2]
        high_ow, low_ow = two_terms(ref[...] if place is None else ref[place])
        got = dot(here, high_ow) + dot(here, low_ow)
        coeff = got if coeff is None else coeff + got
    image = one_hot(at[:, 2:3], slopes_ref.shape[0]).astype(BF16)
    scaled = coeff * sum(dot(image, term) for term in three_terms(slopes_ref[...]))
    if first:
        offsets_ref, bias_ref, out_ref, relax_ref = rest
        offsets = sum(dot(image, term) for term in three_terms(offsets_ref[...]))
        relax_ref[...] = row_sums(scaled * bias_ref[...] - jnp.minimum(coeff, 0.0) * offsets)
    else:
        out_ref = rest[0]
    rows = scaled.shape[1]
    out_ref[:, :rows], out_ref[:, rows:] = two_terms(scaled)


def scale(at, ow_parts, slopes, *relax):
    specs, rows = at.shape[0], slopes.shape[1]
    outs = [jax.ShapeDtypeStruct((specs, 2 * rows), BF16)]
    if relax:
        outs = outs + [jax.ShapeDtypeStruct((8, specs), F32)]
    return pl.pallas_call(
        functools.partial(scale_kernel, [(array.shape, place) for array, place in ow_parts]),
        out_shape=outs,
        compiler_params=pltpu.CompilerParams(vmem_limit_bytes=VMEM_BYTES),
        cost_estimate=nothing(),
    )(at, slopes, *[array for array, _ in ow_parts], *relax)


def product_kernel(places, pieces, sums, *refs):
    group = len(places) // pieces
    col_ref, scaled_refs, weight_ref = refs[0], refs[1 : group + 2], refs[group + 2]
    w_refs, refs = refs[group + 3 : group + 3 + len(places)], refs[group + 3 + len(places) :]
    scaled_here, w_here, sems = refs[-3:]
    rows, piece = w_here.shape[1], w_here.shape[2] // pieces
    spans = [pl.ds(p * piece, piece) for p in range(pieces)]

    def columns(i):
        return pl.ds(pl.multiple_of(col_ref[i] * piece, piece), piece)

    sources = [weight_ref.at[:, columns(p)] for p in range(pieces)]
    sources += [ref if where is None else ref.at[where] for ref, where in zip(w_refs, places)]
    copies = []

    def fetch(source, target):
        copies.append(pltpu.make_async_copy(source, target, sems.at[len(copies)]))
        copies[-1].start()

    for j in range(group + 1):
        fetch(scaled_refs[j], scaled_here.at[j])
        for p in range(pieces):
            fetch(sources[j * pieces + p], w_here.at[j, :, spans[p]])
    operands = len(copies)
    if sums is not None:
        sum_refs, (near_ref, at_ref, margin_in) = refs[:sums], refs[sums : sums + 3]
        out_ref, margin_ref, block, near_here, sums_here = refs[-8:-3]
        for p in range(pieces):
            fetch(near_ref.at[:, :, columns(pieces + p)], near_here.at[:, :, spans[p]])
        for i, ref in enumerate(sum_refs):
            fetch(ref, sums_here.at[i])
    total = None
    for j in range(group + 1):
        for copy in copies[j * (pieces + 1) : (j + 1) * (pieces + 1)]:
            copy.wait()
        high, low = two_terms(w_here[j])
        got = dot(scaled_here[j], jnp.concatenate([high, high], axis=0)) + dot(scaled_here[j, :, :rows], low)
        total = got if total is None else total + got
    if sums is None:
        refs[0][...] = total
        return
    for copy in copies[operands:]:
        copy.wait()
    for i in range(sums):
        total = total + sums_here[i]
    block[...] = total
    puts = []
    for p in range(pieces):
        puts.append(pltpu.make_async_copy(block.at[:, spans[p]], out_ref.at[:, columns(pieces + p)], sems.at[p]))
        puts[-1].start()
    image = one_hot(at_ref[...][:, 5:6], near_here.shape[1]).astype(BF16)
    center = sum(dot(image, term) for term in three_terms(near_here[0]))
    radius = sum(dot(image, term) for term in three_terms(near_here[1]))
    margin_ref[...] = margin_in[...] + row_sums(total * center - jnp.abs(total) * radius)
    for put in puts:
        put.wait()


def product(scaled, weight, col, w_parts, final=None):
    specs, rows = scaled[0].shape[0], scaled[0].shape[1] // 2
    piece = w_parts[0][0].shape[-1]
    pieces = len(w_parts) // (len(scaled) - 1)
    whole = pl.BlockSpec(memory_space=pltpu.VMEM)
    there = pl.BlockSpec(memory_space=pltpu.HBM)
    args = [col, *scaled, weight, *[array for array, _ in w_parts]]
    in_specs = [pl.BlockSpec(memory_space=pltpu.SMEM)] + [there] * (len(args) - 1)
    scratch, n_sems = [], (1 + pieces) * len(scaled)
    aliases, sums = {}, None
    if final is None:
        out_shape, out_specs = jax.ShapeDtypeStruct((specs, pieces * piece), F32), whole
    else:
        sum_parts, at, near, margin, out = final
        sums = len(sum_parts)
        in_specs += [there] * (sums + 1) + [whole] * 2
        args += [*sum_parts, near, at, margin]
        if out is not None:
            aliases = {len(args): 0}
            in_specs.append(there)
            args.append(out)
        out_shape = [jax.ShapeDtypeStruct((specs, QUARTERS * piece), F32), jax.ShapeDtypeStruct((8, specs), F32)]
        out_specs = [there, whole]
        scratch = [
            pltpu.VMEM((specs, pieces * piece), F32),
            pltpu.VMEM((2, near.shape[1], pieces * piece), F32),
            pltpu.VMEM((sums, specs, pieces * piece), F32),
        ]
        n_sems += pieces + sums
    scratch += [
        pltpu.VMEM((len(scaled), specs, 2 * rows), BF16),
        pltpu.VMEM((len(scaled), rows, pieces * piece), F32),
        pltpu.SemaphoreType.DMA((n_sems,)),
    ]
    return pl.pallas_call(
        functools.partial(product_kernel, [place for _, place in w_parts], pieces, sums),
        out_shape=out_shape,
        in_specs=in_specs,
        out_specs=out_specs,
        scratch_shapes=scratch,
        input_output_aliases=aliases,
        compiler_params=pltpu.CompilerParams(vmem_limit_bytes=MORE_VMEM_BYTES),
        cost_estimate=nothing(),
    )(*args)


class Rounds:
    def __init__(self):
        self.got, self.fresh = {}, []

    def keep(self, name, value):
        self.got[name] = value
        self.fresh.append(name)

    def edge(self, *sends):
        held = [self.got[name] for name in self.fresh]
        done = lax.optimization_barrier((*[value for _, value, _ in sends], *held))
        self.got.update(zip(self.fresh, done[len(sends) :]))
        self.fresh = []
        for (name, _, move), value in zip(sends, done):
            self.keep(name, move(value))

    def send(self, name, value, move):
        self.keep(name, move(value))


def local(members, sites, center, radius, weight, bias, out_weight, masks, image_labels, runner_up, spec_image):
    g, n = lax.axis_index("spec"), lax.axis_index("neuron")
    q = g % QUARTERS
    rows, cols = weight.shape[0], center.shape[1]
    images, classes = center.shape[0], out_weight.shape[0]
    piece = cols // QUARTERS
    cut = sites // 2
    group = (1, cut, cut + 1)
    targets = [2 * m for m in range(1, sites // 4)] + [0]

    def to_site(k):
        return functools.partial(swap, axis="neuron", size=sites, k=k)

    def to_member(k):
        return functools.partial(swap, axis="spec", size=members, k=k)

    work = Rounds()
    got, keep, edge, send = work.got, work.keep, work.edge, work.send
    where = {}

    share = -(-classes // QUARTERS // 8) * 8

    def start_of(part):
        return jnp.minimum(part * share, classes - share)

    def columns(t, j):
        block = lax.dynamic_slice(weight, (0, (n ^ j ^ t) * cols + q * piece), (rows, piece))
        where[t, j, 0] = (t, j, 0), None
        return (t, j, 0), block, to_site(j)

    def part(name):
        key, place = where[name]
        return got[key], place

    def value(name):
        array, place = part(name)
        return array if place is None else array[place]

    def share_out(k, *names):
        pieces = [value(name) for name in names]
        names = [(what, j, r ^ k) for what, j, r in names]
        if len(names) == 1:
            where[names[0]] = names[0], None
            return names[0], pieces[0], to_member(k)
        for i, name in enumerate(names):
            where[name] = tuple(names), i
        return tuple(names), jnp.stack(pieces), to_member(k)

    ow = lax.dynamic_slice(out_weight, (start_of(q), 0), (share, rows))
    for j in group:
        where["ow", j, 0] = ("ow", j, 0), None
    send(("ow", 1, 0), ow, to_site(1))
    near = jnp.stack([center, radius])
    boxes = near[None]
    order = [0]
    k = cut
    while k:
        if k == 1:
            keep("boxes", boxes)
            edge((("ow", cut, 0), ow, to_site(cut)))
            boxes = got["boxes"]
        boxes = jnp.concatenate([boxes, to_site(k)(boxes)])
        order = order + [o ^ k for o in order]
        k //= 2
    keep("boxes", boxes)
    t = targets[0]
    send(*columns(t, 1))
    k = 1
    while k < members:
        near = jnp.concatenate([near, to_member(k)(near)], axis=1)
        k *= 2
    keep("near", near)
    spot = jnp.zeros((sites,), jnp.int32)
    for s, o in enumerate(order):
        spot = jnp.where((n ^ jnp.arange(sites)) == o, s, spot)

    edge(columns(t, cut))
    send(("ow", cut + 1, 0), got["ow", cut, 0], to_site(1))
    send(*share_out(2, ("ow", 1, 0)))
    send(*share_out(2, ("ow", cut, 0)))
    if len(targets) > 1:
        send(*columns(targets[1], 1))
    both = interval(got["boxes"], weight, bias[None], masks, jnp.append(spot, g))
    keep("both", lax.all_gather(both, "spec", axis=1, tiled=True))
    labels = jnp.sum(jnp.where(spec_image[:, None] == jnp.arange(image_labels.shape[0]), image_labels, 0), axis=1)

    def place(label):
        part = label // share
        return (part ^ q) * share + label - start_of(part)

    near_image = ((spec_image // images) ^ g) * images + spec_image % images
    keep("at", jnp.stack([place(labels), place(runner_up), spec_image, labels, runner_up, near_image], axis=1))

    edge(columns(t, cut + 1))
    send(*share_out(2, ("ow", cut + 1, 0)))
    send(*share_out(2, (t, 1, 0)))
    send(*share_out(1, *[("ow", j, r) for j in (1, cut) for r in (0, 2)]))
    slopes, offsets = got["both"][0], got["both"][1]
    keep("slopes", jnp.stack([slopes, to_site(cut)(slopes)]))
    *scaled, margin = scale(got["at"], [(out_weight, None)], slopes, offsets, bias[None])
    keep("scaled0", scaled[0])
    out, sums = None, {}

    def some_product(t, *members_at):
        parts = [part((t, j, r)) for j in group for r in members_at]
        col = jnp.stack([(n ^ t) * QUARTERS + (q ^ r) for r in members_at] + [q ^ r for r in members_at])
        scaled = [got["scaled0"]] + [got["scaled", j] for j in group]
        if t:
            return product(scaled, weight, col, parts)
        had = [got["sum", f, members_at] for f in targets[:-1]]
        return product(scaled, weight, col, parts, (had, got["at"], got["near"], margin, out))

    for i, t in enumerate(targets):
        after = targets[i + 1 :][:1]
        late = [cut, cut + 1] if i == 0 else [cut + 1]
        early = [j for j in group if j not in late]
        edge(*([columns(after[0], cut)] if after else []))
        if i:
            send(("sum", targets[i - 1], (2, 3)), got["product"], to_site(targets[i - 1]))
        if i == 0:
            slopes = jnp.concatenate([got["slopes"], to_site(1)(got["slopes"])])
        elif after:
            send(*columns(after[0], 1))
        send(*share_out(2, *[(t, j, 0) for j in late]))
        send(*share_out(1, *[(t, j, 0) for j in group], *[(t, j, 2) for j in early]))
        if i == 0:
            send(*share_out(1, ("ow", cut + 1, 0), ("ow", cut + 1, 2)))
            for j, slot in ((cut, 1), (1, 2), (cut + 1, 3)):
                parts = [part(("ow", j, r)) for r in range(QUARTERS)]
                (got["scaled", j],) = scale(got["at"], parts, slopes[slot])
        if t:
            keep("product", some_product(t, 0, 1))
        else:
            out, margin = some_product(t, 0, 1)
            keep("out", out)
            keep("margin", margin)
        edge(*([columns(after[0], cut + 1)] if after else []))
        if after:
            send(*share_out(2, (after[0], 1, 0), (after[0], cut, 0)))
        send(*share_out(1, *[(t, j, 2) for j in late]))
        if t:
            send(("sum", t, (0, 1)), got["product"], to_site(t))
            keep("product", some_product(t, 2, 3))
        else:
            out, margin = got["out"], got["margin"]
            out, margin = some_product(t, 2, 3)
    margin = margin + (to_site(1)(margin) + to_site(2)(margin) + to_site(3)(margin))
    k = 4
    while k < sites:
        margin = margin + to_site(k)(margin)
        k *= 2
    return out, margin[0]


def solution(mesh):
    members, sites = mesh.shape["spec"], mesh.shape["neuron"]
    return jax.shard_map(
        functools.partial(local, members, sites),
        mesh=mesh,
        in_specs=(
            P("spec", "neuron"),
            P("spec", "neuron"),
            P("neuron", None),
            P("neuron"),
            P(None, "neuron"),
            P(None, "neuron"),
            P(),
            P("spec"),
            P("spec"),
        ),
        out_specs=(P("spec", "neuron"), P("spec")),
        check_vma=False,
    )
```

time: 467 us -> 232 us (0.50)
  waiting for transfers between devices: 303 us -> 95.2 us
  matrix products: 68.8 us -> 0 us
  Pallas kernels: 0 us -> 53.6 us
  starting transfers between devices: 0.12 us -> 37.7 us
  blocking collectives: 34.7 us -> 5.61 us
  between operations: 13.9 us -> 1.07 us
  other arithmetic: 26.7 us -> 19.4 us
    reduce_scatter x1 -> x0, waiting for transfers between devices: 275 us -> none  [local(): lax.psum_scatter(lax.dot_general(weight, scaled, (((0,), (1,)), ((), ()))...]
    ppermute x0 -> x35, waiting for transfers between devices: none -> 95.2 us  [swap(): return lax.ppermute(array, axis, [(i, i ^ k) for i in range(size)])]
    dot_general x3 -> x0, matrix products: 68.8 us -> none  [the longest x1 32 us: local(): lax.dot_general(weight, scaled, (((0,), (1,)), ((), ())), precision=highest)]
    pallas_call x0 -> x9, Pallas kernels: none -> 53.6 us  [the longest x4 31.1 us: product(): pl.pallas_call(functools.partial(product_kernel, [place for _, place in w...]
    ppermute x0 -> x35, starting transfers between devices: none -> 37.7 us  [swap(): return lax.ppermute(array, axis, [(i, i ^ k) for i in range(size)])]
    all_gather x2 -> x0, waiting for transfers between devices: 27.9 us -> none  [the longest x1 22.7 us: local(): lax.all_gather(center_all, 'neuron', axis=1, tiled=True)]
    and x3 -> x0, other arithmetic: 20.7 us -> none  [the longest x1 20.7 us: local(): jnp.take(out_weight, true_class, axis=0)]
    psum x1 -> x0, blocking collectives: 20.1 us -> none  [local(): margin_bounds = lax.psum(input_part + relax_part, 'neuron')]
  transfers between devices with their start and end apart: 3 -> 35, of which waited for: 3 -> 18; matrix products, arithmetic and copies ran while one was open for 11% -> 7% of each run, Pallas kernels for 0% -> 20%
where the time goes in v2:
time: 232 us; the launch traced here: 231 us
  waiting for transfers between devices  95.2 us (41%)
  Pallas kernels  53.6 us (23%)
  starting transfers between devices  37.7 us (16%)
  other arithmetic  19.4 us (8%)
  local copies, waits for them, and re-layouts  18.2 us (8%)
  blocking collectives  5.61 us (2%)
    ppermute x35, waiting for transfers between devices, swap(): return lax.ppermute(array, axis, [(i, i ^ k) for i in range(size)])  95.2 us
    ppermute x35, starting transfers between devices, swap(): return lax.ppermute(array, axis, [(i, i ^ k) for i in range(size)])  37.7 us
    pallas_call x4, Pallas kernels, product(): pl.pallas_call(functools.partial(product_kernel, [place for _, place in w...  31.1 us
    pallas_call x1, Pallas kernels, interval(): pl.pallas_call(interval_kernel, out_shape=jax.ShapeDtypeStruct((2, images...  14.3 us
    another operation x6, other arithmetic, share_out(): return (tuple(names), jnp.stack(pieces), to_member(k))  12.9 us
    unnamed x70, local copies, waits for them, and re-layouts  11.6 us
    pallas_call x4, Pallas kernels, scale(): pl.pallas_call(functools.partial(scale_kernel, [(array.shape, place) for...  8.29 us
    all_gather x1, blocking collectives, local(): keep('both', lax.all_gather(both, 'spec', axis=1, tiled=True))  5.61 us
  transfers between devices with their start and end apart: 35, of which 18 were waited for; matrix products, arithmetic and copies ran while one was open for 7% of the time, Pallas kernels for 20%

profile of v2, /device:TPU:0, one launch (start us, length us, event | category | flops | bytes accessed | tf_op | source)
XLA Modules:
  0.0 230.9 jit_solution(11195422808192454731)
XLA Ops:
  1.8 3.0 %collective-permute-start = (f32[256,512]{1,0:T(8,128)S(1)}, f32[256,512]{1,0:T(8,128)S(1)}, u32[]{:S(2)}, u32[]{:S(2)}) collective-permute-start(f32[256,512]{1,0:T(8,128)S(1)} %constant_dynamic-slice_fusion.3), channel_id=1, source_target_pairs={{0,1},{1,0},{2,3},{3,2},{4,5},{5,4},{6,7},{7,6},{8,9},{9,8},{10,11... | collective-permute-start | bytes 1572872 | tf_op jit(solution)/shard_map/ppermute | solution.py:19
  5.6 2.7 %collective-permute-start.1 = (f32[1,2,8,1024]{3,2,1,0:T(8,128)S(1)}, f32[1,2,8,1024]{3,2,1,0:T(8,128)S(1)}, u32[]{:S(2)}, u32[]{:S(2)}) collective-permute-start(f32[1,2,8,1024]{3,2,1,0:T(8,128)S(1)} %get-tuple-element.100), channel_id=1, source_target_pairs={{0,4},{1,5},{2,6},{3,7},{4,0},{5,1},{6,2},{7,3},{8,12},{9,13},{10,... | collective-permute-start | bytes 196616 | tf_op jit(solution)/shard_map/ppermute | solution.py:19
  8.2 2.9 %collective-permute-done.1 = f32[1,2,8,1024]{3,2,1,0:T(8,128)S(1)} collective-permute-done((f32[1,2,8,1024]{3,2,1,0:T(8,128)S(1)}, f32[1,2,8,1024]{3,2,1,0:T(8,128)S(1)}, u32[]{:S(2)}, u32[]{:S(2)}) %collective-permute-start.1) | collective-permute-done | bytes 65568 | tf_op jit(solution)/shard_map/ppermute | solution.py:19
  12.5 3.4 %constant_dynamic-slice_fusion = (f32[512,256]{1,0:T(8,128)}, f32[512,256]{1,0:T(8,128)}, f32[512,256]{1,0:T(8,128)S(1)}, f32[512,256]{1,0:T(8,128)}, f32[512,256]{1,0:T(8,128)}, /*index=5*/f32[512,256]{1,0:T(8,128)}) fusion(f32[512,8192]{1,0:T(8,128)} %refs_5_.7, s32[]{:T(128)S(6)} %select_n.101, s32[]{:T(128)S(6)} %select_n.87, s32[]{:T(128)S(6)} %select_n.86, ...), kind=kLoop, calls=%fused_computation.52 | loop fusion | bytes 6291480 | tf_op jit(solution)/shard_map/dynamic_slice | solution.py:298
  23.5 3.3 %collective-permute-done.7 = f32[2,16,1024]{2,1,0:T(8,128)S(1)} collective-permute-done((f32[2,16,1024]{2,1,0:T(8,128)S(1)}, f32[2,16,1024]{2,1,0:T(8,128)S(1)}, u32[]{:S(2)}, u32[]{:S(2)}) %collective-permute-start.7) | collective-permute-done | bytes 131104 | tf_op jit(solution)/shard_map/ppermute | solution.py:19
  29.0 7.5 %collective-permute-done.4 = f32[4,2,8,1024]{3,2,1,0:T(8,128)S(1)} collective-permute-done((f32[4,2,8,1024]{3,2,1,0:T(8,128)S(1)}, f32[4,2,8,1024]{3,2,1,0:T(8,128)S(1)}, u32[]{:S(2)}, u32[]{:S(2)}) %collective-permute-start.4) | collective-permute-done | bytes 262176 | tf_op jit(solution)/shard_map/ppermute | solution.py:19
  36.5 6.7 %collective-permute-done.3.refs_0_ = f32[256,512]{1,0:T(8,128)S(1)} collective-permute-done((f32[256,512]{1,0:T(8,128)S(1)}, f32[256,512]{1,0:T(8,128)S(1)}, u32[]{:S(2)}, u32[]{:S(2)}) %collective-permute-start.3) | collective-permute-done | bytes 524320 | tf_op jit(solution)/shard_map/ppermute | solution.py:19
  47.0 14.3 %shard_map.104 = f32[2,8,512]{2,1,0:T(8,128)S(1)} custom-call(s32[9]{0:T(128)S(1)} %pad_add_fusion.spot_ref, f32[8,2,8,1024]{3,2,1,0:T(8,128)S(1)} %pad_maximum_fusion.6.boxes_ref, f32[512,8192]{1,0:T(8,128)} %refs_5_.7, f32[1,512]{1,0:T(1,128)S(1)} %bitcast.54, s32[32,512]{1,0:T(8,128)S(1)} %copy-done.18), custom_call_target="tpu_custom_call" | custom-call | tf_op jit(solution)/shard_map/pallas_call | solution.py:90
  61.3 5.6 %all_gather.3 = f32[2,32,512]{2,1,0:T(8,128)S(1)} all-gather(f32[2,8,512]{2,1,0:T(8,128)S(1)} %shard_map.104), channel_id=1, replica_groups=mesh['spec'=4,'neuron'=8] {'spec'}, dimensions={1}, use_global_device_ids=true | all-gather | bytes 163840 | tf_op jit(solution)/shard_map/all_gather | solution.py:355
  66.9 3.4 %collective-permute-done.8.refs_8_ = f32[512,256]{1,0:T(8,128)} collective-permute-done((f32[512,256]{1,0:T(8,128)}, f32[512,256]{1,0:T(8,128)}, u32[]{:S(2)}, u32[]{:S(2)}) %collective-permute-start.8) | collective-permute-done | bytes 524320 | tf_op jit(solution)/shard_map/ppermute | solution.py:19
  75.3 2.9 %collective-permute-start.17 = (f32[32,512]{1,0:T(8,128)S(1)}, f32[32,512]{1,0:T(8,128)}, u32[]{:S(2)}, u32[]{:S(2)}) collective-permute-start(f32[32,512]{1,0:T(8,128)S(1)} %get-tuple-element.97.slopes_ref), channel_id=1, source_target_pairs={{0,4},{1,5},{2,6},{3,7},{4,0},{5,1},{6,2},{7,3},{8,12},{9,13},{10,... | collective-permute-start | bytes 196616 | tf_op jit(solution)/shard_map/ppermute | solution.py:19
  80.7 2.9 %shard_map.105 = (bf16[512,1024]{1,0:T(8,128)(2,1)S(1)}, f32[8,512]{1,0:T(8,128)S(1)}) custom-call(s32[512,6]{1,0:T(8,128)S(1)} %copy.28.at_ref.refs_14_, f32[32,512]{1,0:T(8,128)S(1)} %get-tuple-element.97.slopes_ref, f32[1000,512]{1,0:T(8,128)S(1)} %copy-done.5, f32[32,512]{1,0:T(8,128)S(1)} %get-tuple-element.96.refs_1_, f32[1,512]{1,0:T(1,128)S(1)} %bitcast.55), custom_call_target="tpu_custom_call" | custom-call | tf_op jit(solution)/shard_map/pallas_call | solution.py:140
  83.6 18.8 %collective-permute-done.17 = f32[32,512]{1,0:T(8,128)} collective-permute-done((f32[32,512]{1,0:T(8,128)S(1)}, f32[32,512]{1,0:T(8,128)}, u32[]{:S(2)}, u32[]{:S(2)}) %collective-permute-start.17) | collective-permute-done | bytes 65568 | tf_op jit(solution)/shard_map/ppermute | solution.py:19
  103.3 3.2 %pad_maximum_fusion.2 = f32[4,512,256]{2,1,0:T(8,128)} fusion(f32[1,512,256]{2,1,0:T(8,128)} %bitcast.29, f32[1,512,256]{2,1,0:T(8,128)} %bitcast.27, f32[1,512,256]{2,1,0:T(8,128)} %bitcast.26, f32[1,512,256]{2,1,0:T(8,128)} %bitcast.28), kind=kLoop, calls=%fused_computation.2 | loop fusion | flops 1572864 | bytes 4194304 | tf_op jit(solution)/shard_map/stack | solution.py:318
  123.7 6.9 %shard_map.109 = f32[512,512]{1,0:T(8,128)} custom-call(s32[4]{0:T(128)} %add_add_fusion.2.refs_0_, bf16[512,1024]{1,0:T(8,128)(2,1)} %copy-done.3, bf16[512,1024]{1,0:T(8,128)(2,1)} %copy-done.1, bf16[512,1024]{1,0:T(8,128)(2,1)} %copy-done, bf16[512,1024]{1,0:T(8,128)(2,1)} %copy-done.2, f32[512,8192]{1,0:T(8,128)} %refs_5_.7, ...), custom_call_target="tpu_custom_call" | custom-call | tf_op jit(solution)/shard_map/pallas_call | solution.py:240
  130.7 5.6 %collective-permute-done.20.refs_8_ = f32[512,256]{1,0:T(8,128)S(1)} collective-permute-done((f32[512,256]{1,0:T(8,128)}, f32[512,256]{1,0:T(8,128)S(1)}, u32[]{:S(2)}, u32[]{:S(2)}) %collective-permute-start.20) | collective-permute-done | bytes 524320 | tf_op jit(solution)/shard_map/ppermute | solution.py:19
  139.7 3.4 %collective-permute-start.23 = (f32[512,256]{1,0:T(8,128)S(1)}, f32[512,256]{1,0:T(8,128)}, u32[]{:S(2)}, u32[]{:S(2)}) collective-permute-start(f32[512,256]{1,0:T(8,128)S(1)} %copy-done.28), channel_id=1, source_target_pairs={{0,5},{1,4},{2,7},{3,6},{4,1},{5,0},{6,3},{7,2},{8,13},{9,12},{10,... | collective-permute-start | bytes 1572872 | tf_op jit(solution)/shard_map/ppermute | solution.py:19
  144.7 7.1 %shard_map.110 = f32[512,512]{1,0:T(8,128)} custom-call(s32[4]{0:T(128)} %add_add_fusion.3.refs_0_, bf16[512,1024]{1,0:T(8,128)(2,1)} %copy-done.3, bf16[512,1024]{1,0:T(8,128)(2,1)} %copy-done.1, bf16[512,1024]{1,0:T(8,128)(2,1)} %copy-done, bf16[512,1024]{1,0:T(8,128)(2,1)} %copy-done.2, f32[512,8192]{1,0:T(8,128)} %refs_5_.7, ...), custom_call_target="tpu_custom_call" | custom-call | tf_op jit(solution)/shard_map/pallas_call | solution.py:240
  151.9 21.9 %collective-permute-done.23.refs_10_ = f32[512,256]{1,0:T(8,128)} collective-permute-done((f32[512,256]{1,0:T(8,128)S(1)}, f32[512,256]{1,0:T(8,128)}, u32[]{:S(2)}, u32[]{:S(2)}) %collective-permute-start.23) | collective-permute-done | bytes 524320 | tf_op jit(solution)/shard_map/ppermute | solution.py:19
  176.1 2.9 %pad_maximum_fusion = f32[5,512,256]{2,1,0:T(8,128)} fusion(f32[2,512,256]{2,1,0:T(8,128)S(1)} %collective-permute-done.24.refs_6_.refs_8_, f32[1,512,256]{2,1,0:T(8,128)} %bitcast.38, f32[1,512,256]{2,1,0:T(8,128)S(1)} %bitcast.57, f32[1,512,256]{2,1,0:T(8,128)} %bitcast.34), kind=kLoop, calls=%fused_computation | loop fusion | flops 1966080 | bytes 5242880 | tf_op jit(solution)/shard_map/stack | solution.py:318
  185.6 8.5 %shard_map.111 = (f32[512,1024]{1,0:T(8,128)}, f32[8,512]{1,0:T(8,128)}) custom-call(s32[4]{0:T(128)} %add_add_fusion.4.refs_0_, bf16[512,1024]{1,0:T(8,128)(2,1)} %copy-done.3, bf16[512,1024]{1,0:T(8,128)(2,1)} %copy-done.1, bf16[512,1024]{1,0:T(8,128)(2,1)} %copy-done, bf16[512,1024]{1,0:T(8,128)(2,1)} %copy-done.2, f32[512,8192]{1,0:T(8,128)} %refs_5_.7, ...), custom_call_target="tpu_custom_call" | custom-call | tf_op jit(solution)/shard_map/pallas_call | solution.py:240
  196.0 9.9 %collective-permute-done.27.refs_12_ = f32[512,512]{1,0:T(8,128)} collective-permute-done((f32[512,512]{1,0:T(8,128)}, f32[512,512]{1,0:T(8,128)}, u32[]{:S(2)}, u32[]{:S(2)}) %collective-permute-start.27) | collective-permute-done | bytes 1048608 | tf_op jit(solution)/shard_map/ppermute | solution.py:19
  208.6 8.5 %shard_map.112 = (f32[512,1024]{1,0:T(8,128)}, f32[8,512]{1,0:T(8,128)}) custom-call(s32[4]{0:T(128)} %add_add_fusion.1.refs_0_, bf16[512,1024]{1,0:T(8,128)(2,1)} %copy-done.3, bf16[512,1024]{1,0:T(8,128)(2,1)} %copy-done.1, bf16[512,1024]{1,0:T(8,128)(2,1)} %copy-done, bf16[512,1024]{1,0:T(8,128)(2,1)} %copy-done.2, ...), custom_call_target="tpu_custom_call", output_to_operand_aliasing={{0}: (16, {})} | custom-call | tf_op jit(solution)/shard_map/pallas_call | solution.py:240
  225.8 4.5 %collective-permute-done.34 = f32[8,512]{1,0:T(8,128)S(1)} collective-permute-done((f32[8,512]{1,0:T(8,128)S(1)}, f32[8,512]{1,0:T(8,128)S(1)}, u32[]{:S(2)}, u32[]{:S(2)}) %collective-permute-start.34) | collective-permute-done | bytes 16416 | tf_op jit(solution)/shard_map/ppermute | solution.py:19
  (157 shorter events, 70.1 us)
Async XLA Ops:
  1.8 15.4 %collective-permute-start = (f32[256,512]{1,0:T(8,128)S(1)}, f32[256,512]{1,0:T(8,128)S(1)}, u32[]{:S(2)}, u32[]{:S(2)}) collective-permute-start(f32[256,512]{1,0:T(8,128)S(1)} %constant_dynamic-slice_fusion.3), channel_id=1, source_target_pairs={{0,1},{1,0},{2,3},{3,2},{4,5},{5,4},{6,7},{7,6},{8,9},{9,8},{10,11... | collective-permute-start | bytes 1572872 | tf_op jit(solution)/shard_map/ppermute | solution.py:19
  15.9 20.6 %collective-permute-start.5 = (f32[512,256]{1,0:T(8,128)S(1)}, f32[512,256]{1,0:T(8,128)}, u32[]{:S(2)}, u32[]{:S(2)}) collective-permute-start(f32[512,256]{1,0:T(8,128)S(1)} %get-tuple-element.90), channel_id=1, source_target_pairs={{0,1},{1,0},{2,3},{3,2},{4,5},{5,4},{6,7},{7,6},{8,9},{9,8},{10,11... | collective-permute-start | bytes 1572872 | tf_op jit(solution)/shard_map/ppermute | solution.py:19
  17.1 26.1 %collective-permute-start.3 = (f32[256,512]{1,0:T(8,128)S(1)}, f32[256,512]{1,0:T(8,128)S(1)}, u32[]{:S(2)}, u32[]{:S(2)}) collective-permute-start(f32[256,512]{1,0:T(8,128)S(1)} %constant_dynamic-slice_fusion.3), channel_id=1, source_target_pairs={{0,4},{1,5},{2,6},{3,7},{4,0},{5,1},{6,2},{7,3},{8,12},{9,13},{10,... | collective-permute-start | bytes 1572872 | tf_op jit(solution)/shard_map/ppermute | solution.py:19
  19.8 16.7 %collective-permute-start.4 = (f32[4,2,8,1024]{3,2,1,0:T(8,128)S(1)}, f32[4,2,8,1024]{3,2,1,0:T(8,128)S(1)}, u32[]{:S(2)}, u32[]{:S(2)}) collective-permute-start(f32[4,2,8,1024]{3,2,1,0:T(8,128)S(1)} %pad_maximum_fusion.7), channel_id=1, source_target_pairs={{0,1},{1,0},{2,3},{3,2},{4,5},{5,4},{6,7},{7,6},{8,9},{9,8},{10,11... | collective-permute-start | bytes 786440 | tf_op jit(solution)/shard_map/ppermute | solution.py:19
  23.3 43.7 %collective-permute-start.12 = (f32[512,256]{1,0:T(8,128)}, f32[512,256]{1,0:T(8,128)}, u32[]{:S(2)}, u32[]{:S(2)}) collective-permute-start(f32[512,256]{1,0:T(8,128)} %get-tuple-element.89), channel_id=1, source_target_pairs={{0,1},{1,0},{2,3},{3,2},{4,5},{5,4},{6,7},{7,6},{8,9},{9,8},{10,11... | collective-permute-start | bytes 1572872 | tf_op jit(solution)/shard_map/ppermute | solution.py:19
  27.5 39.4 %collective-permute-start.10 = (f32[256,512]{1,0:T(8,128)S(1)}, f32[256,512]{1,0:T(8,128)S(1)}, u32[]{:S(2)}, u32[]{:S(2)}) collective-permute-start(f32[256,512]{1,0:T(8,128)S(1)} %collective-permute-done.refs_0_), channel_id=1, source_target_pairs={{0,16},{8,24},{16,0},{24,8},{1,17},{9,25},{17,1},{25,9},{2,18},{10... | collective-permute-start | bytes 1572872 | tf_op jit(solution)/shard_map/ppermute | solution.py:19
  43.2 23.7 %collective-permute-start.11 = (f32[256,512]{1,0:T(8,128)S(1)}, f32[256,512]{1,0:T(8,128)S(1)}, u32[]{:S(2)}, u32[]{:S(2)}) collective-permute-start(f32[256,512]{1,0:T(8,128)S(1)} %collective-permute-done.3.refs_0_), channel_id=1, source_target_pairs={{0,16},{8,24},{16,0},{24,8},{1,17},{9,25},{17,1},{25,9},{2,18},{10... | collective-permute-start | bytes 1572872 | tf_op jit(solution)/shard_map/ppermute | solution.py:19
  44.7 25.6 %collective-permute-start.9 = (f32[256,512]{1,0:T(8,128)S(1)}, f32[256,512]{1,0:T(8,128)S(1)}, u32[]{:S(2)}, u32[]{:S(2)}) collective-permute-start(f32[256,512]{1,0:T(8,128)S(1)} %collective-permute-done.3.refs_0_), channel_id=1, source_target_pairs={{0,1},{1,0},{2,3},{3,2},{4,5},{5,4},{6,7},{7,6},{8,9},{9,8},{10,11... | collective-permute-start | bytes 1572872 | tf_op jit(solution)/shard_map/ppermute | solution.py:19
  46.2 24.1 %collective-permute-start.8 = (f32[512,256]{1,0:T(8,128)}, f32[512,256]{1,0:T(8,128)}, u32[]{:S(2)}, u32[]{:S(2)}) collective-permute-start(f32[512,256]{1,0:T(8,128)} %get-tuple-element.47), channel_id=1, source_target_pairs={{0,4},{1,5},{2,6},{3,7},{4,0},{5,1},{6,2},{7,3},{8,12},{9,13},{10,... | collective-permute-start | bytes 1572872 | tf_op jit(solution)/shard_map/ppermute | solution.py:19
  72.6 30.7 %collective-permute-start.16 = (f32[4,256,512]{2,1,0:T(8,128)}, f32[4,256,512]{2,1,0:T(8,128)S(1)}, u32[]{:S(2)}, u32[]{:S(2)}) collective-permute-start(f32[4,256,512]{2,1,0:T(8,128)} %pad_maximum_fusion.1), channel_id=1, source_target_pairs={{0,8},{8,0},{16,24},{24,16},{1,9},{9,1},{17,25},{25,17},{2,10},{10... | collective-permute-start | bytes 6291464 | tf_op jit(solution)/shard_map/ppermute | solution.py:19
  72.6 30.6 %collective-permute-start.15 = (f32[512,256]{1,0:T(8,128)}, f32[512,256]{1,0:T(8,128)}, u32[]{:S(2)}, u32[]{:S(2)}) collective-permute-start(f32[512,256]{1,0:T(8,128)} %collective-permute-done.5.refs_6_), channel_id=1, source_target_pairs={{0,16},{8,24},{16,0},{24,8},{1,17},{9,25},{17,1},{25,9},{2,18},{10... | collective-permute-start | bytes 1572872 | tf_op jit(solution)/shard_map/ppermute | solution.py:19
  73.2 30.1 %collective-permute-start.13 = (f32[512,256]{1,0:T(8,128)}, f32[512,256]{1,0:T(8,128)}, u32[]{:S(2)}, u32[]{:S(2)}) collective-permute-start(f32[512,256]{1,0:T(8,128)} %get-tuple-element.51), channel_id=1, source_target_pairs={{0,5},{1,4},{2,7},{3,6},{4,1},{5,0},{6,3},{7,2},{8,13},{9,12},{10,... | collective-permute-start | bytes 1572872 | tf_op jit(solution)/shard_map/ppermute | solution.py:19
  73.2 30.1 %collective-permute-start.14 = (f32[256,512]{1,0:T(8,128)S(1)}, f32[256,512]{1,0:T(8,128)S(1)}, u32[]{:S(2)}, u32[]{:S(2)}) collective-permute-start(f32[256,512]{1,0:T(8,128)S(1)} %collective-permute-done.9.refs_0_), channel_id=1, source_target_pairs={{0,16},{8,24},{16,0},{24,8},{1,17},{9,25},{17,1},{25,9},{2,18},{10... | collective-permute-start | bytes 1572872 | tf_op jit(solution)/shard_map/ppermute | solution.py:19
  75.3 27.1 %collective-permute-start.17 = (f32[32,512]{1,0:T(8,128)S(1)}, f32[32,512]{1,0:T(8,128)}, u32[]{:S(2)}, u32[]{:S(2)}) collective-permute-start(f32[32,512]{1,0:T(8,128)S(1)} %get-tuple-element.97.slopes_ref), channel_id=1, source_target_pairs={{0,4},{1,5},{2,6},{3,7},{4,0},{5,1},{6,2},{7,3},{8,12},{9,13},{10,... | collective-permute-start | bytes 196616 | tf_op jit(solution)/shard_map/ppermute | solution.py:19
  106.5 17.3 %collective-permute-start.22 = (f32[4,512,256]{2,1,0:T(8,128)}, f32[4,512,256]{2,1,0:T(8,128)}, u32[]{:S(2)}, u32[]{:S(2)}) collective-permute-start(f32[4,512,256]{2,1,0:T(8,128)} %pad_maximum_fusion.2), channel_id=1, source_target_pairs={{0,8},{8,0},{16,24},{24,16},{1,9},{9,1},{17,25},{25,17},{2,10},{10... | collective-permute-start | bytes 6291464 | tf_op jit(solution)/shard_map/ppermute | solution.py:19
  107.5 13.4 %collective-permute-start.19 = (f32[2,256,512]{2,1,0:T(8,128)}, f32[2,256,512]{2,1,0:T(8,128)S(1)}, u32[]{:S(2)}, u32[]{:S(2)}) collective-permute-start(f32[2,256,512]{2,1,0:T(8,128)} %pad_maximum_fusion.3), channel_id=1, source_target_pairs={{0,8},{8,0},{16,24},{24,16},{1,9},{9,1},{17,25},{25,17},{2,10},{10... | collective-permute-start | bytes 3145736 | tf_op jit(solution)/shard_map/ppermute | solution.py:19
  110.3 26.0 %collective-permute-start.21 = (f32[2,512,256]{2,1,0:T(8,128)}, f32[2,512,256]{2,1,0:T(8,128)}, u32[]{:S(2)}, u32[]{:S(2)}) collective-permute-start(f32[2,512,256]{2,1,0:T(8,128)} %pad_maximum_fusion.4), channel_id=1, source_target_pairs={{0,16},{8,24},{16,0},{24,8},{1,17},{9,25},{17,1},{25,9},{2,18},{10... | collective-permute-start | bytes 3145736 | tf_op jit(solution)/shard_map/ppermute | solution.py:19
  111.8 24.5 %collective-permute-start.20 = (f32[512,256]{1,0:T(8,128)}, f32[512,256]{1,0:T(8,128)S(1)}, u32[]{:S(2)}, u32[]{:S(2)}) collective-permute-start(f32[512,256]{1,0:T(8,128)} %get-tuple-element.63), channel_id=1, source_target_pairs={{0,4},{1,5},{2,6},{3,7},{4,0},{5,1},{6,2},{7,3},{8,12},{9,13},{10,... | collective-permute-start | bytes 1572872 | tf_op jit(solution)/shard_map/ppermute | solution.py:19
  136.3 7.4 %collective-permute-start.25 = (f32[2,512,256]{2,1,0:T(8,128)}, f32[2,512,256]{2,1,0:T(8,128)S(1)}, u32[]{:S(2)}, u32[]{:S(2)}) collective-permute-start(f32[2,512,256]{2,1,0:T(8,128)} %collective-permute-done.21.refs_8_.refs_10_), channel_id=1, source_target_pairs={{0,8},{8,0},{16,24},{24,16},{1,9},{9,1},{17,25},{25,17},{2,10},{10... | collective-permute-start | bytes 3145736 | tf_op jit(solution)/shard_map/ppermute | solution.py:19
  139.2 34.6 %collective-permute-start.24 = (f32[2,512,256]{2,1,0:T(8,128)}, f32[2,512,256]{2,1,0:T(8,128)S(1)}, u32[]{:S(2)}, u32[]{:S(2)}) collective-permute-start(f32[2,512,256]{2,1,0:T(8,128)} %pad_maximum_fusion.5), channel_id=1, source_target_pairs={{0,16},{8,24},{16,0},{24,8},{1,17},{9,25},{17,1},{25,9},{2,18},{10... | collective-permute-start | bytes 3145736 | tf_op jit(solution)/shard_map/ppermute | solution.py:19
  139.7 36.4 %collective-permute-start.26 = (f32[512,512]{1,0:T(8,128)}, f32[512,512]{1,0:T(8,128)}, u32[]{:S(2)}, u32[]{:S(2)}) collective-permute-start(f32[512,512]{1,0:T(8,128)} %shard_map.109), channel_id=1, source_target_pairs={{0,2},{1,3},{2,0},{3,1},{4,6},{5,7},{6,4},{7,5},{8,10},{9,11},{10,... | collective-permute-start | bytes 3145736 | tf_op jit(solution)/shard_map/ppermute | solution.py:19
  139.7 34.1 %collective-permute-start.23 = (f32[512,256]{1,0:T(8,128)S(1)}, f32[512,256]{1,0:T(8,128)}, u32[]{:S(2)}, u32[]{:S(2)}) collective-permute-start(f32[512,256]{1,0:T(8,128)S(1)} %copy-done.28), channel_id=1, source_target_pairs={{0,5},{1,4},{2,7},{3,6},{4,1},{5,0},{6,3},{7,2},{8,13},{9,12},{10,... | collective-permute-start | bytes 1572872 | tf_op jit(solution)/shard_map/ppermute | solution.py:19
  179.0 26.8 %collective-permute-start.27 = (f32[512,512]{1,0:T(8,128)}, f32[512,512]{1,0:T(8,128)}, u32[]{:S(2)}, u32[]{:S(2)}) collective-permute-start(f32[512,512]{1,0:T(8,128)} %shard_map.110), channel_id=1, source_target_pairs={{0,2},{1,3},{2,0},{3,1},{4,6},{5,7},{6,4},{7,5},{8,10},{9,11},{10,... | collective-permute-start | bytes 3145736 | tf_op jit(solution)/shard_map/ppermute | solution.py:19
  181.7 14.3 %collective-permute-start.28 = (f32[512,256]{1,0:T(8,128)}, f32[512,256]{1,0:T(8,128)S(1)}, u32[]{:S(2)}, u32[]{:S(2)}) collective-permute-start(f32[512,256]{1,0:T(8,128)} %collective-permute-done.23.refs_10_), channel_id=1, source_target_pairs={{0,16},{8,24},{16,0},{24,8},{1,17},{9,25},{17,1},{25,9},{2,18},{10... | collective-permute-start | bytes 1572872 | tf_op jit(solution)/shard_map/ppermute | solution.py:19
  (46 other events, 501.7 us)

commit v3 on v2

--- a/solution.py
+++ b/solution.py
@@ -145,10 +145,10 @@
     )(at, slopes, *[array for array, _ in ow_parts], *relax)
 
 
-def product_kernel(places, pieces, sums, *refs):
-    group = len(places) // pieces
-    col_ref, scaled_refs, weight_ref = refs[0], refs[1 : group + 2], refs[group + 2]
-    w_refs, refs = refs[group + 3 : group + 3 + len(places)], refs[group + 3 + len(places) :]
+def product_kernel(places, pieces, count, sum_places, *refs):
+    col_ref, scaled_refs, refs = refs[0], refs[1 : count + 1], refs[count + 1 :]
+    own_refs, refs = refs[: count * pieces - len(places)][:1], refs[min(1, count * pieces - len(places)) :]
+    w_refs, refs = refs[: len(places)], refs[len(places) :]
     scaled_here, w_here, sems = refs[-3:]
     rows, piece = w_here.shape[1], w_here.shape[2] // pieces
     spans = [pl.ds(p * piece, piece) for p in range(pieces)]
@@ -156,7 +156,7 @@
     def columns(i):
         return pl.ds(pl.multiple_of(col_ref[i] * piece, piece), piece)
 
-    sources = [weight_ref.at[:, columns(p)] for p in range(pieces)]
+    sources = [ref.at[:, columns(p)] for ref in own_refs for p in range(pieces)]
     sources += [ref if where is None else ref.at[where] for ref, where in zip(w_refs, places)]
     copies = []
 
@@ -164,31 +164,37 @@
         copies.append(pltpu.make_async_copy(source, target, sems.at[len(copies)]))
         copies[-1].start()
 
-    for j in range(group + 1):
+    for j in range(count):
         fetch(scaled_refs[j], scaled_here.at[j])
         for p in range(pieces):
             fetch(sources[j * pieces + p], w_here.at[j, :, spans[p]])
     operands = len(copies)
-    if sums is not None:
+    if sum_places is not None:
+        sums = len(sum_places)
         sum_refs, (near_ref, at_ref, margin_in) = refs[:sums], refs[sums : sums + 3]
         out_ref, margin_ref, block, near_here, sums_here = refs[-8:-3]
         for p in range(pieces):
             fetch(near_ref.at[:, :, columns(pieces + p)], near_here.at[:, :, spans[p]])
-        for i, ref in enumerate(sum_refs):
-            fetch(ref, sums_here.at[i])
+        for i, (ref, where) in enumerate(zip(sum_refs, sum_places)):
+            (far, p, row), column = where
+            target = sums_here.at[far, pl.ds(row, ref.shape[0]), spans[p]]
+            fetch(ref.at[:, pl.ds(column * piece, piece)], target)
     total = None
-    for j in range(group + 1):
+    for j in range(count):
         for copy in copies[j * (pieces + 1) : (j + 1) * (pieces + 1)]:
             copy.wait()
         high, low = two_terms(w_here[j])
         got = dot(scaled_here[j], jnp.concatenate([high, high], axis=0)) + dot(scaled_here[j, :, :rows], low)
         total = got if total is None else total + got
-    if sums is None:
-        refs[0][...] = total
+    if sum_places is None:
+        outs = refs[:-3]
+        height = total.shape[0] // len(outs)
+        for i, ref in enumerate(outs):
+            ref[...] = total[i * height : (i + 1) * height]
         return
     for copy in copies[operands:]:
         copy.wait()
-    for i in range(sums):
+    for i in range(sums_here.shape[0]):
         total = total + sums_here[i]
     block[...] = total
     puts = []
@@ -203,23 +209,24 @@
         put.wait()
 
 
-def product(scaled, weight, col, w_parts, final=None):
+def product(scaled, weight, col, w_parts, split=1, final=None):
     specs, rows = scaled[0].shape[0], scaled[0].shape[1] // 2
     piece = w_parts[0][0].shape[-1]
-    pieces = len(w_parts) // (len(scaled) - 1)
+    pieces = col.shape[0] // 2
+    weight = [weight] if len(w_parts) < len(scaled) * pieces else []
     whole = pl.BlockSpec(memory_space=pltpu.VMEM)
     there = pl.BlockSpec(memory_space=pltpu.HBM)
-    args = [col, *scaled, weight, *[array for array, _ in w_parts]]
+    args = [col, *scaled, *weight, *[array for array, _ in w_parts]]
     in_specs = [pl.BlockSpec(memory_space=pltpu.SMEM)] + [there] * (len(args) - 1)
     scratch, n_sems = [], (1 + pieces) * len(scaled)
-    aliases, sums = {}, None
+    aliases, sum_places = {}, None
     if final is None:
-        out_shape, out_specs = jax.ShapeDtypeStruct((specs, pieces * piece), F32), whole
+        out_shape, out_specs = [jax.ShapeDtypeStruct((specs // split, pieces * piece), F32)] * split, [whole] * split
     else:
         sum_parts, at, near, margin, out = final
-        sums = len(sum_parts)
+        sums, sum_places = len(sum_parts), [where for _, where in sum_parts]
         in_specs += [there] * (sums + 1) + [whole] * 2
-        args += [*sum_parts, near, at, margin]
+        args += [*[array for array, _ in sum_parts], near, at, margin]
         if out is not None:
             aliases = {len(args): 0}
             in_specs.append(there)
@@ -229,7 +236,7 @@
         scratch = [
             pltpu.VMEM((specs, pieces * piece), F32),
             pltpu.VMEM((2, near.shape[1], pieces * piece), F32),
-            pltpu.VMEM((sums, specs, pieces * piece), F32),
+            pltpu.VMEM((1 + max(where[0][0] for where in sum_places), specs, pieces * piece), F32),
         ]
         n_sems += pieces + sums
     scratch += [
@@ -238,7 +245,7 @@
         pltpu.SemaphoreType.DMA((n_sems,)),
     ]
     return pl.pallas_call(
-        functools.partial(product_kernel, [place for _, place in w_parts], pieces, sums),
+        functools.partial(product_kernel, [place for _, place in w_parts], pieces, len(scaled), sum_places),
         out_shape=out_shape,
         in_specs=in_specs,
         out_specs=out_specs,
@@ -257,11 +264,12 @@
         self.got[name] = value
         self.fresh.append(name)
 
-    def edge(self, *sends):
-        held = [self.got[name] for name in self.fresh]
+    def edge(self, *sends, only=None):
+        names = self.fresh if only is None else only
+        held = [self.got[name] for name in names]
         done = lax.optimization_barrier((*[value for _, value, _ in sends], *held))
-        self.got.update(zip(self.fresh, done[len(sends) :]))
-        self.fresh = []
+        self.got.update(zip(names, done[len(sends) :]))
+        self.fresh = [name for name in self.fresh if name not in names]
         for (name, _, move), value in zip(sends, done):
             self.keep(name, move(value))
 
@@ -276,8 +284,9 @@
     images, classes = center.shape[0], out_weight.shape[0]
     piece = cols // QUARTERS
     cut = sites // 2
-    group = (1, cut, cut + 1)
-    targets = [2 * m for m in range(1, sites // 4)] + [0]
+    pair = 2
+    group = (pair, cut, cut + pair)
+    targets = [m for m in range(1, sites) if not m & (cut + pair)] + [0]
 
     def to_site(k):
         return functools.partial(swap, axis="neuron", size=sites, k=k)
@@ -320,7 +329,7 @@
     ow = lax.dynamic_slice(out_weight, (start_of(q), 0), (share, rows))
     for j in group:
         where["ow", j, 0] = ("ow", j, 0), None
-    send(("ow", 1, 0), ow, to_site(1))
+    t = targets[0]
     near = jnp.stack([center, radius])
     boxes = near[None]
     order = [0]
@@ -328,14 +337,12 @@
     while k:
         if k == 1:
             keep("boxes", boxes)
-            edge((("ow", cut, 0), ow, to_site(cut)))
+            edge((("ow", cut, 0), ow, to_site(cut)), (("ow", pair, 0), ow, to_site(pair)), only=["boxes"])
             boxes = got["boxes"]
         boxes = jnp.concatenate([boxes, to_site(k)(boxes)])
         order = order + [o ^ k for o in order]
         k //= 2
     keep("boxes", boxes)
-    t = targets[0]
-    send(*columns(t, 1))
     k = 1
     while k < members:
         near = jnp.concatenate([near, to_member(k)(near)], axis=1)
@@ -346,11 +353,9 @@
         spot = jnp.where((n ^ jnp.arange(sites)) == o, s, spot)
 
     edge(columns(t, cut))
-    send(("ow", cut + 1, 0), got["ow", cut, 0], to_site(1))
-    send(*share_out(2, ("ow", 1, 0)))
+    send(("ow", cut + pair, 0), got["ow", cut, 0], to_site(pair))
+    send(*share_out(2, ("ow", pair, 0)))
     send(*share_out(2, ("ow", cut, 0)))
-    if len(targets) > 1:
-        send(*columns(targets[1], 1))
     both = interval(got["boxes"], weight, bias[None], masks, jnp.append(spot, g))
     keep("both", lax.all_gather(both, "spec", axis=1, tiled=True))
     labels = jnp.sum(jnp.where(spec_image[:, None] == jnp.arange(image_labels.shape[0]), image_labels, 0), axis=1)
@@ -362,59 +367,80 @@
     near_image = ((spec_image // images) ^ g) * images + spec_image % images
     keep("at", jnp.stack([place(labels), place(runner_up), spec_image, labels, runner_up, near_image], axis=1))
 
-    edge(columns(t, cut + 1))
-    send(*share_out(2, ("ow", cut + 1, 0)))
-    send(*share_out(2, (t, 1, 0)))
-    send(*share_out(1, *[("ow", j, r) for j in (1, cut) for r in (0, 2)]))
+    edge(columns(t, cut + pair), columns(t, pair))
+    send(*share_out(2, ("ow", cut + pair, 0)))
+    send(*share_out(2, (t, cut, 0)))
     slopes, offsets = got["both"][0], got["both"][1]
-    keep("slopes", jnp.stack([slopes, to_site(cut)(slopes)]))
-    *scaled, margin = scale(got["at"], [(out_weight, None)], slopes, offsets, bias[None])
-    keep("scaled0", scaled[0])
-    out, sums = None, {}
-
-    def some_product(t, *members_at):
-        parts = [part((t, j, r)) for j in group for r in members_at]
+    slopes = jnp.stack([slopes, to_site(pair)(slopes)])
+    slopes = jnp.concatenate([slopes, to_site(cut)(slopes)])
+    keep("slopes", slopes)
+    slopes = slopes[0]
+    scaled, margin = scale(got["at"], [(out_weight, None)], slopes, offsets, bias[None])
+    keep("margin", margin)
+    keep(("scaled", 0), scaled)
+
+    sum_parts = {}
+
+    def some_product(t, *members_at, sites=(0, *group), last=True):
+        parts = [part((t, j, r)) for j in sites if j for r in members_at]
         col = jnp.stack([(n ^ t) * QUARTERS + (q ^ r) for r in members_at] + [q ^ r for r in members_at])
-        scaled = [got["scaled0"]] + [got["scaled", j] for j in group]
-        if t:
-            return product(scaled, weight, col, parts)
-        had = [got["sum", f, members_at] for f in targets[:-1]]
-        return product(scaled, weight, col, parts, (had, got["at"], got["near"], margin, out))
+        scaled = [got["scaled", j] for j in sites]
+        if t or not last:
+            (made,) = product(scaled, weight, col, parts)
+            keep(("product", t, members_at), made)
+            return
+        had = []
+        for i, f in enumerate(targets):
+            for p, r in enumerate(members_at):
+                if f:
+                    had.append((got["sum", f, members_at], ((i, p, 0), p)))
+                elif len(sites) <= len(group):
+                    had.append((got["product", t, members_at], ((i, p, 0), p)))
+        final = had, got["at"], got["near"], got["margin"], got.get("out")
+        out, margin = product(scaled, weight, col, parts, final=final)
+        keep("out", out)
+        keep("margin", margin)
+
+    def send_sum(t, *members_at):
+        send(("sum", t, members_at), got["product", t, members_at], to_site(t))
 
     for i, t in enumerate(targets):
         after = targets[i + 1 :][:1]
-        late = [cut, cut + 1] if i == 0 else [cut + 1]
-        early = [j for j in group if j not in late]
-        edge(*([columns(after[0], cut)] if after else []))
+        edge(*([columns(after[0], cut), columns(after[0], pair)] if after else []))
         if i:
-            send(("sum", targets[i - 1], (2, 3)), got["product"], to_site(targets[i - 1]))
+            send_sum(targets[i - 1], 2, 3)
+        else:
+            slopes = got["slopes"]
         if i == 0:
-            slopes = jnp.concatenate([got["slopes"], to_site(1)(got["slopes"])])
-        elif after:
-            send(*columns(after[0], 1))
-        send(*share_out(2, *[(t, j, 0) for j in late]))
-        send(*share_out(1, *[(t, j, 0) for j in group], *[(t, j, 2) for j in early]))
+            send(*share_out(2, (t, pair, 0)))
+        send(*share_out(2, (t, cut + pair, 0)))
+        if t:
+            send(*share_out(1, *[(t, j, 0) for j in group]))
+        else:
+            send(*share_out(1, (t, pair, 0), (t, cut, 0)))
+            send(*share_out(1, (t, cut + pair, 0)))
+            send(*share_out(1, (t, pair, 2), (t, cut, 2)))
         if i == 0:
-            send(*share_out(1, ("ow", cut + 1, 0), ("ow", cut + 1, 2)))
-            for j, slot in ((cut, 1), (1, 2), (cut + 1, 3)):
+            send(*share_out(1, *[("ow", j, r) for j in group for r in (0, 2)]))
+            for j, slot in ((pair, 1), (cut, 2), (cut + pair, 3)):
                 parts = [part(("ow", j, r)) for r in range(QUARTERS)]
                 (got["scaled", j],) = scale(got["at"], parts, slopes[slot])
+        some_product(t, 0, 1)
+        if not t:
+            some_product(t, 2, 3, sites=(0, pair, cut), last=False)
+        names = [name for name in work.fresh if name[0] != "sum" or t]
+        edge(*([columns(after[0], cut + pair)] if after else []), only=names)
+        if after:
+            send(*share_out(2, (after[0], cut, 0)))
+            send(*share_out(2, (after[0], pair, 0)))
         if t:
-            keep("product", some_product(t, 0, 1))
+            send(*share_out(1, *[(t, j, 2) for j in group]))
+            send_sum(t, 0, 1)
+            some_product(t, 2, 3)
         else:
-            out, margin = some_product(t, 0, 1)
-            keep("out", out)
-            keep("margin", margin)
-        edge(*([columns(after[0], cut + 1)] if after else []))
-        if after:
-            send(*share_out(2, (after[0], 1, 0), (after[0], cut, 0)))
-        send(*share_out(1, *[(t, j, 2) for j in late]))
-        if t:
-            send(("sum", t, (0, 1)), got["product"], to_site(t))
-            keep("product", some_product(t, 2, 3))
-        else:
-            out, margin = got["out"], got["margin"]
-            out, margin = some_product(t, 2, 3)
+            send(*share_out(1, (t, cut + pair, 2)))
+            some_product(t, 2, 3, sites=(cut + pair,))
+    out, margin = got["out"], got["margin"]
     margin = margin + (to_site(1)(margin) + to_site(2)(margin) + to_site(3)(margin))
     k = 4
     while k < sites:

time: 232 us -> 216 us (0.931)
  waiting for transfers between devices: 95.2 us -> 67.7 us
  starting transfers between devices: 37.7 us -> 43.2 us
  Pallas kernels: 53.6 us -> 57 us
    ppermute x35 -> x38, waiting for transfers between devices: 95.2 us -> 67.7 us  [swap(): return lax.ppermute(array, axis, [(i, i ^ k) for i in range(size)])]
    ppermute x35 -> x38, starting transfers between devices: 37.7 us -> 43.2 us  [swap(): return lax.ppermute(array, axis, [(i, i ^ k) for i in range(size)])]
    pallas_call x4 -> x5, Pallas kernels: 31.1 us -> 34.5 us  [product(): pl.pallas_call(functools.partial(product_kernel, [place for _, place in w...]
    another operation x6 -> x4, other arithmetic: 12.9 us -> 9.97 us  [share_out(): return (tuple(names), jnp.stack(pieces), to_member(k))]
    unnamed x70 -> x65, local copies, waits for them, and re-layouts: 11.6 us -> 12.2 us
  transfers between devices with their start and end apart: 35 -> 38, of which waited for: 18 -> 18; matrix products, arithmetic and copies ran while one was open for 7% -> 11% of each run, Pallas kernels for 20% -> 24%
where the time goes in v3:
time: 216 us; the launch traced here: 215 us
  waiting for transfers between devices  67.7 us (31%)
  Pallas kernels  57 us (26%)
  starting transfers between devices  43.2 us (20%)
  other arithmetic  20.3 us (9%)
  local copies, waits for them, and re-layouts  20 us (9%)
  blocking collectives  5.74 us (3%)
    ppermute x38, waiting for transfers between devices, swap(): return lax.ppermute(array, axis, [(i, i ^ k) for i in range(size)])  67.7 us
    ppermute x38, starting transfers between devices, swap(): return lax.ppermute(array, axis, [(i, i ^ k) for i in range(size)])  43.2 us
    pallas_call x5, Pallas kernels, product(): pl.pallas_call(functools.partial(product_kernel, [place for _, place in w...  34.5 us
    pallas_call x1, Pallas kernels, interval(): pl.pallas_call(interval_kernel, out_shape=jax.ShapeDtypeStruct((2, images...  14.3 us
    unnamed x65, local copies, waits for them, and re-layouts  12.2 us
    another operation x4, other arithmetic, share_out(): return (tuple(names), jnp.stack(pieces), to_member(k))  9.97 us
    pallas_call x4, Pallas kernels, scale(): pl.pallas_call(functools.partial(scale_kernel, [(array.shape, place) for...  8.27 us
    all_gather x1, blocking collectives, local(): keep('both', lax.all_gather(both, 'spec', axis=1, tiled=True))  5.74 us
  transfers between devices with their start and end apart: 38, of which 18 were waited for; matrix products, arithmetic and copies ran while one was open for 11% of the time, Pallas kernels for 24%

profile of v3, /device:TPU:0, one launch (start us, length us, event | category | flops | bytes accessed | tf_op | source)
XLA Modules:
  0.0 215.1 jit_solution(2557914294794927257)
XLA Ops:
  1.4 4.1 %collective-permute-start = (f32[1,2,8,1024]{3,2,1,0:T(8,128)S(1)}, f32[1,2,8,1024]{3,2,1,0:T(8,128)S(1)}, u32[]{:S(2)}, u32[]{:S(2)}) collective-permute-start(f32[1,2,8,1024]{3,2,1,0:T(8,128)S(1)} %get-tuple-element.107), channel_id=1, source_target_pairs={{0,4},{1,5},{2,6},{3,7},{4,0},{5,1},{6,2},{7,3},{8,12},{9,13},{10,... | collective-permute-start | bytes 196616 | tf_op jit(solution)/shard_map/ppermute | solution.py:19
  11.7 2.5 %collective-permute-done.1 = f32[2,2,8,1024]{3,2,1,0:T(8,128)S(1)} collective-permute-done((f32[2,2,8,1024]{3,2,1,0:T(8,128)S(1)}, f32[2,2,8,1024]{3,2,1,0:T(8,128)S(1)}, u32[]{:S(2)}, u32[]{:S(2)}) %collective-permute-start.1) | collective-permute-done | bytes 131104 | tf_op jit(solution)/shard_map/ppermute | solution.py:19
  14.2 2.4 %collective-permute-start.2 = (f32[256,512]{1,0:T(8,128)S(1)}, f32[256,512]{1,0:T(8,128)S(1)}, u32[]{:S(2)}, u32[]{:S(2)}) collective-permute-start(f32[256,512]{1,0:T(8,128)S(1)} %constant_dynamic-slice_fusion.3), channel_id=1, source_target_pairs={{0,4},{1,5},{2,6},{3,7},{4,0},{5,1},{6,2},{7,3},{8,12},{9,13},{10,... | collective-permute-start | bytes 1572872 | tf_op jit(solution)/shard_map/ppermute | solution.py:19
  22.3 3.4 %constant_dynamic-slice_fusion = (f32[512,256]{1,0:T(8,128)}, f32[512,256]{1,0:T(8,128)}, f32[512,256]{1,0:T(8,128)}, f32[512,256]{1,0:T(8,128)S(1)}, f32[512,256]{1,0:T(8,128)}, /*index=5*/f32[512,256]{1,0:T(8,128)}) fusion(f32[512,8192]{1,0:T(8,128)} %refs_4_.1, s32[]{:T(128)S(6)} %select_n.101, s32[]{:T(128)S(6)} %select_n.100, s32[]{:T(128)S(6)} %select_n.99, ...), kind=kLoop, calls=%fused_computation.57 | loop fusion | bytes 6291480 | tf_op jit(solution)/shard_map/dynamic_slice | solution.py:307
  27.2 12.0 %collective-permute-done.2.refs_0_ = f32[256,512]{1,0:T(8,128)S(1)} collective-permute-done((f32[256,512]{1,0:T(8,128)S(1)}, f32[256,512]{1,0:T(8,128)S(1)}, u32[]{:S(2)}, u32[]{:S(2)}) %collective-permute-start.2) | collective-permute-done | bytes 524320 | tf_op jit(solution)/shard_map/ppermute | solution.py:19
  42.3 2.3 %collective-permute-start.7 = (f32[512,256]{1,0:T(8,128)S(1)}, f32[512,256]{1,0:T(8,128)}, u32[]{:S(2)}, u32[]{:S(2)}) collective-permute-start(f32[512,256]{1,0:T(8,128)S(1)} %get-tuple-element.51), channel_id=1, source_target_pairs={{0,4},{1,5},{2,6},{3,7},{4,0},{5,1},{6,2},{7,3},{8,12},{9,13},{10,... | collective-permute-start | bytes 1572872 | tf_op jit(solution)/shard_map/ppermute | solution.py:19
  45.3 14.3 %shard_map.104 = f32[2,8,512]{2,1,0:T(8,128)S(1)} custom-call(s32[9]{0:T(128)S(1)} %pad_add_fusion.spot_ref, f32[8,2,8,1024]{3,2,1,0:T(8,128)S(1)} %pad_maximum_fusion.4.boxes_ref, f32[512,8192]{1,0:T(8,128)} %refs_4_.1, f32[1,512]{1,0:T(1,128)S(1)} %bitcast.57, s32[32,512]{1,0:T(8,128)S(1)} %copy-done.18), custom_call_target="tpu_custom_call" | custom-call | tf_op jit(solution)/shard_map/pallas_call | solution.py:90
  59.6 5.7 %all_gather.3 = f32[2,32,512]{2,1,0:T(8,128)S(1)} all-gather(f32[2,8,512]{2,1,0:T(8,128)S(1)} %shard_map.104), channel_id=1, replica_groups=mesh['spec'=4,'neuron'=8] {'spec'}, dimensions={1}, use_global_device_ids=true | all-gather | bytes 163840 | tf_op jit(solution)/shard_map/all_gather | solution.py:360
  76.7 2.9 %shard_map.105 = (bf16[512,1024]{1,0:T(8,128)(2,1)S(1)}, f32[8,512]{1,0:T(8,128)S(1)}) custom-call(s32[512,6]{1,0:T(8,128)S(1)} %copy.29.at_ref.refs_15_.refs_9_, f32[32,512]{1,0:T(8,128)S(1)} %get-tuple-element.104.slopes_ref, f32[1000,512]{1,0:T(8,128)S(1)} %copy-done.5, f32[32,512]{1,0:T(8,128)S(1)} %get-tuple-element.103.refs_1_, f32[1,512]{1,0:T(1,128)S(1)} %bitcast.58), custom_call_target="tpu_custom_call" | custom-call | tf_op jit(solution)/shard_map/pallas_call | solution.py:140
  82.6 19.6 %collective-permute-done.16 = f32[2,32,512]{2,1,0:T(8,128)S(1)} collective-permute-done((f32[2,32,512]{2,1,0:T(8,128)S(1)}, f32[2,32,512]{2,1,0:T(8,128)S(1)}, u32[]{:S(2)}, u32[]{:S(2)}) %collective-permute-start.16) | collective-permute-done | bytes 131104 | tf_op jit(solution)/shard_map/ppermute | solution.py:19
  105.5 2.6 %pad_maximum_fusion = f32[3,512,256]{2,1,0:T(8,128)} fusion(f32[1,512,256]{2,1,0:T(8,128)} %bitcast.26, f32[1,512,256]{2,1,0:T(8,128)} %bitcast.25, f32[1,512,256]{2,1,0:T(8,128)} %bitcast.24), kind=kLoop, calls=%fused_computation | loop fusion | flops 786432 | bytes 3145728 | tf_op jit(solution)/shard_map/stack | solution.py:327
  110.1 3.2 %collective-permute-start.19 = (f32[512,256]{1,0:T(8,128)}, f32[512,256]{1,0:T(8,128)}, u32[]{:S(2)}, u32[]{:S(2)}) collective-permute-start(f32[512,256]{1,0:T(8,128)} %get-tuple-element.68), channel_id=1, source_target_pairs={{0,2},{1,3},{2,0},{3,1},{4,6},{5,7},{6,4},{7,5},{8,10},{9,11},{10,... | collective-permute-start | bytes 1572872 | tf_op jit(solution)/shard_map/ppermute | solution.py:19
  125.1 7.0 %shard_map.109 = f32[512,512]{1,0:T(8,128)} custom-call(s32[4]{0:T(128)} %add_add_fusion.2.refs_0_, bf16[512,1024]{1,0:T(8,128)(2,1)} %copy-done.3, bf16[512,1024]{1,0:T(8,128)(2,1)} %copy-done.2, bf16[512,1024]{1,0:T(8,128)(2,1)} %copy-done.1, bf16[512,1024]{1,0:T(8,128)(2,1)} %copy-done, f32[512,8192]{1,0:T(8,128)} %refs_4_.1, ...), custom_call_target="tpu_custom_call" | custom-call | tf_op jit(solution)/shard_map/pallas_call | solution.py:247
  132.1 4.1 %collective-permute-done.18.refs_8_ = f32[512,256]{1,0:T(8,128)} collective-permute-done((f32[512,256]{1,0:T(8,128)}, f32[512,256]{1,0:T(8,128)}, u32[]{:S(2)}, u32[]{:S(2)}) %collective-permute-start.18) | collective-permute-done | bytes 524320 | tf_op jit(solution)/shard_map/ppermute | solution.py:19
  136.4 2.6 %pad_maximum_fusion.1 = f32[3,512,256]{2,1,0:T(8,128)} fusion(f32[1,512,256]{2,1,0:T(8,128)} %bitcast.35, f32[1,512,256]{2,1,0:T(8,128)} %bitcast.34, f32[1,512,256]{2,1,0:T(8,128)} %bitcast.33), kind=kLoop, calls=%fused_computation.1 | loop fusion | flops 786432 | bytes 3145728 | tf_op jit(solution)/shard_map/stack | solution.py:327
  148.1 7.2 %shard_map.110 = f32[512,512]{1,0:T(8,128)} custom-call(s32[4]{0:T(128)} %add_add_fusion.3.refs_0_, bf16[512,1024]{1,0:T(8,128)(2,1)} %copy-done.3, bf16[512,1024]{1,0:T(8,128)(2,1)} %copy-done.2, bf16[512,1024]{1,0:T(8,128)(2,1)} %copy-done.1, bf16[512,1024]{1,0:T(8,128)(2,1)} %copy-done, f32[512,8192]{1,0:T(8,128)} %refs_4_.1, ...), custom_call_target="tpu_custom_call" | custom-call | tf_op jit(solution)/shard_map/pallas_call | solution.py:247
  157.0 10.3 %collective-permute-done.25.refs_5_ = f32[512,256]{1,0:T(8,128)} collective-permute-done((f32[512,256]{1,0:T(8,128)}, f32[512,256]{1,0:T(8,128)}, u32[]{:S(2)}, u32[]{:S(2)}) %collective-permute-start.25) | collective-permute-done | bytes 524320 | tf_op jit(solution)/shard_map/ppermute | solution.py:19
  167.3 2.5 %pad_maximum_fusion.3 = f32[2,512,256]{2,1,0:T(8,128)} fusion(f32[1,512,256]{2,1,0:T(8,128)S(1)} %bitcast.59, f32[1,512,256]{2,1,0:T(8,128)} %bitcast.40), kind=kLoop, calls=%fused_computation.3 | loop fusion | flops 262144 | bytes 2097152 | tf_op jit(solution)/shard_map/stack | solution.py:327
  173.6 8.5 %shard_map.111 = (f32[512,1024]{1,0:T(8,128)}, f32[8,512]{1,0:T(8,128)}) custom-call(s32[4]{0:T(128)} %add_add_fusion.4.refs_0_, bf16[512,1024]{1,0:T(8,128)(2,1)} %copy-done.3, bf16[512,1024]{1,0:T(8,128)(2,1)} %copy-done.2, bf16[512,1024]{1,0:T(8,128)(2,1)} %copy-done.1, bf16[512,1024]{1,0:T(8,128)(2,1)} %copy-done, f32[512,8192]{1,0:T(8,128)} %refs_4_.1, ...), custom_call_target="tpu_custom_call" | custom-call | tf_op jit(solution)/shard_map/pallas_call | solution.py:247
  182.1 6.0 %shard_map.112.refs_6_.refs_7_ = f32[512,512]{1,0:T(8,128)} custom-call(s32[4]{0:T(128)} %add_add_fusion.1.refs_0_, bf16[512,1024]{1,0:T(8,128)(2,1)} %copy-done.3, bf16[512,1024]{1,0:T(8,128)(2,1)} %copy-done.2, bf16[512,1024]{1,0:T(8,128)(2,1)} %copy-done.1, f32[512,8192]{1,0:T(8,128)} %refs_4_.1, f32[512,256]{1,0:T(8,128)} %collective-permute-done.25.refs_5_, ...), custom_call_target="tpu_custom_call" | custom-call | tf_op jit(solution)/shard_map/pallas_call | solution.py:247
  188.4 7.5 %collective-permute-done.33.refs_4_.refs_5_ = f32[512,512]{1,0:T(8,128)S(1)} collective-permute-done((f32[512,512]{1,0:T(8,128)}, f32[512,512]{1,0:T(8,128)S(1)}, u32[]{:S(2)}, u32[]{:S(2)}) %collective-permute-start.33) | collective-permute-done | bytes 1048608 | tf_op jit(solution)/shard_map/ppermute | solution.py:19
  197.7 5.8 %shard_map.113 = (f32[512,1024]{1,0:T(8,128)}, f32[8,512]{1,0:T(8,128)}) custom-call(s32[4]{0:T(128)} %add_add_fusion.1.refs_0_, bf16[512,1024]{1,0:T(8,128)(2,1)} %copy-done, f32[512,256]{1,0:T(8,128)} %copy-done.26, f32[512,256]{1,0:T(8,128)} %copy-done.27, f32[512,512]{1,0:T(8,128)} %copy-done.22, ...), custom_call_target="tpu_custom_call", output_to_operand_aliasing={{0}: (11, {})} | custom-call | tf_op jit(solution)/shard_map/pallas_call | solution.py:247
  204.1 3.0 %collective-permute-start.36 = (f32[8,512]{1,0:T(8,128)}, f32[8,512]{1,0:T(8,128)S(1)}, u32[]{:S(2)}, u32[]{:S(2)}) collective-permute-start(f32[8,512]{1,0:T(8,128)} %get-tuple-element.93), channel_id=1, source_target_pairs={{0,3},{1,2},{2,1},{3,0},{4,7},{5,6},{6,5},{7,4},{8,11},{9,10},{10,... | collective-permute-start | bytes 49160 | tf_op jit(solution)/shard_map/ppermute | solution.py:19
  209.9 2.7 %collective-permute-start.37 = (f32[8,512]{1,0:T(8,128)S(1)}, f32[8,512]{1,0:T(8,128)S(1)}, u32[]{:S(2)}, u32[]{:S(2)}) collective-permute-start(f32[8,512]{1,0:T(8,128)S(1)} %add_add_fusion), channel_id=1, source_target_pairs={{0,4},{1,5},{2,6},{3,7},{4,0},{5,1},{6,2},{7,3},{8,12},{9,13},{10,... | collective-permute-start | bytes 49160 | tf_op jit(solution)/shard_map/ppermute | solution.py:19
  (158 shorter events, 71.7 us)
Async XLA Ops:
  5.5 12.8 %collective-permute-start.5 = (f32[2,8,1024]{2,1,0:T(8,128)S(1)}, f32[2,8,1024]{2,1,0:T(8,128)S(1)}, u32[]{:S(2)}, u32[]{:S(2)}) collective-permute-start(f32[2,8,1024]{2,1,0:T(8,128)S(1)} %get-tuple-element.106), channel_id=1, source_target_pairs={{0,8},{8,0},{16,24},{24,16},{1,9},{9,1},{17,25},{25,17},{2,10},{10... | collective-permute-start | bytes 196616 | tf_op jit(solution)/shard_map/ppermute | solution.py:19
  14.2 24.9 %collective-permute-start.2 = (f32[256,512]{1,0:T(8,128)S(1)}, f32[256,512]{1,0:T(8,128)S(1)}, u32[]{:S(2)}, u32[]{:S(2)}) collective-permute-start(f32[256,512]{1,0:T(8,128)S(1)} %constant_dynamic-slice_fusion.3), channel_id=1, source_target_pairs={{0,4},{1,5},{2,6},{3,7},{4,0},{5,1},{6,2},{7,3},{8,12},{9,13},{10,... | collective-permute-start | bytes 1572872 | tf_op jit(solution)/shard_map/ppermute | solution.py:19
  16.6 22.9 %collective-permute-start.3 = (f32[256,512]{1,0:T(8,128)S(1)}, f32[256,512]{1,0:T(8,128)S(1)}, u32[]{:S(2)}, u32[]{:S(2)}) collective-permute-start(f32[256,512]{1,0:T(8,128)S(1)} %constant_dynamic-slice_fusion.3), channel_id=1, source_target_pairs={{0,2},{1,3},{2,0},{3,1},{4,6},{5,7},{6,4},{7,5},{8,10},{9,11},{10,... | collective-permute-start | bytes 1572872 | tf_op jit(solution)/shard_map/ppermute | solution.py:19
  39.5 26.6 %collective-permute-start.10 = (f32[256,512]{1,0:T(8,128)S(1)}, f32[256,512]{1,0:T(8,128)S(1)}, u32[]{:S(2)}, u32[]{:S(2)}) collective-permute-start(f32[256,512]{1,0:T(8,128)S(1)} %collective-permute-done.2.refs_0_), channel_id=1, source_target_pairs={{0,16},{8,24},{16,0},{24,8},{1,17},{9,25},{17,1},{25,9},{2,18},{10... | collective-permute-start | bytes 1572872 | tf_op jit(solution)/shard_map/ppermute | solution.py:19
  41.0 26.5 %collective-permute-start.8 = (f32[256,512]{1,0:T(8,128)S(1)}, f32[256,512]{1,0:T(8,128)S(1)}, u32[]{:S(2)}, u32[]{:S(2)}) collective-permute-start(f32[256,512]{1,0:T(8,128)S(1)} %collective-permute-done.2.refs_0_), channel_id=1, source_target_pairs={{0,2},{1,3},{2,0},{3,1},{4,6},{5,7},{6,4},{7,5},{8,10},{9,11},{10,... | collective-permute-start | bytes 1572872 | tf_op jit(solution)/shard_map/ppermute | solution.py:19
  42.3 25.2 %collective-permute-start.7 = (f32[512,256]{1,0:T(8,128)S(1)}, f32[512,256]{1,0:T(8,128)}, u32[]{:S(2)}, u32[]{:S(2)}) collective-permute-start(f32[512,256]{1,0:T(8,128)S(1)} %get-tuple-element.51), channel_id=1, source_target_pairs={{0,4},{1,5},{2,6},{3,7},{4,0},{5,1},{6,2},{7,3},{8,12},{9,13},{10,... | collective-permute-start | bytes 1572872 | tf_op jit(solution)/shard_map/ppermute | solution.py:19
  44.6 22.9 %collective-permute-start.9 = (f32[256,512]{1,0:T(8,128)S(1)}, f32[256,512]{1,0:T(8,128)S(1)}, u32[]{:S(2)}, u32[]{:S(2)}) collective-permute-start(f32[256,512]{1,0:T(8,128)S(1)} %collective-permute-done.3.refs_0_), channel_id=1, source_target_pairs={{0,16},{8,24},{16,0},{24,8},{1,17},{9,25},{17,1},{25,9},{2,18},{10... | collective-permute-start | bytes 1572872 | tf_op jit(solution)/shard_map/ppermute | solution.py:19
  70.3 33.5 %collective-permute-start.11 = (f32[512,256]{1,0:T(8,128)}, f32[512,256]{1,0:T(8,128)}, u32[]{:S(2)}, u32[]{:S(2)}) collective-permute-start(f32[512,256]{1,0:T(8,128)} %get-tuple-element.56), channel_id=1, source_target_pairs={{0,6},{1,7},{2,4},{3,5},{4,2},{5,3},{6,0},{7,1},{8,14},{9,15},{10,... | collective-permute-start | bytes 1572872 | tf_op jit(solution)/shard_map/ppermute | solution.py:19
  72.5 31.4 %collective-permute-start.12 = (f32[512,256]{1,0:T(8,128)}, f32[512,256]{1,0:T(8,128)}, u32[]{:S(2)}, u32[]{:S(2)}) collective-permute-start(f32[512,256]{1,0:T(8,128)} %get-tuple-element.57), channel_id=1, source_target_pairs={{0,2},{1,3},{2,0},{3,1},{4,6},{5,7},{6,4},{7,5},{8,10},{9,11},{10,... | collective-permute-start | bytes 1572872 | tf_op jit(solution)/shard_map/ppermute | solution.py:19
  73.6 30.2 %collective-permute-start.13 = (f32[256,512]{1,0:T(8,128)S(1)}, f32[256,512]{1,0:T(8,128)S(1)}, u32[]{:S(2)}, u32[]{:S(2)}) collective-permute-start(f32[256,512]{1,0:T(8,128)S(1)} %collective-permute-done.8.refs_0_), channel_id=1, source_target_pairs={{0,16},{8,24},{16,0},{24,8},{1,17},{9,25},{17,1},{25,9},{2,18},{10... | collective-permute-start | bytes 1572872 | tf_op jit(solution)/shard_map/ppermute | solution.py:19
  75.1 28.7 %collective-permute-start.14 = (f32[512,256]{1,0:T(8,128)}, f32[512,256]{1,0:T(8,128)}, u32[]{:S(2)}, u32[]{:S(2)}) collective-permute-start(f32[512,256]{1,0:T(8,128)} %collective-permute-done.7.refs_8_), channel_id=1, source_target_pairs={{0,16},{8,24},{16,0},{24,8},{1,17},{9,25},{17,1},{25,9},{2,18},{10... | collective-permute-start | bytes 1572872 | tf_op jit(solution)/shard_map/ppermute | solution.py:19
  80.6 21.6 %collective-permute-start.16 = (f32[2,32,512]{2,1,0:T(8,128)S(1)}, f32[2,32,512]{2,1,0:T(8,128)S(1)}, u32[]{:S(2)}, u32[]{:S(2)}) collective-permute-start(f32[2,32,512]{2,1,0:T(8,128)S(1)} %pad_maximum_fusion.10), channel_id=1, source_target_pairs={{0,4},{1,5},{2,6},{3,7},{4,0},{5,1},{6,2},{7,3},{8,12},{9,13},{10,... | collective-permute-start | bytes 393224 | tf_op jit(solution)/shard_map/ppermute | solution.py:19
  108.1 16.9 %collective-permute-start.22 = (f32[3,512,256]{2,1,0:T(8,128)}, f32[3,512,256]{2,1,0:T(8,128)}, u32[]{:S(2)}, u32[]{:S(2)}) collective-permute-start(f32[3,512,256]{2,1,0:T(8,128)} %pad_maximum_fusion), channel_id=1, source_target_pairs={{0,8},{8,0},{16,24},{24,16},{1,9},{9,1},{17,25},{25,17},{2,10},{10... | collective-permute-start | bytes 4718600 | tf_op jit(solution)/shard_map/ppermute | solution.py:19
  108.6 27.8 %collective-permute-start.20 = (f32[512,256]{1,0:T(8,128)}, f32[512,256]{1,0:T(8,128)}, u32[]{:S(2)}, u32[]{:S(2)}) collective-permute-start(f32[512,256]{1,0:T(8,128)} %collective-permute-done.12.refs_6_), channel_id=1, source_target_pairs={{0,16},{8,24},{16,0},{24,8},{1,17},{9,25},{17,1},{25,9},{2,18},{10... | collective-permute-start | bytes 1572872 | tf_op jit(solution)/shard_map/ppermute | solution.py:19
  110.1 26.1 %collective-permute-start.18 = (f32[512,256]{1,0:T(8,128)}, f32[512,256]{1,0:T(8,128)}, u32[]{:S(2)}, u32[]{:S(2)}) collective-permute-start(f32[512,256]{1,0:T(8,128)} %get-tuple-element.67), channel_id=1, source_target_pairs={{0,4},{1,5},{2,6},{3,7},{4,0},{5,1},{6,2},{7,3},{8,12},{9,13},{10,... | collective-permute-start | bytes 1572872 | tf_op jit(solution)/shard_map/ppermute | solution.py:19
  110.1 26.3 %collective-permute-start.19 = (f32[512,256]{1,0:T(8,128)}, f32[512,256]{1,0:T(8,128)}, u32[]{:S(2)}, u32[]{:S(2)}) collective-permute-start(f32[512,256]{1,0:T(8,128)} %get-tuple-element.68), channel_id=1, source_target_pairs={{0,2},{1,3},{2,0},{3,1},{4,6},{5,7},{6,4},{7,5},{8,10},{9,11},{10,... | collective-permute-start | bytes 1572872 | tf_op jit(solution)/shard_map/ppermute | solution.py:19
  113.3 23.1 %collective-permute-start.21 = (f32[512,256]{1,0:T(8,128)}, f32[512,256]{1,0:T(8,128)}, u32[]{:S(2)}, u32[]{:S(2)}) collective-permute-start(f32[512,256]{1,0:T(8,128)} %collective-permute-done.11.refs_10_), channel_id=1, source_target_pairs={{0,16},{8,24},{16,0},{24,8},{1,17},{9,25},{17,1},{25,9},{2,18},{10... | collective-permute-start | bytes 1572872 | tf_op jit(solution)/shard_map/ppermute | solution.py:19
  139.0 28.3 %collective-permute-start.27 = (f32[512,512]{1,0:T(8,128)}, f32[512,512]{1,0:T(8,128)S(1)}, u32[]{:S(2)}, u32[]{:S(2)}) collective-permute-start(f32[512,512]{1,0:T(8,128)} %shard_map.109), channel_id=1, source_target_pairs={{0,1},{1,0},{2,3},{3,2},{4,5},{5,4},{6,7},{7,6},{8,9},{9,8},{10,11... | collective-permute-start | bytes 3145736 | tf_op jit(solution)/shard_map/ppermute | solution.py:19
  140.5 16.3 %collective-permute-start.23 = (f32[512,256]{1,0:T(8,128)}, f32[512,256]{1,0:T(8,128)}, u32[]{:S(2)}, u32[]{:S(2)}) collective-permute-start(f32[512,256]{1,0:T(8,128)} %get-tuple-element.72), channel_id=1, source_target_pairs={{0,6},{1,7},{2,4},{3,5},{4,2},{5,3},{6,0},{7,1},{8,14},{9,15},{10,... | collective-permute-start | bytes 1572872 | tf_op jit(solution)/shard_map/ppermute | solution.py:19
  142.0 15.0 %collective-permute-start.24 = (f32[512,256]{1,0:T(8,128)}, f32[512,256]{1,0:T(8,128)S(1)}, u32[]{:S(2)}, u32[]{:S(2)}) collective-permute-start(f32[512,256]{1,0:T(8,128)} %collective-permute-done.18.refs_8_), channel_id=1, source_target_pairs={{0,16},{8,24},{16,0},{24,8},{1,17},{9,25},{17,1},{25,9},{2,18},{10... | collective-permute-start | bytes 1572872 | tf_op jit(solution)/shard_map/ppermute | solution.py:19
  142.5 24.8 %collective-permute-start.25 = (f32[512,256]{1,0:T(8,128)}, f32[512,256]{1,0:T(8,128)}, u32[]{:S(2)}, u32[]{:S(2)}) collective-permute-start(f32[512,256]{1,0:T(8,128)} %collective-permute-done.19.refs_6_), channel_id=1, source_target_pairs={{0,16},{8,24},{16,0},{24,8},{1,17},{9,25},{17,1},{25,9},{2,18},{10... | collective-permute-start | bytes 1572872 | tf_op jit(solution)/shard_map/ppermute | solution.py:19
  146.9 25.7 %collective-permute-start.29 = (f32[2,512,256]{2,1,0:T(8,128)}, f32[2,512,256]{2,1,0:T(8,128)}, u32[]{:S(2)}, u32[]{:S(2)}) collective-permute-start(f32[2,512,256]{2,1,0:T(8,128)} %pad_maximum_fusion.2), channel_id=1, source_target_pairs={{0,8},{8,0},{16,24},{24,16},{1,9},{9,1},{17,25},{25,17},{2,10},{10... | collective-permute-start | bytes 3145736 | tf_op jit(solution)/shard_map/ppermute | solution.py:19
  170.4 17.8 %collective-permute-start.28 = (f32[512,256]{1,0:T(8,128)}, f32[512,256]{1,0:T(8,128)S(1)}, u32[]{:S(2)}, u32[]{:S(2)}) collective-permute-start(f32[512,256]{1,0:T(8,128)} %collective-permute-done.23.refs_10_), channel_id=1, source_target_pairs={{0,16},{8,24},{16,0},{24,8},{1,17},{9,25},{17,1},{25,9},{2,18},{10... | collective-permute-start | bytes 1572872 | tf_op jit(solution)/shard_map/ppermute | solution.py:19
  170.9 25.0 %collective-permute-start.33 = (f32[512,512]{1,0:T(8,128)}, f32[512,512]{1,0:T(8,128)S(1)}, u32[]{:S(2)}, u32[]{:S(2)}) collective-permute-start(f32[512,512]{1,0:T(8,128)} %shard_map.110), channel_id=1, source_target_pairs={{0,1},{1,0},{2,3},{3,2},{4,5},{5,4},{6,7},{7,6},{8,9},{9,8},{10,11... | collective-permute-start | bytes 3145736 | tf_op jit(solution)/shard_map/ppermute | solution.py:19
  (44 other events, 449.2 us)

commit v4 on v3

--- a/solution.py
+++ b/solution.py
@@ -215,7 +215,7 @@
     pieces = col.shape[0] // 2
     weight = [weight] if len(w_parts) < len(scaled) * pieces else []
     whole = pl.BlockSpec(memory_space=pltpu.VMEM)
-    there = pl.BlockSpec(memory_space=pltpu.HBM)
+    there = pl.BlockSpec(memory_space=pl.ANY if len(scaled) == 1 else pltpu.HBM)
     args = [col, *scaled, *weight, *[array for array, _ in w_parts]]
     in_specs = [pl.BlockSpec(memory_space=pltpu.SMEM)] + [there] * (len(args) - 1)
     scratch, n_sems = [], (1 + pieces) * len(scaled)
@@ -251,7 +251,7 @@
         out_specs=out_specs,
         scratch_shapes=scratch,
         input_output_aliases=aliases,
-        compiler_params=pltpu.CompilerParams(vmem_limit_bytes=MORE_VMEM_BYTES),
+        compiler_params=pltpu.CompilerParams(vmem_limit_bytes=MORE_VMEM_BYTES if weight else VMEM_BYTES),
         cost_estimate=nothing(),
     )(*args)
 

time: 216 us -> 213 us (0.986)
    unnamed x65 -> x73, local copies, waits for them, and re-layouts: 12.2 us -> 12.5 us
  transfers between devices with their start and end apart: 38 -> 38, of which waited for: 18 -> 18; matrix products, arithmetic and copies ran while one was open for 11% -> 12% of each run, Pallas kernels for 24% -> 24%
where the time goes in v4:
time: 213 us; the launch traced here: 212 us
  waiting for transfers between devices  66.4 us (31%)
  Pallas kernels  55.2 us (26%)
  starting transfers between devices  43.4 us (20%)
  local copies, waits for them, and re-layouts  20.3 us (10%)
  other arithmetic  19.5 us (9%)
  blocking collectives  5.74 us (3%)
    ppermute x38, waiting for transfers between devices, swap(): return lax.ppermute(array, axis, [(i, i ^ k) for i in range(size)])  66.4 us
    ppermute x38, starting transfers between devices, swap(): return lax.ppermute(array, axis, [(i, i ^ k) for i in range(size)])  43.4 us
    pallas_call x5, Pallas kernels, product(): pl.pallas_call(functools.partial(product_kernel, [place for _, place in w...  32.6 us
    pallas_call x1, Pallas kernels, interval(): pl.pallas_call(interval_kernel, out_shape=jax.ShapeDtypeStruct((2, images...  14.3 us
    unnamed x73, local copies, waits for them, and re-layouts  12.5 us
    another operation x4, other arithmetic, share_out(): return (tuple(names), jnp.stack(pieces), to_member(k))  9.94 us
    pallas_call x4, Pallas kernels, scale(): pl.pallas_call(functools.partial(scale_kernel, [(array.shape, place) for...  8.28 us
    all_gather x1, blocking collectives, local(): keep('both', lax.all_gather(both, 'spec', axis=1, tiled=True))  5.74 us
  transfers between devices with their start and end apart: 38, of which 18 were waited for; matrix products, arithmetic and copies ran while one was open for 12% of the time, Pallas kernels for 24%

profile of v4, /device:TPU:0, one launch (start us, length us, event | category | flops | bytes accessed | tf_op | source)
XLA Modules:
  0.0 211.6 jit_solution(16384271197204276289)
XLA Ops:
  1.4 4.1 %collective-permute-start = (f32[1,2,8,1024]{3,2,1,0:T(8,128)S(1)}, f32[1,2,8,1024]{3,2,1,0:T(8,128)S(1)}, u32[]{:S(2)}, u32[]{:S(2)}) collective-permute-start(f32[1,2,8,1024]{3,2,1,0:T(8,128)S(1)} %get-tuple-element.107), channel_id=1, source_target_pairs={{0,4},{1,5},{2,6},{3,7},{4,0},{5,1},{6,2},{7,3},{8,12},{9,13},{10,... | collective-permute-start | bytes 196616 | tf_op jit(solution)/shard_map/ppermute | solution.py:19
  11.7 2.5 %collective-permute-done.1 = f32[2,2,8,1024]{3,2,1,0:T(8,128)S(1)} collective-permute-done((f32[2,2,8,1024]{3,2,1,0:T(8,128)S(1)}, f32[2,2,8,1024]{3,2,1,0:T(8,128)S(1)}, u32[]{:S(2)}, u32[]{:S(2)}) %collective-permute-start.1) | collective-permute-done | bytes 131104 | tf_op jit(solution)/shard_map/ppermute | solution.py:19
  14.2 2.4 %collective-permute-start.2 = (f32[256,512]{1,0:T(8,128)S(1)}, f32[256,512]{1,0:T(8,128)S(1)}, u32[]{:S(2)}, u32[]{:S(2)}) collective-permute-start(f32[256,512]{1,0:T(8,128)S(1)} %constant_dynamic-slice_fusion.3), channel_id=1, source_target_pairs={{0,4},{1,5},{2,6},{3,7},{4,0},{5,1},{6,2},{7,3},{8,12},{9,13},{10,... | collective-permute-start | bytes 1572872 | tf_op jit(solution)/shard_map/ppermute | solution.py:19
  22.3 3.4 %constant_dynamic-slice_fusion = (f32[512,256]{1,0:T(8,128)}, f32[512,256]{1,0:T(8,128)}, f32[512,256]{1,0:T(8,128)}, f32[512,256]{1,0:T(8,128)S(1)}, f32[512,256]{1,0:T(8,128)}, /*index=5*/f32[512,256]{1,0:T(8,128)}) fusion(f32[512,8192]{1,0:T(8,128)} %refs_4_.1, s32[]{:T(128)S(6)} %select_n.101, s32[]{:T(128)S(6)} %select_n.100, s32[]{:T(128)S(6)} %select_n.99, ...), kind=kLoop, calls=%fused_computation.57 | loop fusion | bytes 6291480 | tf_op jit(solution)/shard_map/dynamic_slice | solution.py:307
  27.2 12.0 %collective-permute-done.2.refs_0_ = f32[256,512]{1,0:T(8,128)S(1)} collective-permute-done((f32[256,512]{1,0:T(8,128)S(1)}, f32[256,512]{1,0:T(8,128)S(1)}, u32[]{:S(2)}, u32[]{:S(2)}) %collective-permute-start.2) | collective-permute-done | bytes 524320 | tf_op jit(solution)/shard_map/ppermute | solution.py:19
  42.3 2.3 %collective-permute-start.7 = (f32[512,256]{1,0:T(8,128)S(1)}, f32[512,256]{1,0:T(8,128)}, u32[]{:S(2)}, u32[]{:S(2)}) collective-permute-start(f32[512,256]{1,0:T(8,128)S(1)} %get-tuple-element.51), channel_id=1, source_target_pairs={{0,4},{1,5},{2,6},{3,7},{4,0},{5,1},{6,2},{7,3},{8,12},{9,13},{10,... | collective-permute-start | bytes 1572872 | tf_op jit(solution)/shard_map/ppermute | solution.py:19
  45.3 14.3 %shard_map.104 = f32[2,8,512]{2,1,0:T(8,128)S(1)} custom-call(s32[9]{0:T(128)S(1)} %pad_add_fusion.spot_ref, f32[8,2,8,1024]{3,2,1,0:T(8,128)S(1)} %pad_maximum_fusion.4.boxes_ref, f32[512,8192]{1,0:T(8,128)} %refs_4_.1, f32[1,512]{1,0:T(1,128)S(1)} %bitcast.57, s32[32,512]{1,0:T(8,128)S(1)} %copy-done.22), custom_call_target="tpu_custom_call" | custom-call | tf_op jit(solution)/shard_map/pallas_call | solution.py:90
  59.6 5.7 %all_gather.3 = f32[2,32,512]{2,1,0:T(8,128)S(1)} all-gather(f32[2,8,512]{2,1,0:T(8,128)S(1)} %shard_map.104), channel_id=1, replica_groups=mesh['spec'=4,'neuron'=8] {'spec'}, dimensions={1}, use_global_device_ids=true | all-gather | bytes 163840 | tf_op jit(solution)/shard_map/all_gather | solution.py:360
  76.7 2.9 %shard_map.105 = (bf16[512,1024]{1,0:T(8,128)(2,1)S(1)}, f32[8,512]{1,0:T(8,128)S(1)}) custom-call(s32[512,6]{1,0:T(8,128)S(1)} %copy.29.at_ref.refs_15_.refs_9_, f32[32,512]{1,0:T(8,128)S(1)} %get-tuple-element.104.slopes_ref, f32[1000,512]{1,0:T(8,128)S(1)} %copy-done.8, f32[32,512]{1,0:T(8,128)S(1)} %get-tuple-element.103.refs_1_, f32[1,512]{1,0:T(1,128)S(1)} %bitcast.58), custom_call_target="tpu_custom_call" | custom-call | tf_op jit(solution)/shard_map/pallas_call | solution.py:140
  82.6 19.6 %collective-permute-done.16 = f32[2,32,512]{2,1,0:T(8,128)S(1)} collective-permute-done((f32[2,32,512]{2,1,0:T(8,128)S(1)}, f32[2,32,512]{2,1,0:T(8,128)S(1)}, u32[]{:S(2)}, u32[]{:S(2)}) %collective-permute-start.16) | collective-permute-done | bytes 131104 | tf_op jit(solution)/shard_map/ppermute | solution.py:19
  105.5 2.6 %pad_maximum_fusion = f32[3,512,256]{2,1,0:T(8,128)} fusion(f32[1,512,256]{2,1,0:T(8,128)} %bitcast.26, f32[1,512,256]{2,1,0:T(8,128)} %bitcast.25, f32[1,512,256]{2,1,0:T(8,128)} %bitcast.24), kind=kLoop, calls=%fused_computation | loop fusion | flops 786432 | bytes 3145728 | tf_op jit(solution)/shard_map/stack | solution.py:327
  110.1 3.2 %collective-permute-start.19 = (f32[512,256]{1,0:T(8,128)}, f32[512,256]{1,0:T(8,128)}, u32[]{:S(2)}, u32[]{:S(2)}) collective-permute-start(f32[512,256]{1,0:T(8,128)} %get-tuple-element.68), channel_id=1, source_target_pairs={{0,2},{1,3},{2,0},{3,1},{4,6},{5,7},{6,4},{7,5},{8,10},{9,11},{10,... | collective-permute-start | bytes 1572872 | tf_op jit(solution)/shard_map/ppermute | solution.py:19
  124.9 7.0 %shard_map.109 = f32[512,512]{1,0:T(8,128)} custom-call(s32[4]{0:T(128)} %add_add_fusion.2.refs_0_, bf16[512,1024]{1,0:T(8,128)(2,1)} %copy-done.4, bf16[512,1024]{1,0:T(8,128)(2,1)} %copy-done.3, bf16[512,1024]{1,0:T(8,128)(2,1)} %copy-done.2, bf16[512,1024]{1,0:T(8,128)(2,1)} %copy-done, f32[512,8192]{1,0:T(8,128)} %refs_4_.1, ...), custom_call_target="tpu_custom_call" | custom-call | tf_op jit(solution)/shard_map/pallas_call | solution.py:247
  131.9 4.3 %collective-permute-done.18.refs_8_ = f32[512,256]{1,0:T(8,128)} collective-permute-done((f32[512,256]{1,0:T(8,128)}, f32[512,256]{1,0:T(8,128)}, u32[]{:S(2)}, u32[]{:S(2)}) %collective-permute-start.18) | collective-permute-done | bytes 524320 | tf_op jit(solution)/shard_map/ppermute | solution.py:19
  136.4 2.6 %pad_maximum_fusion.1 = f32[3,512,256]{2,1,0:T(8,128)} fusion(f32[1,512,256]{2,1,0:T(8,128)} %bitcast.35, f32[1,512,256]{2,1,0:T(8,128)} %bitcast.34, f32[1,512,256]{2,1,0:T(8,128)} %bitcast.33), kind=kLoop, calls=%fused_computation.1 | loop fusion | flops 786432 | bytes 3145728 | tf_op jit(solution)/shard_map/stack | solution.py:327
  148.0 7.2 %shard_map.110 = f32[512,512]{1,0:T(8,128)} custom-call(s32[4]{0:T(128)} %add_add_fusion.3.refs_0_, bf16[512,1024]{1,0:T(8,128)(2,1)} %copy-done.4, bf16[512,1024]{1,0:T(8,128)(2,1)} %copy-done.3, bf16[512,1024]{1,0:T(8,128)(2,1)} %copy-done.2, bf16[512,1024]{1,0:T(8,128)(2,1)} %copy-done, f32[512,8192]{1,0:T(8,128)} %refs_4_.1, ...), custom_call_target="tpu_custom_call" | custom-call | tf_op jit(solution)/shard_map/pallas_call | solution.py:247
  157.0 10.3 %collective-permute-done.25.refs_5_ = f32[512,256]{1,0:T(8,128)} collective-permute-done((f32[512,256]{1,0:T(8,128)}, f32[512,256]{1,0:T(8,128)}, u32[]{:S(2)}, u32[]{:S(2)}) %collective-permute-start.25) | collective-permute-done | bytes 524320 | tf_op jit(solution)/shard_map/ppermute | solution.py:19
  167.3 2.5 %pad_maximum_fusion.3 = f32[2,512,256]{2,1,0:T(8,128)} fusion(f32[1,512,256]{2,1,0:T(8,128)S(1)} %bitcast.59, f32[1,512,256]{2,1,0:T(8,128)} %bitcast.40), kind=kLoop, calls=%fused_computation.3 | loop fusion | flops 262144 | bytes 2097152 | tf_op jit(solution)/shard_map/stack | solution.py:327
  173.9 8.5 %shard_map.111 = (f32[512,1024]{1,0:T(8,128)}, f32[8,512]{1,0:T(8,128)}) custom-call(s32[4]{0:T(128)} %add_add_fusion.4.refs_0_, bf16[512,1024]{1,0:T(8,128)(2,1)} %copy-done.4, bf16[512,1024]{1,0:T(8,128)(2,1)} %copy-done.3, bf16[512,1024]{1,0:T(8,128)(2,1)} %copy-done.2, bf16[512,1024]{1,0:T(8,128)(2,1)} %copy-done, f32[512,8192]{1,0:T(8,128)} %refs_4_.1, ...), custom_call_target="tpu_custom_call" | custom-call | tf_op jit(solution)/shard_map/pallas_call | solution.py:247
  182.5 6.2 %shard_map.112.refs_6_.refs_7_ = f32[512,512]{1,0:T(8,128)} custom-call(s32[4]{0:T(128)} %add_add_fusion.1.refs_0_, bf16[512,1024]{1,0:T(8,128)(2,1)} %copy-done.4, bf16[512,1024]{1,0:T(8,128)(2,1)} %copy-done.3, bf16[512,1024]{1,0:T(8,128)(2,1)} %copy-done.2, f32[512,8192]{1,0:T(8,128)} %refs_4_.1, f32[512,256]{1,0:T(8,128)} %collective-permute-done.25.refs_5_, ...), custom_call_target="tpu_custom_call" | custom-call | tf_op jit(solution)/shard_map/pallas_call | solution.py:247
  189.1 6.8 %collective-permute-done.33.refs_4_.refs_5_ = f32[512,512]{1,0:T(8,128)S(1)} collective-permute-done((f32[512,512]{1,0:T(8,128)}, f32[512,512]{1,0:T(8,128)S(1)}, u32[]{:S(2)}, u32[]{:S(2)}) %collective-permute-start.33) | collective-permute-done | bytes 1048608 | tf_op jit(solution)/shard_map/ppermute | solution.py:19
  197.2 3.8 %shard_map.113 = (f32[512,1024]{1,0:T(8,128)}, f32[8,512]{1,0:T(8,128)S(1)}) custom-call(s32[4]{0:T(128)S(1)} %copy-done.26, bf16[512,1024]{1,0:T(8,128)(2,1)S(1)} %copy-done.1, f32[512,256]{1,0:T(8,128)S(1)} %collective-permute-done.28.refs_2_, f32[512,256]{1,0:T(8,128)S(1)} %collective-permute-done.32.refs_3_, ...), custom_call_target="tpu_custom_call", output_to_operand_aliasing={{0}: (11, {})} | custom-call | tf_op jit(solution)/shard_map/pallas_call | solution.py:247
  201.5 3.0 %collective-permute-start.36 = (f32[8,512]{1,0:T(8,128)S(1)}, f32[8,512]{1,0:T(8,128)S(1)}, u32[]{:S(2)}, u32[]{:S(2)}) collective-permute-start(f32[8,512]{1,0:T(8,128)S(1)} %get-tuple-element.93), channel_id=1, source_target_pairs={{0,3},{1,2},{2,1},{3,0},{4,7},{5,6},{6,5},{7,4},{8,11},{9,10},{10,... | collective-permute-start | bytes 49160 | tf_op jit(solution)/shard_map/ppermute | solution.py:19
  206.4 2.7 %collective-permute-start.37 = (f32[8,512]{1,0:T(8,128)S(1)}, f32[8,512]{1,0:T(8,128)S(1)}, u32[]{:S(2)}, u32[]{:S(2)}) collective-permute-start(f32[8,512]{1,0:T(8,128)S(1)} %add_add_fusion), channel_id=1, source_target_pairs={{0,4},{1,5},{2,6},{3,7},{4,0},{5,1},{6,2},{7,3},{8,12},{9,13},{10,... | collective-permute-start | bytes 49160 | tf_op jit(solution)/shard_map/ppermute | solution.py:19
  (166 shorter events, 70.7 us)
Async XLA Ops:
  5.5 12.8 %collective-permute-start.5 = (f32[2,8,1024]{2,1,0:T(8,128)S(1)}, f32[2,8,1024]{2,1,0:T(8,128)S(1)}, u32[]{:S(2)}, u32[]{:S(2)}) collective-permute-start(f32[2,8,1024]{2,1,0:T(8,128)S(1)} %get-tuple-element.106), channel_id=1, source_target_pairs={{0,8},{8,0},{16,24},{24,16},{1,9},{9,1},{17,25},{25,17},{2,10},{10... | collective-permute-start | bytes 196616 | tf_op jit(solution)/shard_map/ppermute | solution.py:19
  14.2 24.9 %collective-permute-start.2 = (f32[256,512]{1,0:T(8,128)S(1)}, f32[256,512]{1,0:T(8,128)S(1)}, u32[]{:S(2)}, u32[]{:S(2)}) collective-permute-start(f32[256,512]{1,0:T(8,128)S(1)} %constant_dynamic-slice_fusion.3), channel_id=1, source_target_pairs={{0,4},{1,5},{2,6},{3,7},{4,0},{5,1},{6,2},{7,3},{8,12},{9,13},{10,... | collective-permute-start | bytes 1572872 | tf_op jit(solution)/shard_map/ppermute | solution.py:19
  16.6 22.9 %collective-permute-start.3 = (f32[256,512]{1,0:T(8,128)S(1)}, f32[256,512]{1,0:T(8,128)S(1)}, u32[]{:S(2)}, u32[]{:S(2)}) collective-permute-start(f32[256,512]{1,0:T(8,128)S(1)} %constant_dynamic-slice_fusion.3), channel_id=1, source_target_pairs={{0,2},{1,3},{2,0},{3,1},{4,6},{5,7},{6,4},{7,5},{8,10},{9,11},{10,... | collective-permute-start | bytes 1572872 | tf_op jit(solution)/shard_map/ppermute | solution.py:19
  39.5 26.6 %collective-permute-start.10 = (f32[256,512]{1,0:T(8,128)S(1)}, f32[256,512]{1,0:T(8,128)S(1)}, u32[]{:S(2)}, u32[]{:S(2)}) collective-permute-start(f32[256,512]{1,0:T(8,128)S(1)} %collective-permute-done.2.refs_0_), channel_id=1, source_target_pairs={{0,16},{8,24},{16,0},{24,8},{1,17},{9,25},{17,1},{25,9},{2,18},{10... | collective-permute-start | bytes 1572872 | tf_op jit(solution)/shard_map/ppermute | solution.py:19
  41.0 26.5 %collective-permute-start.8 = (f32[256,512]{1,0:T(8,128)S(1)}, f32[256,512]{1,0:T(8,128)S(1)}, u32[]{:S(2)}, u32[]{:S(2)}) collective-permute-start(f32[256,512]{1,0:T(8,128)S(1)} %collective-permute-done.2.refs_0_), channel_id=1, source_target_pairs={{0,2},{1,3},{2,0},{3,1},{4,6},{5,7},{6,4},{7,5},{8,10},{9,11},{10,... | collective-permute-start | bytes 1572872 | tf_op jit(solution)/shard_map/ppermute | solution.py:19
  42.3 25.2 %collective-permute-start.7 = (f32[512,256]{1,0:T(8,128)S(1)}, f32[512,256]{1,0:T(8,128)}, u32[]{:S(2)}, u32[]{:S(2)}) collective-permute-start(f32[512,256]{1,0:T(8,128)S(1)} %get-tuple-element.51), channel_id=1, source_target_pairs={{0,4},{1,5},{2,6},{3,7},{4,0},{5,1},{6,2},{7,3},{8,12},{9,13},{10,... | collective-permute-start | bytes 1572872 | tf_op jit(solution)/shard_map/ppermute | solution.py:19
  44.6 22.9 %collective-permute-start.9 = (f32[256,512]{1,0:T(8,128)S(1)}, f32[256,512]{1,0:T(8,128)S(1)}, u32[]{:S(2)}, u32[]{:S(2)}) collective-permute-start(f32[256,512]{1,0:T(8,128)S(1)} %collective-permute-done.3.refs_0_), channel_id=1, source_target_pairs={{0,16},{8,24},{16,0},{24,8},{1,17},{9,25},{17,1},{25,9},{2,18},{10... | collective-permute-start | bytes 1572872 | tf_op jit(solution)/shard_map/ppermute | solution.py:19
  70.3 33.5 %collective-permute-start.11 = (f32[512,256]{1,0:T(8,128)}, f32[512,256]{1,0:T(8,128)}, u32[]{:S(2)}, u32[]{:S(2)}) collective-permute-start(f32[512,256]{1,0:T(8,128)} %get-tuple-element.56), channel_id=1, source_target_pairs={{0,6},{1,7},{2,4},{3,5},{4,2},{5,3},{6,0},{7,1},{8,14},{9,15},{10,... | collective-permute-start | bytes 1572872 | tf_op jit(solution)/shard_map/ppermute | solution.py:19
  72.5 31.4 %collective-permute-start.12 = (f32[512,256]{1,0:T(8,128)}, f32[512,256]{1,0:T(8,128)}, u32[]{:S(2)}, u32[]{:S(2)}) collective-permute-start(f32[512,256]{1,0:T(8,128)} %get-tuple-element.57), channel_id=1, source_target_pairs={{0,2},{1,3},{2,0},{3,1},{4,6},{5,7},{6,4},{7,5},{8,10},{9,11},{10,... | collective-permute-start | bytes 1572872 | tf_op jit(solution)/shard_map/ppermute | solution.py:19
  73.6 30.2 %collective-permute-start.13 = (f32[256,512]{1,0:T(8,128)S(1)}, f32[256,512]{1,0:T(8,128)S(1)}, u32[]{:S(2)}, u32[]{:S(2)}) collective-permute-start(f32[256,512]{1,0:T(8,128)S(1)} %collective-permute-done.8.refs_0_), channel_id=1, source_target_pairs={{0,16},{8,24},{16,0},{24,8},{1,17},{9,25},{17,1},{25,9},{2,18},{10... | collective-permute-start | bytes 1572872 | tf_op jit(solution)/shard_map/ppermute | solution.py:19
  75.1 28.8 %collective-permute-start.14 = (f32[512,256]{1,0:T(8,128)}, f32[512,256]{1,0:T(8,128)}, u32[]{:S(2)}, u32[]{:S(2)}) collective-permute-start(f32[512,256]{1,0:T(8,128)} %collective-permute-done.7.refs_8_), channel_id=1, source_target_pairs={{0,16},{8,24},{16,0},{24,8},{1,17},{9,25},{17,1},{25,9},{2,18},{10... | collective-permute-start | bytes 1572872 | tf_op jit(solution)/shard_map/ppermute | solution.py:19
  80.6 21.6 %collective-permute-start.16 = (f32[2,32,512]{2,1,0:T(8,128)S(1)}, f32[2,32,512]{2,1,0:T(8,128)S(1)}, u32[]{:S(2)}, u32[]{:S(2)}) collective-permute-start(f32[2,32,512]{2,1,0:T(8,128)S(1)} %pad_maximum_fusion.10), channel_id=1, source_target_pairs={{0,4},{1,5},{2,6},{3,7},{4,0},{5,1},{6,2},{7,3},{8,12},{9,13},{10,... | collective-permute-start | bytes 393224 | tf_op jit(solution)/shard_map/ppermute | solution.py:19
  108.1 16.8 %collective-permute-start.22 = (f32[3,512,256]{2,1,0:T(8,128)}, f32[3,512,256]{2,1,0:T(8,128)}, u32[]{:S(2)}, u32[]{:S(2)}) collective-permute-start(f32[3,512,256]{2,1,0:T(8,128)} %pad_maximum_fusion), channel_id=1, source_target_pairs={{0,8},{8,0},{16,24},{24,16},{1,9},{9,1},{17,25},{25,17},{2,10},{10... | collective-permute-start | bytes 4718600 | tf_op jit(solution)/shard_map/ppermute | solution.py:19
  108.6 27.8 %collective-permute-start.20 = (f32[512,256]{1,0:T(8,128)}, f32[512,256]{1,0:T(8,128)}, u32[]{:S(2)}, u32[]{:S(2)}) collective-permute-start(f32[512,256]{1,0:T(8,128)} %collective-permute-done.12.refs_6_), channel_id=1, source_target_pairs={{0,16},{8,24},{16,0},{24,8},{1,17},{9,25},{17,1},{25,9},{2,18},{10... | collective-permute-start | bytes 1572872 | tf_op jit(solution)/shard_map/ppermute | solution.py:19
  110.1 26.1 %collective-permute-start.18 = (f32[512,256]{1,0:T(8,128)}, f32[512,256]{1,0:T(8,128)}, u32[]{:S(2)}, u32[]{:S(2)}) collective-permute-start(f32[512,256]{1,0:T(8,128)} %get-tuple-element.67), channel_id=1, source_target_pairs={{0,4},{1,5},{2,6},{3,7},{4,0},{5,1},{6,2},{7,3},{8,12},{9,13},{10,... | collective-permute-start | bytes 1572872 | tf_op jit(solution)/shard_map/ppermute | solution.py:19
  110.1 26.3 %collective-permute-start.19 = (f32[512,256]{1,0:T(8,128)}, f32[512,256]{1,0:T(8,128)}, u32[]{:S(2)}, u32[]{:S(2)}) collective-permute-start(f32[512,256]{1,0:T(8,128)} %get-tuple-element.68), channel_id=1, source_target_pairs={{0,2},{1,3},{2,0},{3,1},{4,6},{5,7},{6,4},{7,5},{8,10},{9,11},{10,... | collective-permute-start | bytes 1572872 | tf_op jit(solution)/shard_map/ppermute | solution.py:19
  113.3 23.1 %collective-permute-start.21 = (f32[512,256]{1,0:T(8,128)}, f32[512,256]{1,0:T(8,128)}, u32[]{:S(2)}, u32[]{:S(2)}) collective-permute-start(f32[512,256]{1,0:T(8,128)} %collective-permute-done.11.refs_10_), channel_id=1, source_target_pairs={{0,16},{8,24},{16,0},{24,8},{1,17},{9,25},{17,1},{25,9},{2,18},{10... | collective-permute-start | bytes 1572872 | tf_op jit(solution)/shard_map/ppermute | solution.py:19
  139.0 28.3 %collective-permute-start.27 = (f32[512,512]{1,0:T(8,128)}, f32[512,512]{1,0:T(8,128)S(1)}, u32[]{:S(2)}, u32[]{:S(2)}) collective-permute-start(f32[512,512]{1,0:T(8,128)} %shard_map.109), channel_id=1, source_target_pairs={{0,1},{1,0},{2,3},{3,2},{4,5},{5,4},{6,7},{7,6},{8,9},{9,8},{10,11... | collective-permute-start | bytes 3145736 | tf_op jit(solution)/shard_map/ppermute | solution.py:19
  140.5 16.3 %collective-permute-start.23 = (f32[512,256]{1,0:T(8,128)}, f32[512,256]{1,0:T(8,128)}, u32[]{:S(2)}, u32[]{:S(2)}) collective-permute-start(f32[512,256]{1,0:T(8,128)} %get-tuple-element.72), channel_id=1, source_target_pairs={{0,6},{1,7},{2,4},{3,5},{4,2},{5,3},{6,0},{7,1},{8,14},{9,15},{10,... | collective-permute-start | bytes 1572872 | tf_op jit(solution)/shard_map/ppermute | solution.py:19
  142.0 15.0 %collective-permute-start.24 = (f32[512,256]{1,0:T(8,128)}, f32[512,256]{1,0:T(8,128)S(1)}, u32[]{:S(2)}, u32[]{:S(2)}) collective-permute-start(f32[512,256]{1,0:T(8,128)} %collective-permute-done.18.refs_8_), channel_id=1, source_target_pairs={{0,16},{8,24},{16,0},{24,8},{1,17},{9,25},{17,1},{25,9},{2,18},{10... | collective-permute-start | bytes 1572872 | tf_op jit(solution)/shard_map/ppermute | solution.py:19
  142.5 24.8 %collective-permute-start.25 = (f32[512,256]{1,0:T(8,128)}, f32[512,256]{1,0:T(8,128)}, u32[]{:S(2)}, u32[]{:S(2)}) collective-permute-start(f32[512,256]{1,0:T(8,128)} %collective-permute-done.19.refs_6_), channel_id=1, source_target_pairs={{0,16},{8,24},{16,0},{24,8},{1,17},{9,25},{17,1},{25,9},{2,18},{10... | collective-permute-start | bytes 1572872 | tf_op jit(solution)/shard_map/ppermute | solution.py:19
  146.9 25.7 %collective-permute-start.29 = (f32[2,512,256]{2,1,0:T(8,128)}, f32[2,512,256]{2,1,0:T(8,128)}, u32[]{:S(2)}, u32[]{:S(2)}) collective-permute-start(f32[2,512,256]{2,1,0:T(8,128)} %pad_maximum_fusion.2), channel_id=1, source_target_pairs={{0,8},{8,0},{16,24},{24,16},{1,9},{9,1},{17,25},{25,17},{2,10},{10... | collective-permute-start | bytes 3145736 | tf_op jit(solution)/shard_map/ppermute | solution.py:19
  170.4 18.3 %collective-permute-start.28 = (f32[512,256]{1,0:T(8,128)}, f32[512,256]{1,0:T(8,128)S(1)}, u32[]{:S(2)}, u32[]{:S(2)}) collective-permute-start(f32[512,256]{1,0:T(8,128)} %collective-permute-done.23.refs_10_), channel_id=1, source_target_pairs={{0,16},{8,24},{16,0},{24,8},{1,17},{9,25},{17,1},{25,9},{2,18},{10... | collective-permute-start | bytes 1572872 | tf_op jit(solution)/shard_map/ppermute | solution.py:19
  170.9 25.0 %collective-permute-start.33 = (f32[512,512]{1,0:T(8,128)}, f32[512,512]{1,0:T(8,128)S(1)}, u32[]{:S(2)}, u32[]{:S(2)}) collective-permute-start(f32[512,512]{1,0:T(8,128)} %shard_map.110), channel_id=1, source_target_pairs={{0,1},{1,0},{2,3},{3,2},{4,5},{5,4},{6,7},{7,6},{8,9},{9,8},{10,11... | collective-permute-start | bytes 3145736 | tf_op jit(solution)/shard_map/ppermute | solution.py:19
  (48 other events, 504.0 us)

commit v5 on v4

--- a/solution.py
+++ b/solution.py
@@ -419,7 +419,8 @@
         else:
             send(*share_out(1, (t, pair, 0), (t, cut, 0)))
             send(*share_out(1, (t, cut + pair, 0)))
-            send(*share_out(1, (t, pair, 2), (t, cut, 2)))
+            send(*share_out(1, (t, pair, 2)))
+            send(*share_out(1, (t, cut, 2)))
         if i == 0:
             send(*share_out(1, *[("ow", j, r) for j in group for r in (0, 2)]))
             for j, slot in ((pair, 1), (cut, 2), (cut + pair, 3)):

time: 213 us -> 212 us (level)
  other arithmetic: 19.5 us -> 17.1 us
    another operation x4 -> x3, other arithmetic: 9.94 us -> 7.46 us  [share_out(): return (tuple(names), jnp.stack(pieces), to_member(k))]
    ppermute x38 -> x39, waiting for transfers between devices: 66.4 us -> 68 us  [swap(): return lax.ppermute(array, axis, [(i, i ^ k) for i in range(size)])]
    unnamed x73 -> x75, local copies, waits for them, and re-layouts: 12.5 us -> 12 us
    ppermute x38 -> x39, starting transfers between devices: 43.4 us -> 43.1 us  [swap(): return lax.ppermute(array, axis, [(i, i ^ k) for i in range(size)])]
  transfers between devices with their start and end apart: 38 -> 39, of which waited for: 18 -> 18; matrix products, arithmetic and copies ran while one was open for 12% -> 10% of each run, Pallas kernels for 24% -> 24%
where the time goes in v5:
time: 212 us; the launch traced here: 211 us
  waiting for transfers between devices  68 us (32%)
  Pallas kernels  55.8 us (26%)
  starting transfers between devices  43.1 us (20%)
  local copies, waits for them, and re-layouts  19.8 us (9%)
  other arithmetic  17.1 us (8%)
  blocking collectives  5.74 us (3%)
    ppermute x39, waiting for transfers between devices, swap(): return lax.ppermute(array, axis, [(i, i ^ k) for i in range(size)])  68 us
    ppermute x39, starting transfers between devices, swap(): return lax.ppermute(array, axis, [(i, i ^ k) for i in range(size)])  43.1 us
    pallas_call x5, Pallas kernels, product(): pl.pallas_call(functools.partial(product_kernel, [place for _, place in w...  33.2 us
    pallas_call x1, Pallas kernels, interval(): pl.pallas_call(interval_kernel, out_shape=jax.ShapeDtypeStruct((2, images...  14.3 us
    unnamed x75, local copies, waits for them, and re-layouts  12 us
    pallas_call x4, Pallas kernels, scale(): pl.pallas_call(functools.partial(scale_kernel, [(array.shape, place) for...  8.27 us
    another operation x3, other arithmetic, share_out(): return (tuple(names), jnp.stack(pieces), to_member(k))  7.46 us
    all_gather x1, blocking collectives, local(): keep('both', lax.all_gather(both, 'spec', axis=1, tiled=True))  5.74 us
  transfers between devices with their start and end apart: 39, of which 18 were waited for; matrix products, arithmetic and copies ran while one was open for 10% of the time, Pallas kernels for 24%

profile of v5, /device:TPU:0, one launch (start us, length us, event | category | flops | bytes accessed | tf_op | source)
XLA Modules:
  0.0 210.7 jit_solution(3362480782818193479)
XLA Ops:
  1.4 4.1 %collective-permute-start = (f32[1,2,8,1024]{3,2,1,0:T(8,128)S(1)}, f32[1,2,8,1024]{3,2,1,0:T(8,128)S(1)}, u32[]{:S(2)}, u32[]{:S(2)}) collective-permute-start(f32[1,2,8,1024]{3,2,1,0:T(8,128)S(1)} %get-tuple-element.107), channel_id=1, source_target_pairs={{0,4},{1,5},{2,6},{3,7},{4,0},{5,1},{6,2},{7,3},{8,12},{9,13},{10,... | collective-permute-start | bytes 196616 | tf_op jit(solution)/shard_map/ppermute | solution.py:19
  11.7 2.5 %collective-permute-done.1 = f32[2,2,8,1024]{3,2,1,0:T(8,128)S(1)} collective-permute-done((f32[2,2,8,1024]{3,2,1,0:T(8,128)S(1)}, f32[2,2,8,1024]{3,2,1,0:T(8,128)S(1)}, u32[]{:S(2)}, u32[]{:S(2)}) %collective-permute-start.1) | collective-permute-done | bytes 131104 | tf_op jit(solution)/shard_map/ppermute | solution.py:19
  14.2 2.4 %collective-permute-start.2 = (f32[256,512]{1,0:T(8,128)S(1)}, f32[256,512]{1,0:T(8,128)S(1)}, u32[]{:S(2)}, u32[]{:S(2)}) collective-permute-start(f32[256,512]{1,0:T(8,128)S(1)} %constant_dynamic-slice_fusion.3), channel_id=1, source_target_pairs={{0,4},{1,5},{2,6},{3,7},{4,0},{5,1},{6,2},{7,3},{8,12},{9,13},{10,... | collective-permute-start | bytes 1572872 | tf_op jit(solution)/shard_map/ppermute | solution.py:19
  22.3 3.4 %constant_dynamic-slice_fusion = (f32[512,256]{1,0:T(8,128)}, f32[512,256]{1,0:T(8,128)}, f32[512,256]{1,0:T(8,128)}, f32[512,256]{1,0:T(8,128)S(1)}, f32[512,256]{1,0:T(8,128)}, /*index=5*/f32[512,256]{1,0:T(8,128)}) fusion(f32[512,8192]{1,0:T(8,128)} %refs_4_.1, s32[]{:T(128)S(6)} %select_n.101, s32[]{:T(128)S(6)} %select_n.100, s32[]{:T(128)S(6)} %select_n.99, ...), kind=kLoop, calls=%fused_computation.56 | loop fusion | bytes 6291480 | tf_op jit(solution)/shard_map/dynamic_slice | solution.py:307
  27.2 12.0 %collective-permute-done.2.refs_0_ = f32[256,512]{1,0:T(8,128)S(1)} collective-permute-done((f32[256,512]{1,0:T(8,128)S(1)}, f32[256,512]{1,0:T(8,128)S(1)}, u32[]{:S(2)}, u32[]{:S(2)}) %collective-permute-start.2) | collective-permute-done | bytes 524320 | tf_op jit(solution)/shard_map/ppermute | solution.py:19
  42.3 2.3 %collective-permute-start.7 = (f32[512,256]{1,0:T(8,128)S(1)}, f32[512,256]{1,0:T(8,128)}, u32[]{:S(2)}, u32[]{:S(2)}) collective-permute-start(f32[512,256]{1,0:T(8,128)S(1)} %get-tuple-element.51), channel_id=1, source_target_pairs={{0,4},{1,5},{2,6},{3,7},{4,0},{5,1},{6,2},{7,3},{8,12},{9,13},{10,... | collective-permute-start | bytes 1572872 | tf_op jit(solution)/shard_map/ppermute | solution.py:19
  45.3 14.3 %shard_map.104 = f32[2,8,512]{2,1,0:T(8,128)S(1)} custom-call(s32[9]{0:T(128)S(1)} %pad_add_fusion.spot_ref, f32[8,2,8,1024]{3,2,1,0:T(8,128)S(1)} %pad_maximum_fusion.3.boxes_ref, f32[512,8192]{1,0:T(8,128)} %refs_4_.1, f32[1,512]{1,0:T(1,128)S(1)} %bitcast.55, s32[32,512]{1,0:T(8,128)S(1)} %copy-done.22), custom_call_target="tpu_custom_call" | custom-call | tf_op jit(solution)/shard_map/pallas_call | solution.py:90
  59.6 5.7 %all_gather.3 = f32[2,32,512]{2,1,0:T(8,128)S(1)} all-gather(f32[2,8,512]{2,1,0:T(8,128)S(1)} %shard_map.104), channel_id=1, replica_groups=mesh['spec'=4,'neuron'=8] {'spec'}, dimensions={1}, use_global_device_ids=true | all-gather | bytes 163840 | tf_op jit(solution)/shard_map/all_gather | solution.py:360
  76.7 2.9 %shard_map.105 = (bf16[512,1024]{1,0:T(8,128)(2,1)S(1)}, f32[8,512]{1,0:T(8,128)S(1)}) custom-call(s32[512,6]{1,0:T(8,128)S(1)} %copy.29.at_ref.refs_15_.refs_9_, f32[32,512]{1,0:T(8,128)S(1)} %get-tuple-element.104.slopes_ref, f32[1000,512]{1,0:T(8,128)S(1)} %copy-done.8, f32[32,512]{1,0:T(8,128)S(1)} %get-tuple-element.103.refs_1_, f32[1,512]{1,0:T(1,128)S(1)} %bitcast.56), custom_call_target="tpu_custom_call" | custom-call | tf_op jit(solution)/shard_map/pallas_call | solution.py:140
  82.6 19.6 %collective-permute-done.16 = f32[2,32,512]{2,1,0:T(8,128)S(1)} collective-permute-done((f32[2,32,512]{2,1,0:T(8,128)S(1)}, f32[2,32,512]{2,1,0:T(8,128)S(1)}, u32[]{:S(2)}, u32[]{:S(2)}) %collective-permute-start.16) | collective-permute-done | bytes 131104 | tf_op jit(solution)/shard_map/ppermute | solution.py:19
  105.6 2.6 %pad_maximum_fusion = f32[3,512,256]{2,1,0:T(8,128)} fusion(f32[1,512,256]{2,1,0:T(8,128)} %bitcast.26, f32[1,512,256]{2,1,0:T(8,128)} %bitcast.25, f32[1,512,256]{2,1,0:T(8,128)} %bitcast.24), kind=kLoop, calls=%fused_computation | loop fusion | flops 786432 | bytes 3145728 | tf_op jit(solution)/shard_map/stack | solution.py:327
  110.2 3.2 %collective-permute-start.19 = (f32[512,256]{1,0:T(8,128)}, f32[512,256]{1,0:T(8,128)}, u32[]{:S(2)}, u32[]{:S(2)}) collective-permute-start(f32[512,256]{1,0:T(8,128)} %get-tuple-element.68), channel_id=1, source_target_pairs={{0,2},{1,3},{2,0},{3,1},{4,6},{5,7},{6,4},{7,5},{8,10},{9,11},{10,... | collective-permute-start | bytes 1572872 | tf_op jit(solution)/shard_map/ppermute | solution.py:19
  125.0 7.0 %shard_map.109 = f32[512,512]{1,0:T(8,128)} custom-call(s32[4]{0:T(128)} %add_add_fusion.2.refs_0_, bf16[512,1024]{1,0:T(8,128)(2,1)} %copy-done.4, bf16[512,1024]{1,0:T(8,128)(2,1)} %copy-done.3, bf16[512,1024]{1,0:T(8,128)(2,1)} %copy-done.2, bf16[512,1024]{1,0:T(8,128)(2,1)} %copy-done, f32[512,8192]{1,0:T(8,128)} %refs_4_.1, ...), custom_call_target="tpu_custom_call" | custom-call | tf_op jit(solution)/shard_map/pallas_call | solution.py:247
  132.0 4.2 %collective-permute-done.18.refs_8_ = f32[512,256]{1,0:T(8,128)} collective-permute-done((f32[512,256]{1,0:T(8,128)}, f32[512,256]{1,0:T(8,128)}, u32[]{:S(2)}, u32[]{:S(2)}) %collective-permute-start.18) | collective-permute-done | bytes 524320 | tf_op jit(solution)/shard_map/ppermute | solution.py:19
  136.4 2.6 %pad_maximum_fusion.1 = f32[3,512,256]{2,1,0:T(8,128)} fusion(f32[1,512,256]{2,1,0:T(8,128)} %bitcast.35, f32[1,512,256]{2,1,0:T(8,128)} %bitcast.34, f32[1,512,256]{2,1,0:T(8,128)} %bitcast.33), kind=kLoop, calls=%fused_computation.1 | loop fusion | flops 786432 | bytes 3145728 | tf_op jit(solution)/shard_map/stack | solution.py:327
  144.7 2.3 %pad_maximum_fusion.2 = f32[2,512,256]{2,1,0:T(8,128)} fusion(f32[1,512,256]{2,1,0:T(8,128)} %bitcast.39, f32[1,512,256]{2,1,0:T(8,128)} %bitcast.38), kind=kLoop, calls=%fused_computation.2 | loop fusion | flops 262144 | bytes 2097152 | tf_op jit(solution)/shard_map/stack | solution.py:327
  148.1 7.2 %shard_map.110 = f32[512,512]{1,0:T(8,128)} custom-call(s32[4]{0:T(128)} %add_add_fusion.3.refs_0_, bf16[512,1024]{1,0:T(8,128)(2,1)} %copy-done.4, bf16[512,1024]{1,0:T(8,128)(2,1)} %copy-done.3, bf16[512,1024]{1,0:T(8,128)(2,1)} %copy-done.2, bf16[512,1024]{1,0:T(8,128)(2,1)} %copy-done, f32[512,8192]{1,0:T(8,128)} %refs_4_.1, ...), custom_call_target="tpu_custom_call" | custom-call | tf_op jit(solution)/shard_map/pallas_call | solution.py:247
  157.1 10.2 %collective-permute-done.25.refs_5_ = f32[512,256]{1,0:T(8,128)} collective-permute-done((f32[512,256]{1,0:T(8,128)}, f32[512,256]{1,0:T(8,128)}, u32[]{:S(2)}, u32[]{:S(2)}) %collective-permute-start.25) | collective-permute-done | bytes 524320 | tf_op jit(solution)/shard_map/ppermute | solution.py:19
  172.1 6.0 %shard_map.112.refs_6_.refs_7_ = f32[512,512]{1,0:T(8,128)} custom-call(s32[4]{0:T(128)} %add_add_fusion.1.refs_0_, bf16[512,1024]{1,0:T(8,128)(2,1)} %copy-done.4, bf16[512,1024]{1,0:T(8,128)(2,1)} %copy-done.3, bf16[512,1024]{1,0:T(8,128)(2,1)} %copy-done.2, f32[512,8192]{1,0:T(8,128)} %refs_4_.1, f32[512,256]{1,0:T(8,128)} %collective-permute-done.25.refs_5_, ...), custom_call_target="tpu_custom_call" | custom-call | tf_op jit(solution)/shard_map/pallas_call | solution.py:247
  178.2 8.7 %shard_map.111 = (f32[512,1024]{1,0:T(8,128)}, f32[8,512]{1,0:T(8,128)}) custom-call(s32[4]{0:T(128)} %add_add_fusion.4.refs_0_, bf16[512,1024]{1,0:T(8,128)(2,1)} %copy-done.4, bf16[512,1024]{1,0:T(8,128)(2,1)} %copy-done.3, bf16[512,1024]{1,0:T(8,128)(2,1)} %copy-done.2, bf16[512,1024]{1,0:T(8,128)(2,1)} %copy-done, f32[512,8192]{1,0:T(8,128)} %refs_4_.1, ...), custom_call_target="tpu_custom_call" | custom-call | tf_op jit(solution)/shard_map/pallas_call | solution.py:247
  186.9 8.0 %collective-permute-done.34.refs_4_.refs_5_ = f32[512,512]{1,0:T(8,128)S(1)} collective-permute-done((f32[512,512]{1,0:T(8,128)}, f32[512,512]{1,0:T(8,128)S(1)}, u32[]{:S(2)}, u32[]{:S(2)}) %collective-permute-start.34) | collective-permute-done | bytes 1048608 | tf_op jit(solution)/shard_map/ppermute | solution.py:19
  195.7 4.4 %shard_map.113 = (f32[512,1024]{1,0:T(8,128)}, f32[8,512]{1,0:T(8,128)S(1)}) custom-call(s32[4]{0:T(128)S(1)} %copy-done.26, bf16[512,1024]{1,0:T(8,128)(2,1)S(1)} %copy-done.1, f32[512,256]{1,0:T(8,128)} %collective-permute-done.28.refs_2_, f32[512,256]{1,0:T(8,128)S(1)} %collective-permute-done.33.refs_3_, ...), custom_call_target="tpu_custom_call", output_to_operand_aliasing={{0}: (11, {})} | custom-call | tf_op jit(solution)/shard_map/pallas_call | solution.py:247
  200.6 3.0 %collective-permute-start.37 = (f32[8,512]{1,0:T(8,128)S(1)}, f32[8,512]{1,0:T(8,128)S(1)}, u32[]{:S(2)}, u32[]{:S(2)}) collective-permute-start(f32[8,512]{1,0:T(8,128)S(1)} %get-tuple-element.93), channel_id=1, source_target_pairs={{0,3},{1,2},{2,1},{3,0},{4,7},{5,6},{6,5},{7,4},{8,11},{9,10},{10,... | collective-permute-start | bytes 49160 | tf_op jit(solution)/shard_map/ppermute | solution.py:19
  205.5 2.7 %collective-permute-start.38 = (f32[8,512]{1,0:T(8,128)S(1)}, f32[8,512]{1,0:T(8,128)S(1)}, u32[]{:S(2)}, u32[]{:S(2)}) collective-permute-start(f32[8,512]{1,0:T(8,128)S(1)} %add_add_fusion), channel_id=1, source_target_pairs={{0,4},{1,5},{2,6},{3,7},{4,0},{5,1},{6,2},{7,3},{8,12},{9,13},{10,... | collective-permute-start | bytes 49160 | tf_op jit(solution)/shard_map/ppermute | solution.py:19
  (169 shorter events, 68.3 us)
Async XLA Ops:
  5.5 12.8 %collective-permute-start.5 = (f32[2,8,1024]{2,1,0:T(8,128)S(1)}, f32[2,8,1024]{2,1,0:T(8,128)S(1)}, u32[]{:S(2)}, u32[]{:S(2)}) collective-permute-start(f32[2,8,1024]{2,1,0:T(8,128)S(1)} %get-tuple-element.106), channel_id=1, source_target_pairs={{0,8},{8,0},{16,24},{24,16},{1,9},{9,1},{17,25},{25,17},{2,10},{10... | collective-permute-start | bytes 196616 | tf_op jit(solution)/shard_map/ppermute | solution.py:19
  14.2 24.9 %collective-permute-start.2 = (f32[256,512]{1,0:T(8,128)S(1)}, f32[256,512]{1,0:T(8,128)S(1)}, u32[]{:S(2)}, u32[]{:S(2)}) collective-permute-start(f32[256,512]{1,0:T(8,128)S(1)} %constant_dynamic-slice_fusion.3), channel_id=1, source_target_pairs={{0,4},{1,5},{2,6},{3,7},{4,0},{5,1},{6,2},{7,3},{8,12},{9,13},{10,... | collective-permute-start | bytes 1572872 | tf_op jit(solution)/shard_map/ppermute | solution.py:19
  16.6 22.9 %collective-permute-start.3 = (f32[256,512]{1,0:T(8,128)S(1)}, f32[256,512]{1,0:T(8,128)S(1)}, u32[]{:S(2)}, u32[]{:S(2)}) collective-permute-start(f32[256,512]{1,0:T(8,128)S(1)} %constant_dynamic-slice_fusion.3), channel_id=1, source_target_pairs={{0,2},{1,3},{2,0},{3,1},{4,6},{5,7},{6,4},{7,5},{8,10},{9,11},{10,... | collective-permute-start | bytes 1572872 | tf_op jit(solution)/shard_map/ppermute | solution.py:19
  39.5 26.6 %collective-permute-start.10 = (f32[256,512]{1,0:T(8,128)S(1)}, f32[256,512]{1,0:T(8,128)S(1)}, u32[]{:S(2)}, u32[]{:S(2)}) collective-permute-start(f32[256,512]{1,0:T(8,128)S(1)} %collective-permute-done.2.refs_0_), channel_id=1, source_target_pairs={{0,16},{8,24},{16,0},{24,8},{1,17},{9,25},{17,1},{25,9},{2,18},{10... | collective-permute-start | bytes 1572872 | tf_op jit(solution)/shard_map/ppermute | solution.py:19
  41.0 26.5 %collective-permute-start.8 = (f32[256,512]{1,0:T(8,128)S(1)}, f32[256,512]{1,0:T(8,128)S(1)}, u32[]{:S(2)}, u32[]{:S(2)}) collective-permute-start(f32[256,512]{1,0:T(8,128)S(1)} %collective-permute-done.2.refs_0_), channel_id=1, source_target_pairs={{0,2},{1,3},{2,0},{3,1},{4,6},{5,7},{6,4},{7,5},{8,10},{9,11},{10,... | collective-permute-start | bytes 1572872 | tf_op jit(solution)/shard_map/ppermute | solution.py:19
  42.3 25.2 %collective-permute-start.7 = (f32[512,256]{1,0:T(8,128)S(1)}, f32[512,256]{1,0:T(8,128)}, u32[]{:S(2)}, u32[]{:S(2)}) collective-permute-start(f32[512,256]{1,0:T(8,128)S(1)} %get-tuple-element.51), channel_id=1, source_target_pairs={{0,4},{1,5},{2,6},{3,7},{4,0},{5,1},{6,2},{7,3},{8,12},{9,13},{10,... | collective-permute-start | bytes 1572872 | tf_op jit(solution)/shard_map/ppermute | solution.py:19
  44.6 22.9 %collective-permute-start.9 = (f32[256,512]{1,0:T(8,128)S(1)}, f32[256,512]{1,0:T(8,128)S(1)}, u32[]{:S(2)}, u32[]{:S(2)}) collective-permute-start(f32[256,512]{1,0:T(8,128)S(1)} %collective-permute-done.3.refs_0_), channel_id=1, source_target_pairs={{0,16},{8,24},{16,0},{24,8},{1,17},{9,25},{17,1},{25,9},{2,18},{10... | collective-permute-start | bytes 1572872 | tf_op jit(solution)/shard_map/ppermute | solution.py:19
  70.3 33.5 %collective-permute-start.11 = (f32[512,256]{1,0:T(8,128)}, f32[512,256]{1,0:T(8,128)}, u32[]{:S(2)}, u32[]{:S(2)}) collective-permute-start(f32[512,256]{1,0:T(8,128)} %get-tuple-element.56), channel_id=1, source_target_pairs={{0,6},{1,7},{2,4},{3,5},{4,2},{5,3},{6,0},{7,1},{8,14},{9,15},{10,... | collective-permute-start | bytes 1572872 | tf_op jit(solution)/shard_map/ppermute | solution.py:19
  72.5 31.4 %collective-permute-start.12 = (f32[512,256]{1,0:T(8,128)}, f32[512,256]{1,0:T(8,128)}, u32[]{:S(2)}, u32[]{:S(2)}) collective-permute-start(f32[512,256]{1,0:T(8,128)} %get-tuple-element.57), channel_id=1, source_target_pairs={{0,2},{1,3},{2,0},{3,1},{4,6},{5,7},{6,4},{7,5},{8,10},{9,11},{10,... | collective-permute-start | bytes 1572872 | tf_op jit(solution)/shard_map/ppermute | solution.py:19
  73.6 30.2 %collective-permute-start.13 = (f32[256,512]{1,0:T(8,128)S(1)}, f32[256,512]{1,0:T(8,128)S(1)}, u32[]{:S(2)}, u32[]{:S(2)}) collective-permute-start(f32[256,512]{1,0:T(8,128)S(1)} %collective-permute-done.8.refs_0_), channel_id=1, source_target_pairs={{0,16},{8,24},{16,0},{24,8},{1,17},{9,25},{17,1},{25,9},{2,18},{10... | collective-permute-start | bytes 1572872 | tf_op jit(solution)/shard_map/ppermute | solution.py:19
  75.1 28.8 %collective-permute-start.14 = (f32[512,256]{1,0:T(8,128)}, f32[512,256]{1,0:T(8,128)}, u32[]{:S(2)}, u32[]{:S(2)}) collective-permute-start(f32[512,256]{1,0:T(8,128)} %collective-permute-done.7.refs_8_), channel_id=1, source_target_pairs={{0,16},{8,24},{16,0},{24,8},{1,17},{9,25},{17,1},{25,9},{2,18},{10... | collective-permute-start | bytes 1572872 | tf_op jit(solution)/shard_map/ppermute | solution.py:19
  80.6 21.6 %collective-permute-start.16 = (f32[2,32,512]{2,1,0:T(8,128)S(1)}, f32[2,32,512]{2,1,0:T(8,128)S(1)}, u32[]{:S(2)}, u32[]{:S(2)}) collective-permute-start(f32[2,32,512]{2,1,0:T(8,128)S(1)} %pad_maximum_fusion.9), channel_id=1, source_target_pairs={{0,4},{1,5},{2,6},{3,7},{4,0},{5,1},{6,2},{7,3},{8,12},{9,13},{10,... | collective-permute-start | bytes 393224 | tf_op jit(solution)/shard_map/ppermute | solution.py:19
  108.2 16.8 %collective-permute-start.22 = (f32[3,512,256]{2,1,0:T(8,128)}, f32[3,512,256]{2,1,0:T(8,128)}, u32[]{:S(2)}, u32[]{:S(2)}) collective-permute-start(f32[3,512,256]{2,1,0:T(8,128)} %pad_maximum_fusion), channel_id=1, source_target_pairs={{0,8},{8,0},{16,24},{24,16},{1,9},{9,1},{17,25},{25,17},{2,10},{10... | collective-permute-start | bytes 4718600 | tf_op jit(solution)/shard_map/ppermute | solution.py:19
  108.7 27.8 %collective-permute-start.20 = (f32[512,256]{1,0:T(8,128)}, f32[512,256]{1,0:T(8,128)}, u32[]{:S(2)}, u32[]{:S(2)}) collective-permute-start(f32[512,256]{1,0:T(8,128)} %collective-permute-done.12.refs_6_), channel_id=1, source_target_pairs={{0,16},{8,24},{16,0},{24,8},{1,17},{9,25},{17,1},{25,9},{2,18},{10... | collective-permute-start | bytes 1572872 | tf_op jit(solution)/shard_map/ppermute | solution.py:19
  110.2 26.1 %collective-permute-start.18 = (f32[512,256]{1,0:T(8,128)}, f32[512,256]{1,0:T(8,128)}, u32[]{:S(2)}, u32[]{:S(2)}) collective-permute-start(f32[512,256]{1,0:T(8,128)} %get-tuple-element.67), channel_id=1, source_target_pairs={{0,4},{1,5},{2,6},{3,7},{4,0},{5,1},{6,2},{7,3},{8,12},{9,13},{10,... | collective-permute-start | bytes 1572872 | tf_op jit(solution)/shard_map/ppermute | solution.py:19
  110.2 26.3 %collective-permute-start.19 = (f32[512,256]{1,0:T(8,128)}, f32[512,256]{1,0:T(8,128)}, u32[]{:S(2)}, u32[]{:S(2)}) collective-permute-start(f32[512,256]{1,0:T(8,128)} %get-tuple-element.68), channel_id=1, source_target_pairs={{0,2},{1,3},{2,0},{3,1},{4,6},{5,7},{6,4},{7,5},{8,10},{9,11},{10,... | collective-permute-start | bytes 1572872 | tf_op jit(solution)/shard_map/ppermute | solution.py:19
  113.4 23.1 %collective-permute-start.21 = (f32[512,256]{1,0:T(8,128)}, f32[512,256]{1,0:T(8,128)}, u32[]{:S(2)}, u32[]{:S(2)}) collective-permute-start(f32[512,256]{1,0:T(8,128)} %collective-permute-done.11.refs_10_), channel_id=1, source_target_pairs={{0,16},{8,24},{16,0},{24,8},{1,17},{9,25},{17,1},{25,9},{2,18},{10... | collective-permute-start | bytes 1572872 | tf_op jit(solution)/shard_map/ppermute | solution.py:19
  139.0 28.3 %collective-permute-start.27 = (f32[512,512]{1,0:T(8,128)}, f32[512,512]{1,0:T(8,128)S(1)}, u32[]{:S(2)}, u32[]{:S(2)}) collective-permute-start(f32[512,512]{1,0:T(8,128)} %shard_map.109), channel_id=1, source_target_pairs={{0,1},{1,0},{2,3},{3,2},{4,5},{5,4},{6,7},{7,6},{8,9},{9,8},{10,11... | collective-permute-start | bytes 3145736 | tf_op jit(solution)/shard_map/ppermute | solution.py:19
  140.5 16.1 %collective-permute-start.23 = (f32[512,256]{1,0:T(8,128)S(1)}, f32[512,256]{1,0:T(8,128)}, u32[]{:S(2)}, u32[]{:S(2)}) collective-permute-start(f32[512,256]{1,0:T(8,128)S(1)} %copy-done.30), channel_id=1, source_target_pairs={{0,6},{1,7},{2,4},{3,5},{4,2},{5,3},{6,0},{7,1},{8,14},{9,15},{10,... | collective-permute-start | bytes 1572872 | tf_op jit(solution)/shard_map/ppermute | solution.py:19
  142.0 15.1 %collective-permute-start.24 = (f32[512,256]{1,0:T(8,128)}, f32[512,256]{1,0:T(8,128)}, u32[]{:S(2)}, u32[]{:S(2)}) collective-permute-start(f32[512,256]{1,0:T(8,128)} %collective-permute-done.18.refs_8_), channel_id=1, source_target_pairs={{0,16},{8,24},{16,0},{24,8},{1,17},{9,25},{17,1},{25,9},{2,18},{10... | collective-permute-start | bytes 1572872 | tf_op jit(solution)/shard_map/ppermute | solution.py:19
  142.6 24.8 %collective-permute-start.25 = (f32[512,256]{1,0:T(8,128)}, f32[512,256]{1,0:T(8,128)}, u32[]{:S(2)}, u32[]{:S(2)}) collective-permute-start(f32[512,256]{1,0:T(8,128)} %collective-permute-done.19.refs_6_), channel_id=1, source_target_pairs={{0,16},{8,24},{16,0},{24,8},{1,17},{9,25},{17,1},{25,9},{2,18},{10... | collective-permute-start | bytes 1572872 | tf_op jit(solution)/shard_map/ppermute | solution.py:19
  147.0 31.2 %collective-permute-start.29 = (f32[2,512,256]{2,1,0:T(8,128)}, f32[2,512,256]{2,1,0:T(8,128)}, u32[]{:S(2)}, u32[]{:S(2)}) collective-permute-start(f32[2,512,256]{2,1,0:T(8,128)} %pad_maximum_fusion.2), channel_id=1, source_target_pairs={{0,8},{8,0},{16,24},{24,16},{1,9},{9,1},{17,25},{25,17},{2,10},{10... | collective-permute-start | bytes 3145736 | tf_op jit(solution)/shard_map/ppermute | solution.py:19
  168.0 18.9 %collective-permute-start.28 = (f32[512,256]{1,0:T(8,128)}, f32[512,256]{1,0:T(8,128)}, u32[]{:S(2)}, u32[]{:S(2)}) collective-permute-start(f32[512,256]{1,0:T(8,128)} %collective-permute-done.23.refs_10_), channel_id=1, source_target_pairs={{0,16},{8,24},{16,0},{24,8},{1,17},{9,25},{17,1},{25,9},{2,18},{10... | collective-permute-start | bytes 1572872 | tf_op jit(solution)/shard_map/ppermute | solution.py:19
  169.5 25.4 %collective-permute-start.34 = (f32[512,512]{1,0:T(8,128)}, f32[512,512]{1,0:T(8,128)S(1)}, u32[]{:S(2)}, u32[]{:S(2)}) collective-permute-start(f32[512,512]{1,0:T(8,128)} %shard_map.110), channel_id=1, source_target_pairs={{0,1},{1,0},{2,3},{3,2},{4,5},{5,4},{6,7},{7,6},{8,9},{9,8},{10,11... | collective-permute-start | bytes 3145736 | tf_op jit(solution)/shard_map/ppermute | solution.py:19
  (50 other events, 505.3 us)
